TPU v7x, 256 devices: a whole 4x4x8 slice. The times are simulated.
256 devices in a mesh: seq: 32 (over z, y), tp: 8 (over x, core).
Axes of the slice: x: 4, y: 4, z: 8, core: 2. Of those that a mesh axis runs over, the one named last changes fastest.
Arguments:
- tokens: bfloat16 [8192, 4096], P('seq', 'tp'), may hold values from -6 to 6
- w_query: bfloat16 [4096, 4096], P(None, 'tp'), may hold values from -0.09375 to 0.09375
- w_key: bfloat16 [4096, 1024], P(None, 'tp'), may hold values from -0.09375 to 0.09375
- w_value: bfloat16 [4096, 1024], P(None, 'tp'), may hold values from -0.09375 to 0.09375
- q_gain: float32 [128], replicated, may hold values from 0.1 to 1.9
- k_gain: float32 [128], replicated, may hold values from 0.1 to 1.9
- doc_lengths: int32 [16], replicated, may hold values from 1 to 4096, 8192 in all
- w_out: bfloat16 [4096, 4096], P('tp'), may hold values from -0.09375 to 0.09375
Outputs:
- mixed: bfloat16 [8192, 4096], P('seq', 'tp')
Inputs may be any that keep to these rules, and one draw needn't show every extreme that they name: `doc_lengths`: whole numbers that sum to 8192; the largest is exactly 4096.
All inputs are finite; a program needn't handle non-finite values.
Results may differ from a plain program's by a relative error of at most 0.0073.
Values may be sent and summed in bfloat16 or wider, within the bound.
No kernel may reach another device: no remote copies, remote signals or barrier semaphores. Data moves between devices by JAX's collectives and lax.ppermute only.
A program may use at most 128 MiB of HBM per device.

v0:
```python
import functools
import math

import jax
import jax.numpy as jnp
from jax import lax
from jax.experimental import pallas as pl
from jax.experimental.pallas import tpu as pltpu
from jax.sharding import PartitionSpec as P

EPSILON = 1e-06
ROPE_THETA = 1000000.0
BF = jnp.bfloat16
F32 = jnp.float32
VMEM = pltpu.VMEM
VLIMIT = 24 * 1024 * 1024


def params():
    return pltpu.CompilerParams(vmem_limit_bytes=VLIMIT)


def doc_tables(doc_lengths, token_index):
    doc_ends = jnp.cumsum(doc_lengths)
    passed = (token_index[:, None] >= doc_ends[None, :]).astype(jnp.int32)
    return jnp.sum(passed * doc_lengths[None, :], axis=1)


def rope_tables(position, head_width):
    half = head_width // 2
    frequency = ROPE_THETA ** (-(jnp.arange(half, dtype=F32) * 2.0 / head_width))
    angles = position.astype(F32)[:, None] * frequency[None, :]
    cos, sin = jnp.cos(angles), jnp.sin(angles)
    return jnp.concatenate([cos, cos], axis=1), jnp.concatenate([-sin, sin], axis=1)


NX, NY = 4, 4


class Place:
    def __init__(self):
        seq, tp = lax.axis_index("seq"), lax.axis_index("tp")
        self.seq, self.z, self.y = seq, seq // NY, lax.rem(seq, NY)
        self.x, self.c = tp // 2, lax.rem(tp, 2)

        def flip(a):
            return a + 1 - 2 * lax.rem(a, 2)

        even = self.c == 0
        self.y1 = jnp.where(even, flip(self.y), NY - 1 - self.y)
        self.y2 = jnp.where(even, NY - 1 - self.y, flip(self.y))
        self.y3 = jnp.where(even, flip(self.y2), NY - 1 - self.y2)

    def chip(self, turn):
        return lax.rem(self.x + NX + turn * (1 - 2 * self.c), NX)

    def part(self, turn, other):
        return 2 * self.chip(turn) + (1 - self.c if other else self.c)

    def base(self, block, tok):
        back, who = block
        y = (self.y, self.y1, self.y2, self.y3)[who]
        if back is None:
            back = jnp.where(self.y > y, 0, 4)
        return ((self.z - back) * NY + y) * tok


def stage_kernel(plan, sources, *refs):
    ins, rest = refs[:sources], refs[sources:]
    outs, flag, sem = rest[:-2], rest[-2], rest[-1]
    place = Place()
    copies = []
    for n, (src, axis, size, (turn, other), dst, row, col, cols) in enumerate(plan):
        cut = pl.ds(pl.multiple_of(place.part(turn, other) * size, size), size)
        view = ins[src].at[cut, :] if axis == 0 else ins[src].at[:, cut]
        copies.append(
            pltpu.make_async_copy(view, outs[dst].at[row, :, col : col + cols], sem.at[n])
        )
    for c in copies:
        c.start()
    flag[...] = jnp.zeros_like(flag)
    for c in copies:
        c.wait()


FLAG = (8, 128)


def stage(arrays, plan, shapes, name):
    vm = pl.BlockSpec(memory_space=VMEM)
    return pl.pallas_call(
        functools.partial(stage_kernel, plan, len(arrays)),
        in_specs=[pl.BlockSpec(memory_space=pltpu.HBM)] * len(arrays),
        out_specs=[vm] * (len(shapes) + 1),
        out_shape=[VMEM(shape, BF) for shape in shapes] + [jax.ShapeDtypeStruct(FLAG, F32)],
        scratch_shapes=[pltpu.SemaphoreType.DMA((len(plan),))],
        compiler_params=params(),
        cost_estimate=pl.CostEstimate(
            flops=0, bytes_accessed=sum(4 * math.prod(shape) for shape in shapes), transcendentals=0
        ),
        name=name,
    )(*[pltpu.with_memory_space_constraint(a, pltpu.HBM) for a in arrays])


def after(flags, *arrays):
    out = lax.optimization_barrier((*arrays, *flags))
    return (*out[: len(arrays)], list(out[len(arrays) :]))


def pack_kernel(pieces, tok, count, *refs):
    ins, out, flag = refs[:count], refs[-2], refs[-1]
    flag[...] = jnp.zeros_like(flag)
    place = Place()
    here = (place.y, place.y1)
    for n, piece in enumerate(pieces):
        to = slice(n * tok, (n + 1) * tok)
        if len(piece) == 2:
            src, at = piece
            out[to, :] = ins[src][at * tok : (at + 1) * tok, :]
        else:
            who, one, two = piece
            later = place.y2 > here[who]

            def put(src, at, to=to):
                out[to, :] = ins[src][at * tok : (at + 1) * tok, :]

            pl.when(later)(functools.partial(put, *one))
            pl.when(jnp.logical_not(later))(functools.partial(put, *two))


def pack(arrays, pieces, tok, flags=()):
    vm = pl.BlockSpec(memory_space=VMEM)
    count = len(arrays)
    return pl.pallas_call(
        functools.partial(pack_kernel, tuple(pieces), tok, count),
        in_specs=[vm] * count + [pl.BlockSpec(memory_space=pl.ANY)] * len(flags),
        out_specs=[vm, vm],
        out_shape=[
            VMEM((len(pieces) * tok, arrays[0].shape[1]), BF),
            jax.ShapeDtypeStruct(FLAG, F32),
        ],
        compiler_params=params(),
        name="pack",
    )(*arrays, *flags)


def project_kernel(count, at, head, first, last, flags, *refs):
    chunks, w = refs[:count], refs[count]
    rest = refs[count + 1 :]
    outs = 2 if last else 1
    rest = rest[: len(rest) - flags - outs] + rest[len(rest) - outs :]
    total = None
    for k in range(count):
        prod = jnp.dot(chunks[k][...], w[at + k], preferred_element_type=F32)
        total = prod if total is None else total + prod
    if not first:
        total = total + rest[0][...]
        rest = rest[1:]
    if not last:
        rest[0][...] = total
        return
    cos_ref, sin_ref, qg, kg, q_out, kv_out = rest
    cos = cos_ref[...]
    sin = sin_ref[...]
    rows = total.shape[0]
    heads = total.shape[1] // head - 2

    def norm_rotate(x, gain):
        inv = lax.rsqrt(jnp.mean(x * x, axis=-1, keepdims=True) + EPSILON)
        x = x * inv * gain
        return (x * cos + pltpu.roll(x, head // 2, 1) * sin).astype(BF)

    kcol = heads * head
    kv_out[:, :head] = norm_rotate(total[:, kcol : kcol + head], kg[...])
    kv_out[:, head:] = total[:, kcol + head : kcol + 2 * head].astype(BF)
    for h in range(heads):
        q_out[h * rows : (h + 1) * rows, :] = norm_rotate(
            total[:, h * head : (h + 1) * head], qg[...]
        )


def project(chunks, w, at, acc=None, last=None, flags=()):
    count = len(chunks)
    rows, depth = chunks[0].shape
    width = w.shape[2]
    args = [*chunks, w] + ([] if acc is None else [acc]) + (list(last) if last else [])
    head = last[0].shape[1] if last else 128
    if last:
        heads = width // head - 2
        shape = [
            VMEM((heads * rows, head), BF),
            VMEM((rows, 2 * head), BF),
        ]
    else:
        shape = VMEM((rows, width), F32)
    vm = pl.BlockSpec(memory_space=VMEM)
    return pl.pallas_call(
        functools.partial(
            project_kernel, count, at, head, acc is None, last is not None, len(flags)
        ),
        in_specs=[vm] * len(args) + [pl.BlockSpec(memory_space=pl.ANY)] * len(flags),
        out_specs=[vm, vm] if last else vm,
        out_shape=shape,
        compiler_params=params(),
        cost_estimate=pl.CostEstimate(
            flops=4 * rows * depth * count * width,
            bytes_accessed=2 * depth * count * width,
            transcendentals=0,
        ),
        name="project",
    )(*args, *flags)


def attend_kernel(layout, first, final, flags, start_s, *refs):
    n = len(layout)
    q_ref, start_ref, index_ref = refs[:3]
    kvs = refs[3 : 3 + n]
    rest = refs[3 + n :]
    if first:
        out, flag, acc = rest[flags:]
    else:
        acc_in = rest[0]
        out, flag, acc = rest[1 + flags :]
    flag[...] = jnp.zeros_like(flag)
    rows, head = q_ref.shape
    tok = start_ref.shape[0]
    heads = rows // tok
    scale = math.log2(math.e) / math.sqrt(head)
    acc[...] = jnp.zeros_like(acc) if first else acc_in[...]
    place = Place()
    own = place.seq * tok
    least = start_s[0]
    ones = jnp.ones((tok, head), BF)

    def unit(kv, bases):
        for j, base in enumerate(bases):
            at = slice(j * tok, (j + 1) * tok)
            keys = kv[at, :head]
            values = jnp.concatenate([kv[at, head:], ones], axis=1)
            col = base + lax.broadcasted_iota(jnp.int32, (tok, tok), 1)
            keep = (col >= start_ref[...]) & (col <= index_ref[...])
            for h in range(heads):
                part = slice(h * tok, (h + 1) * tok)
                s = lax.dot_general(
                    q_ref[part, :], keys, (((1,), (1,)), ((), ())), preferred_element_type=F32
                )
                p = jnp.where(keep, jnp.exp2(s * scale), 0.0).astype(BF)
                acc[part, :] += jnp.dot(p, values, preferred_element_type=F32)

    for kv, blocks in zip(kvs, layout):
        bases = [place.base(block, tok) for block in blocks]
        if blocks[0] == (0, 0):
            unit(kv, bases)
            continue
        needed = functools.reduce(
            jnp.logical_or, [(base + tok > least) & (base <= own) for base in bases]
        )
        pl.when(needed)(functools.partial(unit, kv, bases))
    if final:
        for h in range(heads):
            part = slice(h * tok, (h + 1) * tok)
            out[:, h * head : (h + 1) * head] = (acc[part, :head] / acc[part, head:]).astype(BF)
    else:
        out[...] = acc[...]


def attend(start, queries, start_col, index_col, pieces, acc=None, final=False, flags=()):
    rows, head = queries.shape
    tok = start_col.shape[0]
    kvs = [kv for kv, _ in pieces]
    layout = tuple(tuple(blocks) for _, blocks in pieces)
    first = acc is None
    args = [queries, start_col, index_col, *kvs] + ([] if first else [acc])
    if final:
        shape = VMEM((tok, rows // tok * head), BF)
    else:
        shape = VMEM((rows, 2 * head), F32)
    blocks = sum(len(blocks) for blocks in layout)
    vm = pl.BlockSpec(memory_space=VMEM)
    return pl.pallas_call(
        functools.partial(attend_kernel, layout, first, final, len(flags)),
        in_specs=[pl.BlockSpec(memory_space=pltpu.SMEM)]
        + [vm] * len(args)
        + [pl.BlockSpec(memory_space=pl.ANY)] * len(flags),
        out_specs=[vm, vm],
        out_shape=[shape, jax.ShapeDtypeStruct(FLAG, F32)],
        scratch_shapes=[pltpu.VMEM((rows, 2 * head), F32)],
        compiler_params=params(),
        cost_estimate=pl.CostEstimate(
            flops=blocks * rows * tok * head * 8,
            bytes_accessed=rows * head * 16,
            transcendentals=blocks * rows * tok,
        ),
        name="attend",
    )(start, *args, *flags)


def out_kernel(targets, a_ref, b_ref, wa, wb, *outs):
    for n, (target, out) in enumerate(zip(targets, outs)):
        s = jnp.dot(a_ref[...], wa[target], preferred_element_type=F32)
        s += jnp.dot(b_ref[...], wb[target], preferred_element_type=F32)
        out[...] = s.astype(out.dtype)


def out_project(targets, kinds, a, b, w_own, w_sib):
    rows, depth = a.shape
    cols = w_own.shape[2]
    vm = pl.BlockSpec(memory_space=VMEM)
    return pl.pallas_call(
        functools.partial(out_kernel, targets),
        in_specs=[vm] * 4,
        out_specs=[vm] * len(targets),
        out_shape=[VMEM((rows, cols), kind) for kind in kinds],
        compiler_params=params(),
        cost_estimate=pl.CostEstimate(
            flops=4 * rows * depth * cols * len(targets),
            bytes_accessed=4 * depth * cols * len(targets),
            transcendentals=0,
        ),
        name="out_project",
    )(a, b, w_own, pltpu.with_memory_space_constraint(w_sib, VMEM))


def sum_kernel(mine, a, b, c, out):
    out[...] = (mine[...] + a[...].astype(F32) + b[...].astype(F32) + c[...].astype(F32)).astype(
        out.dtype
    )


def add_up(mine, others):
    vm = pl.BlockSpec(memory_space=VMEM)
    return pl.pallas_call(
        sum_kernel,
        in_specs=[vm] * 4,
        out_specs=vm,
        out_shape=jax.ShapeDtypeStruct(mine.shape, BF),
        compiler_params=params(),
        name="add_up",
    )(mine, *others)


def on_device(tokens, w_query, w_key, w_value, q_gain, k_gain, doc_lengths, w_out):
    tok, part = tokens.shape
    head = q_gain.shape[0]
    seqs, tps = lax.axis_size("seq"), lax.axis_size("tp")
    ny = 4
    nz = seqs // ny
    nx = tps // 2
    my_seq = lax.axis_index("seq")

    def sibling(a):
        return lax.ppermute(a, "tp", [(i, i ^ 1) for i in range(tps)])

    def along_x(a, d):
        return lax.ppermute(
            a,
            "tp",
            [(i, (i // 2 + (d if i % 2 == 0 else -d)) % nx * 2 + i % 2) for i in range(tps)],
        )

    def along_y(a, d):
        return lax.ppermute(a, "seq", [(i, i // ny * ny + (i + d) % ny) for i in range(seqs)])

    def along_z(a, d):
        return lax.ppermute(a, "seq", [(i, (i // ny + d) % nz * ny + i % ny) for i in range(seqs)])

    def swap_y(a, turned):
        pairs = []
        for s in range(seqs):
            for t in range(tps):
                y = s % ny
                other = y ^ 1 if t % 2 == turned else ny - 1 - y
                pairs.append((s * tps + t, (s // ny * ny + other) * tps + t))
        return lax.ppermute(a, ("seq", "tp"), pairs)

    nq, nk = w_query.shape[1], w_key.shape[1]
    arrivals = [(0, 0), (0, 1), (-1, 0), (1, 0), (1, 1), (-1, 1), (2, 0), (2, 1)]
    plan = []
    for k, shard in enumerate(arrivals):
        plan += [(0, 0, part, shard, 0, k, 0, nq), (1, 0, part, shard, 0, k, nq, nk)]
        plan += [(2, 0, part, shard, 0, k, nq + nk, nk)]
    w_in, flag_in = stage(
        [w_query, w_key, w_value], tuple(plan), [(tps, part, nq + 2 * nk)], "stage_in"
    )
    cols = w_out.shape[1] // tps
    plan = [(0, 1, cols, (d, 0), 0, k, 0, cols) for k, d in enumerate((2, 1, -1, 0))]
    plan += [(0, 1, cols, (d, 1), 1, k, 0, cols) for k, d in enumerate((2, -1, 1, 0))]
    w_own, w_send, flag_out = stage(
        [w_out], tuple(plan), [(nx, w_out.shape[0], cols)] * 2, "stage_out"
    )

    token_index = my_seq * tok + jnp.arange(tok, dtype=jnp.int32)
    start = doc_tables(doc_lengths, token_index)
    cos, sin = rope_tables(token_index - start, head)
    start_col, index_col = start[:, None], token_index[:, None]

    own = tokens
    a1, a3, a2 = along_x(own, 1), along_x(own, nx - 1), along_x(own, 2)
    b0 = sibling(own)
    acc = project([own, b0], w_in, 0)
    a1, flags = after([flag_in], a1)
    b1 = sibling(a1)
    a3, acc, _ = after([], a3, acc)
    b3 = sibling(a3)
    a2, cos, sin, start_col, index_col, more = after(
        [flag_out], a2, cos, sin, start_col, index_col
    )
    b2 = sibling(a2)
    acc = project([a1, a3, b1, b3], w_in, 2, acc, flags=flags)
    queries, kv = project(
        [a2, b2], w_in, 6, acc, last=(cos, sin, q_gain[None, :], k_gain[None, :]), flags=more
    )
    w_send, kv = lax.optimization_barrier((w_send, kv))
    w_sib = sibling(w_send)

    attn = (start, queries, start_col, index_col)
    r0 = kv
    r1 = along_z(r0, 1)
    r4 = along_z(r0, 4)
    r2 = along_z(r1, 1)
    r3 = along_z(r1, 2)
    x01, _ = pack([r0, r1], [(0, 0), (1, 0)], tok)
    s01 = swap_y(x01, 0)
    o, flag_a = attend(*attn, [(r0, [(0, 0)]), (r1, [(1, 0)])])
    x_near, flag_n = pack([r1, s01], [(0, 0), (1, 1)], tok)
    near = swap_y(x_near, 1)
    x234, _ = pack([r2, r3, r4], [(0, 0), (1, 0), (2, 0)], tok, flags=[flag_a, flag_n])
    s234 = swap_y(x234, 0)
    o, flag_b = attend(
        *attn,
        [(s01, [(0, 1), (1, 1)]), (r2, [(2, 0)]), (r3, [(3, 0)]), (r4, [(4, 0)])],
        o,
    )
    x_last, flag_l = pack(
        [r2, r3, s234, r0, r4, s01],
        [(0, 0), (1, 0), (2, 0), (2, 1), (0, (3, 0), (4, 0)), (1, (5, 0), (2, 2))],
        tok,
        flags=[flag_b, near],
    )
    last = swap_y(x_last, 1)
    o, _ = attend(
        *attn,
        [(near, [(1, 2), (1, 3)]), (s234, [(2, 1), (3, 1), (4, 1)])],
        o,
        flags=[flag_l],
    )
    attended, _ = attend(
        *attn,
        [(last, [(2, 2), (3, 2), (2, 3), (3, 3), (None, 2), (None, 3)])],
        o,
        final=True,
    )

    attended_sib = sibling(attended)
    (p2,) = out_project((0,), (BF,), attended, attended_sib, w_own, w_sib)
    t2 = along_x(p2, 2)
    p1, p3 = out_project((1, 2), (BF, BF), attended, attended_sib, w_own, w_sib)
    t1 = along_x(p1, 1)
    t3 = along_x(p3, nx - 1)
    (mine,) = out_project((3,), (F32,), attended, attended_sib, w_own, w_sib)
    return add_up(mine, [t1, t2, t3])


def solution(mesh):
    return jax.shard_map(
        on_device,
        mesh=mesh,
        in_specs=(
            P("seq", "tp"),
            P(None, "tp"),
            P(None, "tp"),
            P(None, "tp"),
            P(),
            P(),
            P(),
            P("tp", None),
        ),
        out_specs=P("seq", "tp"),
        check_vma=False,
    )
```

profile of v0, /device:TPU:1, one launch (start us, length us, event | category | flops | bytes accessed | tf_op | source)
XLA Modules:
  0.0 99.4 jit_solution(10470793504395271280)
XLA Ops:
  0.0 3.6 %collective-permute-start = (bf16[256,512]{1,0:T(8,128)(2,1)}, bf16[256,512]{1,0:T(8,128)(2,1)S(1)}, u32[]{:S(2)}, u32[]{:S(2)}) collective-permute-start(bf16[256,512]{1,0:T(8,128)(2,1)} %refs_0_.5), channel_id=1, source_target_pairs={{0,4},{1,5},{2,6},{3,7},{4,0},{5,1},{6,2},{7,3},{8,12},{9,13},{10,... | collective-permute-start | bytes 786440 | tf_op jit(solution)/shard_map/ppermute | solution.py:355
  3.6 1.0 collective-permute-start.4
  4.5 0.3 collective-permute-start.3
  4.8 2.4 %collective-permute-start.2 = (bf16[256,512]{1,0:T(8,128)(2,1)}, bf16[256,512]{1,0:T(8,128)(2,1)S(1)}, u32[]{:S(2)}, u32[]{:S(2)}) collective-permute-start(bf16[256,512]{1,0:T(8,128)(2,1)} %refs_0_.5), channel_id=1, source_target_pairs={{0,2},{1,7},{2,4},{3,1},{4,6},{5,3},{6,0},{7,5},{8,10},{9,15},{10,... | collective-permute-start | bytes 786440 | tf_op jit(solution)/shard_map/ppermute | solution.py:355
  7.2 0.7 copy.15
  8.0 0.1 reduce
  8.1 0.7 select_reduce_fusion.start_s
  8.9 3.0 %stage_in.1 = (bf16[8,512,768]{2,1,0:T(8,128)(2,1)S(1)}, f32[8,128]{1,0:T(8,128)S(1)}) custom-call(bf16[4096,512]{1,0:T(8,128)(2,1)} %refs_0_.4, bf16[4096,128]{1,0:T(8,128)(2,1)} %refs_1_.1, bf16[4096,128]{1,0:T(8,128)(2,1)} %refs_2_.1), custom_call_target="tpu_custom_call" | custom-call | bytes 12582912 | tf_op jit(solution)/shard_map/stage_in/pallas_call | solution.py:91
  11.8 0.5 fusion
  12.4 0.0 collective-permute-done.4.refs_1_
  12.4 0.6 project.3.refs_5_
  13.0 3.0 %collective-permute-done.3.refs_1_ = bf16[256,512]{1,0:T(8,128)(2,1)S(1)} collective-permute-done((bf16[256,512]{1,0:T(8,128)(2,1)}, bf16[256,512]{1,0:T(8,128)(2,1)S(1)}, u32[]{:S(2)}, u32[]{:S(2)}) %collective-permute-start.3) | collective-permute-done | bytes 262176 | tf_op jit(solution)/shard_map/ppermute | solution.py:355
  15.9 1.1 %collective-permute-start.6 = (bf16[256,512]{1,0:T(8,128)(2,1)S(1)}, bf16[256,512]{1,0:T(8,128)(2,1)S(1)}, u32[]{:S(2)}, u32[]{:S(2)}) collective-permute-start(bf16[256,512]{1,0:T(8,128)(2,1)S(1)} %collective-permute-done.3.refs_1_), channel_id=1, source_target_pairs={{0,1},{1,0},{2,3},{3,2},{4,5},{5,4},{6,7},{7,6},{8,9},{9,8},{10,11... | collective-permute-start | bytes 786440 | tf_op jit(solution)/shard_map/ppermute | solution.py:352
  17.0 0.0 collective-permute-done.2.refs_0_
  17.0 0.2 collective-permute-start.5
  17.2 3.6 %stage_out.1 = (bf16[4,512,512]{2,1,0:T(8,128)(2,1)S(1)}, bf16[4,512,512]{2,1,0:T(8,128)(2,1)}, f32[8,128]{1,0:T(8,128)S(1)}) custom-call(bf16[512,4096]{1,0:T(8,128)(2,1)} %refs_0_.3), custom_call_target="tpu_custom_call" | custom-call | bytes 8388608 | tf_op jit(solution)/shard_map/stage_out/pallas_call | solution.py:91
  20.9 0.1 pad_maximum_fusion
  21.0 0.0 collective-permute-done.refs_0_
  21.0 0.0 copy-start.1
  21.0 0.0 copy-start.2
  21.0 0.4 collective-permute-start.1
  21.4 0.0 collective-permute-done.6.refs_3_
  21.4 0.0 collective-permute-done.5.refs_2_
  21.4 1.0 %project.4.refs_3_ = f32[256,768]{1,0:T(8,128)S(1)} custom-call(bf16[256,512]{1,0:T(8,128)(2,1)S(1)} %collective-permute-done.2.refs_0_, bf16[256,512]{1,0:T(8,128)(2,1)S(1)} %collective-permute-done.3.refs_1_, bf16[256,512]{1,0:T(8,128)(2,1)S(1)} %collective-permute-done.5.refs_2_, bf16[256,512]{1,0:T(8,128)(2,1)S(1)} %collective-permute-done.6.refs_3_, ...), custom_call_target="tpu_custom_call" | custom-call | flops 1610612736 | bytes 3145728 | tf_op jit(solution)/shard_map/project/pallas_call | solution.py:197
  22.5 0.2 collective-permute-done.1.refs_1_
  22.7 1.0 %project.5 = (bf16[1024,128]{1,0:T(8,128)(2,1)S(1)}, bf16[256,256]{1,0:T(8,128)(2,1)S(1)}) custom-call(bf16[256,512]{1,0:T(8,128)(2,1)S(1)} %collective-permute-done.refs_0_, bf16[256,512]{1,0:T(8,128)(2,1)S(1)} %collective-permute-done.1.refs_1_, bf16[8,512,768]{2,1,0:T(8,128)(2,1)S(1)} %get-tuple-element.40.refs_2_.refs_4_, ...), custom_call_target="tpu_custom_call" | custom-call | flops 805306368 | bytes 1572864 | tf_op jit(solution)/shard_map/project/pallas_call | solution.py:197
  23.7 0.0 copy-start.3
  23.7 0.4 collective-permute-start.16
  24.1 1.6 %collective-permute-start.7 = (bf16[256,256]{1,0:T(8,128)(2,1)S(1)}, bf16[256,256]{1,0:T(8,128)(2,1)S(1)}, u32[]{:S(2)}, u32[]{:S(2)}) collective-permute-start(bf16[256,256]{1,0:T(8,128)(2,1)S(1)} %get-tuple-element.54.refs_3_.refs_0_), channel_id=1, source_target_pairs={{0,32},{8,40},{16,48},{24,56},{32,64},{40,72},{48,80},{56,88},{64,... | collective-permute-start | bytes 393224 | tf_op jit(solution)/shard_map/ppermute | solution.py:365
  25.7 7.7 %collective-permute-done.7.refs_4_.refs_1_.refs_0_ = bf16[256,256]{1,0:T(8,128)(2,1)S(1)} collective-permute-done((bf16[256,256]{1,0:T(8,128)(2,1)S(1)}, bf16[256,256]{1,0:T(8,128)(2,1)S(1)}, u32[]{:S(2)}, u32[]{:S(2)}) %collective-permute-start.7) | collective-permute-done | bytes 131104 | tf_op jit(solution)/shard_map/ppermute | solution.py:365
  33.4 0.7 pack.4
  34.2 2.7 %collective-permute-start.11 = (bf16[512,256]{1,0:T(8,128)(2,1)}, bf16[512,256]{1,0:T(8,128)(2,1)S(1)}, u32[]{:S(2)}, u32[]{:S(2)}) collective-permute-start(bf16[512,256]{1,0:T(8,128)(2,1)} %get-tuple-element.56), channel_id=1, source_target_pairs={{0,8},{1,25},{2,10},{3,27},{4,12},{5,29},{6,14},{7,31},{8,0},{9,17... | collective-permute-start | bytes 786440 | tf_op jit(solution)/shard_map/ppermute | solution.py:374
  36.9 3.8 %collective-permute-start.10 = (bf16[256,256]{1,0:T(8,128)(2,1)S(1)}, bf16[256,256]{1,0:T(8,128)(2,1)S(1)}, u32[]{:S(2)}, u32[]{:S(2)}) collective-permute-start(bf16[256,256]{1,0:T(8,128)(2,1)S(1)} %get-tuple-element.54.refs_3_.refs_0_), channel_id=1, source_target_pairs={{0,128},{8,136},{16,144},{24,152},{32,160},{40,168},{48,176},{56,1... | collective-permute-start | bytes 393224 | tf_op jit(solution)/shard_map/ppermute | solution.py:365
  40.7 0.0 collective-permute-start.8
  40.7 0.7 collective-permute-start.9
  41.4 0.1 copy.19.refs_1_
  41.5 0.0 copy-start.4
  41.6 0.9 copy-done.4
  42.5 1.3 %attend.4 = (f32[1024,256]{1,0:T(8,128)S(1)}, f32[8,128]{1,0:T(8,128)S(1)}) custom-call(s32[256]{0:T(256)S(1)} %select_reduce_fusion.start_s, bf16[1024,128]{1,0:T(8,128)(2,1)S(1)} %copy-done.4, s32[256,1]{1,0:T(8,128)S(1)} %copy.19.refs_1_, s32[256,1]{1,0:T(8,128)S(1)} %iota_add_fusion.refs_2_, bf16[256,256]{1,0:T(8,128)(2,1)S(1)} %get-tuple-element.54.refs_3_.refs_0_, ...), custom_call_target="tpu_custom_call" | custom-call | flops 536870912 | bytes 2097152 | tf_op jit(solution)/shard_map/attend/pallas_call | solution.py:280
  43.8 0.0 collective-permute-done.11.refs_1_.refs_3_.refs_5_
  43.9 5.2 %collective-permute-done.10.refs_2_.refs_6_.refs_4_ = bf16[256,256]{1,0:T(8,128)(2,1)S(1)} collective-permute-done((bf16[256,256]{1,0:T(8,128)(2,1)S(1)}, bf16[256,256]{1,0:T(8,128)(2,1)S(1)}, u32[]{:S(2)}, u32[]{:S(2)}) %collective-permute-start.10) | collective-permute-done | bytes 131104 | tf_op jit(solution)/shard_map/ppermute | solution.py:365
  49.1 1.2 %collective-permute-done.8.refs_0_.refs_4_ = bf16[256,256]{1,0:T(8,128)(2,1)S(1)} collective-permute-done((bf16[256,256]{1,0:T(8,128)(2,1)S(1)}, bf16[256,256]{1,0:T(8,128)(2,1)S(1)}, u32[]{:S(2)}, u32[]{:S(2)}) %collective-permute-start.8) | collective-permute-done | bytes 131104 | tf_op jit(solution)/shard_map/ppermute | solution.py:365
  50.4 3.1 %collective-permute-done.9.refs_1_.refs_5_ = bf16[256,256]{1,0:T(8,128)(2,1)S(1)} collective-permute-done((bf16[256,256]{1,0:T(8,128)(2,1)S(1)}, bf16[256,256]{1,0:T(8,128)(2,1)S(1)}, u32[]{:S(2)}, u32[]{:S(2)}) %collective-permute-start.9) | collective-permute-done | bytes 131104 | tf_op jit(solution)/shard_map/ppermute | solution.py:365
  53.5 0.6 pack.6
  54.1 0.7 attend.5
  54.8 6.5 %collective-permute-done.13.refs_7_.refs_3_ = bf16[512,256]{1,0:T(8,128)(2,1)S(1)} collective-permute-done((bf16[512,256]{1,0:T(8,128)(2,1)S(1)}, bf16[512,256]{1,0:T(8,128)(2,1)S(1)}, u32[]{:S(2)}, u32[]{:S(2)}) %collective-permute-start.13) | collective-permute-done | bytes 262176 | tf_op jit(solution)/shard_map/ppermute | solution.py:374
  61.3 3.6 %collective-permute-done.12.refs_2_.refs_4_ = bf16[768,256]{1,0:T(8,128)(2,1)S(1)} collective-permute-done((bf16[768,256]{1,0:T(8,128)(2,1)S(1)}, bf16[768,256]{1,0:T(8,128)(2,1)S(1)}, u32[]{:S(2)}, u32[]{:S(2)}) %collective-permute-start.12) | collective-permute-done | bytes 393248 | tf_op jit(solution)/shard_map/ppermute | solution.py:374
  64.9 0.1 pack.7
  65.0 0.1 collective-permute-start.14
  65.1 1.2 %attend.6 = (f32[1024,256]{1,0:T(8,128)S(1)}, f32[8,128]{1,0:T(8,128)}) custom-call(s32[256]{0:T(256)S(1)} %select_reduce_fusion.start_s, bf16[1024,128]{1,0:T(8,128)(2,1)S(1)} %copy-done.4, s32[256,1]{1,0:T(8,128)S(1)} %copy.19.refs_1_, s32[256,1]{1,0:T(8,128)S(1)} %iota_add_fusion.refs_2_, bf16[512,256]{1,0:T(8,128)(2,1)S(1)} %collective-permute-done.13.refs_7_.refs_3_, ...), custom_call_target="tpu_custom_call" | custom-call | flops 1342177280 | bytes 2097152 | tf_op jit(solution)/shard_map/attend/pallas_call | solution.py:280
  66.3 9.9 %collective-permute-done.14.refs_3_ = bf16[1536,256]{1,0:T(8,128)(2,1)S(1)} collective-permute-done((bf16[1536,256]{1,0:T(8,128)(2,1)S(1)}, bf16[1536,256]{1,0:T(8,128)(2,1)S(1)}, u32[]{:S(2)}, u32[]{:S(2)}) %collective-permute-start.14) | collective-permute-done | bytes 786464 | tf_op jit(solution)/shard_map/ppermute | solution.py:374
  76.2 1.2 %attend.7 = (bf16[256,512]{1,0:T(8,128)(2,1)S(1)}, f32[8,128]{1,0:T(8,128)}) custom-call(s32[256]{0:T(256)S(1)} %select_reduce_fusion.start_s, bf16[1024,128]{1,0:T(8,128)(2,1)S(1)} %copy-done.4, s32[256,1]{1,0:T(8,128)S(1)} %copy.19.refs_1_, s32[256,1]{1,0:T(8,128)S(1)} %iota_add_fusion.refs_2_, bf16[1536,256]{1,0:T(8,128)(2,1)S(1)} %collective-permute-done.14.refs_3_, ...), custom_call_target="tpu_custom_call" | custom-call | flops 1610612736 | bytes 2097152 | tf_op jit(solution)/shard_map/attend/pallas_call | solution.py:280
  77.4 2.5 %collective-permute-start.15 = (bf16[256,512]{1,0:T(8,128)(2,1)S(1)}, bf16[256,512]{1,0:T(8,128)(2,1)S(1)}, u32[]{:S(2)}, u32[]{:S(2)}) collective-permute-start(bf16[256,512]{1,0:T(8,128)(2,1)S(1)} %get-tuple-element.66.a_ref), channel_id=1, source_target_pairs={{0,1},{1,0},{2,3},{3,2},{4,5},{5,4},{6,7},{7,6},{8,9},{9,8},{10,11... | collective-permute-start | bytes 786440 | tf_op jit(solution)/shard_map/ppermute | solution.py:352
  79.9 1.2 %collective-permute-done.15.b_ref = bf16[256,512]{1,0:T(8,128)(2,1)S(1)} collective-permute-done((bf16[256,512]{1,0:T(8,128)(2,1)S(1)}, bf16[256,512]{1,0:T(8,128)(2,1)S(1)}, u32[]{:S(2)}, u32[]{:S(2)}) %collective-permute-start.15) | collective-permute-done | bytes 262176 | tf_op jit(solution)/shard_map/ppermute | solution.py:352
  81.0 2.0 %out_project.5 = bf16[256,512]{1,0:T(8,128)(2,1)S(1)} custom-call(bf16[256,512]{1,0:T(8,128)(2,1)S(1)} %get-tuple-element.66.a_ref, bf16[256,512]{1,0:T(8,128)(2,1)S(1)} %collective-permute-done.15.b_ref, bf16[4,512,512]{2,1,0:T(8,128)(2,1)S(1)} %get-tuple-element.67.wa, bf16[4,512,512]{2,1,0:T(8,128)(2,1)} %collective-permute-done.16.wb), custom_call_target="tpu_custom_call" | custom-call | flops 268435456 | bytes 1048576 | tf_op jit(solution)/shard_map/out_project/pallas_call | solution.py:309
  83.1 2.1 %collective-permute-start.18 = (bf16[256,512]{1,0:T(8,128)(2,1)S(1)}, bf16[256,512]{1,0:T(8,128)(2,1)S(1)}, u32[]{:S(2)}, u32[]{:S(2)}) collective-permute-start(bf16[256,512]{1,0:T(8,128)(2,1)S(1)} %out_project.5), channel_id=1, source_target_pairs={{0,4},{1,5},{2,6},{3,7},{4,0},{5,1},{6,2},{7,3},{8,12},{9,13},{10,... | collective-permute-start | bytes 786440 | tf_op jit(solution)/shard_map/ppermute | solution.py:355
  85.2 2.3 %out_project.4 = (bf16[256,512]{1,0:T(8,128)(2,1)S(1)}, bf16[256,512]{1,0:T(8,128)(2,1)S(1)}) custom-call(bf16[256,512]{1,0:T(8,128)(2,1)S(1)} %get-tuple-element.66.a_ref, bf16[256,512]{1,0:T(8,128)(2,1)S(1)} %collective-permute-done.15.b_ref, bf16[4,512,512]{2,1,0:T(8,128)(2,1)S(1)} %get-tuple-element.67.wa, bf16[4,512,512]{2,1,0:T(8,128)(2,1)} %collective-permute-done.16.wb), custom_call_target="tpu_custom_call" | custom-call | flops 536870912 | bytes 2097152 | tf_op jit(solution)/shard_map/out_project/pallas_call | solution.py:309
  87.5 1.5 %collective-permute-start.17 = (bf16[256,512]{1,0:T(8,128)(2,1)S(1)}, bf16[256,512]{1,0:T(8,128)(2,1)S(1)}, u32[]{:S(2)}, u32[]{:S(2)}) collective-permute-start(bf16[256,512]{1,0:T(8,128)(2,1)S(1)} %get-tuple-element.69), channel_id=1, source_target_pairs={{0,2},{1,7},{2,4},{3,1},{4,6},{5,3},{6,0},{7,5},{8,10},{9,15},{10,... | collective-permute-start | bytes 786440 | tf_op jit(solution)/shard_map/ppermute | solution.py:355
  89.0 0.0 collective-permute-start.19
  89.0 2.0 %out_project.3.mine = f32[256,512]{1,0:T(8,128)S(1)} custom-call(bf16[256,512]{1,0:T(8,128)(2,1)S(1)} %get-tuple-element.66.a_ref, bf16[256,512]{1,0:T(8,128)(2,1)S(1)} %collective-permute-done.15.b_ref, bf16[4,512,512]{2,1,0:T(8,128)(2,1)S(1)} %get-tuple-element.67.wa, bf16[4,512,512]{2,1,0:T(8,128)(2,1)} %collective-permute-done.16.wb), custom_call_target="tpu_custom_call" | custom-call | flops 268435456 | bytes 1048576 | tf_op jit(solution)/shard_map/out_project/pallas_call | solution.py:309
  91.0 1.1 %collective-permute-done.18.b = bf16[256,512]{1,0:T(8,128)(2,1)S(1)} collective-permute-done((bf16[256,512]{1,0:T(8,128)(2,1)S(1)}, bf16[256,512]{1,0:T(8,128)(2,1)S(1)}, u32[]{:S(2)}, u32[]{:S(2)}) %collective-permute-start.18) | collective-permute-done | bytes 262176 | tf_op jit(solution)/shard_map/ppermute | solution.py:355
  92.2 5.5 %collective-permute-done.17.a = bf16[256,512]{1,0:T(8,128)(2,1)S(1)} collective-permute-done((bf16[256,512]{1,0:T(8,128)(2,1)S(1)}, bf16[256,512]{1,0:T(8,128)(2,1)S(1)}, u32[]{:S(2)}, u32[]{:S(2)}) %collective-permute-start.17) | collective-permute-done | bytes 262176 | tf_op jit(solution)/shard_map/ppermute | solution.py:355
  97.6 1.0 %collective-permute-done.19.c = bf16[256,512]{1,0:T(8,128)(2,1)S(1)} collective-permute-done((bf16[256,512]{1,0:T(8,128)(2,1)S(1)}, bf16[256,512]{1,0:T(8,128)(2,1)S(1)}, u32[]{:S(2)}, u32[]{:S(2)}) %collective-permute-start.19) | collective-permute-done | bytes 262176 | tf_op jit(solution)/shard_map/ppermute | solution.py:355
  98.6 0.8 add_up.1
  (14 shorter events, 0.1 us)
Async XLA Ops:
  0.0 12.4 %copy-start = (bf16[256,512]{1,0:T(8,128)(2,1)S(1)}, bf16[256,512]{1,0:T(8,128)(2,1)}, u32[]{:S(2)}) copy-start(bf16[256,512]{1,0:T(8,128)(2,1)} %refs_0_.5) | copy-start | bytes 786436
  0.0 21.0 %collective-permute-start = (bf16[256,512]{1,0:T(8,128)(2,1)}, bf16[256,512]{1,0:T(8,128)(2,1)S(1)}, u32[]{:S(2)}, u32[]{:S(2)}) collective-permute-start(bf16[256,512]{1,0:T(8,128)(2,1)} %refs_0_.5), channel_id=1, source_target_pairs={{0,4},{1,5},{2,6},{3,7},{4,0},{5,1},{6,2},{7,3},{8,12},{9,13},{10,... | collective-permute-start | bytes 786440 | tf_op jit(solution)/shard_map/ppermute | solution.py:355
  3.6 8.8 %collective-permute-start.4 = (bf16[256,512]{1,0:T(8,128)(2,1)}, bf16[256,512]{1,0:T(8,128)(2,1)S(1)}, u32[]{:S(2)}, u32[]{:S(2)}) collective-permute-start(bf16[256,512]{1,0:T(8,128)(2,1)} %refs_0_.5), channel_id=1, source_target_pairs={{0,1},{1,0},{2,3},{3,2},{4,5},{5,4},{6,7},{7,6},{8,9},{9,8},{10,11... | collective-permute-start | bytes 786440 | tf_op jit(solution)/shard_map/ppermute | solution.py:352
  4.5 11.4 %collective-permute-start.3 = (bf16[256,512]{1,0:T(8,128)(2,1)}, bf16[256,512]{1,0:T(8,128)(2,1)S(1)}, u32[]{:S(2)}, u32[]{:S(2)}) collective-permute-start(bf16[256,512]{1,0:T(8,128)(2,1)} %refs_0_.5), channel_id=1, source_target_pairs={{0,6},{1,3},{2,0},{3,5},{4,2},{5,7},{6,4},{7,1},{8,14},{9,11},{10,... | collective-permute-start | bytes 786440 | tf_op jit(solution)/shard_map/ppermute | solution.py:355
  4.8 12.2 %collective-permute-start.2 = (bf16[256,512]{1,0:T(8,128)(2,1)}, bf16[256,512]{1,0:T(8,128)(2,1)S(1)}, u32[]{:S(2)}, u32[]{:S(2)}) collective-permute-start(bf16[256,512]{1,0:T(8,128)(2,1)} %refs_0_.5), channel_id=1, source_target_pairs={{0,2},{1,7},{2,4},{3,1},{4,6},{5,3},{6,0},{7,5},{8,10},{9,15},{10,... | collective-permute-start | bytes 786440 | tf_op jit(solution)/shard_map/ppermute | solution.py:355
  15.9 5.5 %collective-permute-start.6 = (bf16[256,512]{1,0:T(8,128)(2,1)S(1)}, bf16[256,512]{1,0:T(8,128)(2,1)S(1)}, u32[]{:S(2)}, u32[]{:S(2)}) collective-permute-start(bf16[256,512]{1,0:T(8,128)(2,1)S(1)} %collective-permute-done.3.refs_1_), channel_id=1, source_target_pairs={{0,1},{1,0},{2,3},{3,2},{4,5},{5,4},{6,7},{7,6},{8,9},{9,8},{10,11... | collective-permute-start | bytes 786440 | tf_op jit(solution)/shard_map/ppermute | solution.py:352
  17.0 4.4 %collective-permute-start.5 = (bf16[256,512]{1,0:T(8,128)(2,1)S(1)}, bf16[256,512]{1,0:T(8,128)(2,1)S(1)}, u32[]{:S(2)}, u32[]{:S(2)}) collective-permute-start(bf16[256,512]{1,0:T(8,128)(2,1)S(1)} %collective-permute-done.2.refs_0_), channel_id=1, source_target_pairs={{0,1},{1,0},{2,3},{3,2},{4,5},{5,4},{6,7},{7,6},{8,9},{9,8},{10,11... | collective-permute-start | bytes 786440 | tf_op jit(solution)/shard_map/ppermute | solution.py:352
  21.0 1.6 %copy-start.1 = (f32[128]{0:T(128)S(1)}, f32[128]{0:T(128)}, u32[]{:S(2)}) copy-start(f32[128]{0:T(128)} %param.12) | copy-start | bytes 1540
  21.0 1.6 %copy-start.2 = (f32[128]{0:T(128)S(1)}, f32[128]{0:T(128)}, u32[]{:S(2)}) copy-start(f32[128]{0:T(128)} %param.13) | copy-start | bytes 1540
  21.0 1.6 %collective-permute-start.1 = (bf16[256,512]{1,0:T(8,128)(2,1)S(1)}, bf16[256,512]{1,0:T(8,128)(2,1)S(1)}, u32[]{:S(2)}, u32[]{:S(2)}) collective-permute-start(bf16[256,512]{1,0:T(8,128)(2,1)S(1)} %collective-permute-done.refs_0_), channel_id=1, source_target_pairs={{0,1},{1,0},{2,3},{3,2},{4,5},{5,4},{6,7},{7,6},{8,9},{9,8},{10,11... | collective-permute-start | bytes 786440 | tf_op jit(solution)/shard_map/ppermute | solution.py:352
  23.7 10.5 %copy-start.3 = (bf16[1024,128]{1,0:T(8,128)(2,1)}, bf16[1024,128]{1,0:T(8,128)(2,1)S(1)}, u32[]{:S(2)}) copy-start(bf16[1024,128]{1,0:T(8,128)(2,1)S(1)} %get-tuple-element.49.refs_0_) | copy-start | bytes 786436
  23.7 57.3 %collective-permute-start.16 = (bf16[4,512,512]{2,1,0:T(8,128)(2,1)}, bf16[4,512,512]{2,1,0:T(8,128)(2,1)}, u32[]{:S(2)}, u32[]{:S(2)}) collective-permute-start(bf16[4,512,512]{2,1,0:T(8,128)(2,1)} %get-tuple-element.68), channel_id=1, source_target_pairs={{0,1},{1,0},{2,3},{3,2},{4,5},{5,4},{6,7},{7,6},{8,9},{9,8},{10,11... | collective-permute-start | bytes 6291464 | tf_op jit(solution)/shard_map/ppermute | solution.py:352
  24.1 9.3 %collective-permute-start.7 = (bf16[256,256]{1,0:T(8,128)(2,1)S(1)}, bf16[256,256]{1,0:T(8,128)(2,1)S(1)}, u32[]{:S(2)}, u32[]{:S(2)}) collective-permute-start(bf16[256,256]{1,0:T(8,128)(2,1)S(1)} %get-tuple-element.54.refs_3_.refs_0_), channel_id=1, source_target_pairs={{0,32},{8,40},{16,48},{24,56},{32,64},{40,72},{48,80},{56,88},{64,... | collective-permute-start | bytes 393224 | tf_op jit(solution)/shard_map/ppermute | solution.py:365
  34.2 9.7 %collective-permute-start.11 = (bf16[512,256]{1,0:T(8,128)(2,1)}, bf16[512,256]{1,0:T(8,128)(2,1)S(1)}, u32[]{:S(2)}, u32[]{:S(2)}) collective-permute-start(bf16[512,256]{1,0:T(8,128)(2,1)} %get-tuple-element.56), channel_id=1, source_target_pairs={{0,8},{1,25},{2,10},{3,27},{4,12},{5,29},{6,14},{7,31},{8,0},{9,17... | collective-permute-start | bytes 786440 | tf_op jit(solution)/shard_map/ppermute | solution.py:374
  36.9 12.2 %collective-permute-start.10 = (bf16[256,256]{1,0:T(8,128)(2,1)S(1)}, bf16[256,256]{1,0:T(8,128)(2,1)S(1)}, u32[]{:S(2)}, u32[]{:S(2)}) collective-permute-start(bf16[256,256]{1,0:T(8,128)(2,1)S(1)} %get-tuple-element.54.refs_3_.refs_0_), channel_id=1, source_target_pairs={{0,128},{8,136},{16,144},{24,152},{32,160},{40,168},{48,176},{56,1... | collective-permute-start | bytes 393224 | tf_op jit(solution)/shard_map/ppermute | solution.py:365
  40.7 9.7 %collective-permute-start.8 = (bf16[256,256]{1,0:T(8,128)(2,1)S(1)}, bf16[256,256]{1,0:T(8,128)(2,1)S(1)}, u32[]{:S(2)}, u32[]{:S(2)}) collective-permute-start(bf16[256,256]{1,0:T(8,128)(2,1)S(1)} %collective-permute-done.7.refs_4_.refs_1_.refs_0_), channel_id=1, source_target_pairs={{0,32},{8,40},{16,48},{24,56},{32,64},{40,72},{48,80},{56,88},{64,... | collective-permute-start | bytes 393224 | tf_op jit(solution)/shard_map/ppermute | solution.py:365
  40.7 12.8 %collective-permute-start.9 = (bf16[256,256]{1,0:T(8,128)(2,1)S(1)}, bf16[256,256]{1,0:T(8,128)(2,1)S(1)}, u32[]{:S(2)}, u32[]{:S(2)}) collective-permute-start(bf16[256,256]{1,0:T(8,128)(2,1)S(1)} %collective-permute-done.7.refs_4_.refs_1_.refs_0_), channel_id=1, source_target_pairs={{0,64},{8,72},{16,80},{24,88},{32,96},{40,104},{48,112},{56,120},{... | collective-permute-start | bytes 393224 | tf_op jit(solution)/shard_map/ppermute | solution.py:365
  41.5 1.0 copy-start.4
  54.1 10.8 %collective-permute-start.12 = (bf16[768,256]{1,0:T(8,128)(2,1)S(1)}, bf16[768,256]{1,0:T(8,128)(2,1)S(1)}, u32[]{:S(2)}, u32[]{:S(2)}) collective-permute-start(bf16[768,256]{1,0:T(8,128)(2,1)S(1)} %get-tuple-element.58), channel_id=1, source_target_pairs={{0,8},{1,25},{2,10},{3,27},{4,12},{5,29},{6,14},{7,31},{8,0},{9,17... | collective-permute-start | bytes 1179656 | tf_op jit(solution)/shard_map/ppermute | solution.py:374
  54.1 7.2 %collective-permute-start.13 = (bf16[512,256]{1,0:T(8,128)(2,1)S(1)}, bf16[512,256]{1,0:T(8,128)(2,1)S(1)}, u32[]{:S(2)}, u32[]{:S(2)}) collective-permute-start(bf16[512,256]{1,0:T(8,128)(2,1)S(1)} %get-tuple-element.61), channel_id=1, source_target_pairs={{0,24},{1,9},{2,26},{3,11},{4,28},{5,13},{6,30},{7,15},{8,16},{9,1... | collective-permute-start | bytes 786440 | tf_op jit(solution)/shard_map/ppermute | solution.py:374
  65.0 11.2 %collective-permute-start.14 = (bf16[1536,256]{1,0:T(8,128)(2,1)S(1)}, bf16[1536,256]{1,0:T(8,128)(2,1)S(1)}, u32[]{:S(2)}, u32[]{:S(2)}) collective-permute-start(bf16[1536,256]{1,0:T(8,128)(2,1)S(1)} %get-tuple-element.62), channel_id=1, source_target_pairs={{0,24},{1,9},{2,26},{3,11},{4,28},{5,13},{6,30},{7,15},{8,16},{9,1... | collective-permute-start | bytes 2359304 | tf_op jit(solution)/shard_map/ppermute | solution.py:374
  77.4 3.6 %collective-permute-start.15 = (bf16[256,512]{1,0:T(8,128)(2,1)S(1)}, bf16[256,512]{1,0:T(8,128)(2,1)S(1)}, u32[]{:S(2)}, u32[]{:S(2)}) collective-permute-start(bf16[256,512]{1,0:T(8,128)(2,1)S(1)} %get-tuple-element.66.a_ref), channel_id=1, source_target_pairs={{0,1},{1,0},{2,3},{3,2},{4,5},{5,4},{6,7},{7,6},{8,9},{9,8},{10,11... | collective-permute-start | bytes 786440 | tf_op jit(solution)/shard_map/ppermute | solution.py:352
  83.1 9.1 %collective-permute-start.18 = (bf16[256,512]{1,0:T(8,128)(2,1)S(1)}, bf16[256,512]{1,0:T(8,128)(2,1)S(1)}, u32[]{:S(2)}, u32[]{:S(2)}) collective-permute-start(bf16[256,512]{1,0:T(8,128)(2,1)S(1)} %out_project.5), channel_id=1, source_target_pairs={{0,4},{1,5},{2,6},{3,7},{4,0},{5,1},{6,2},{7,3},{8,12},{9,13},{10,... | collective-permute-start | bytes 786440 | tf_op jit(solution)/shard_map/ppermute | solution.py:355
  87.5 10.2 %collective-permute-start.17 = (bf16[256,512]{1,0:T(8,128)(2,1)S(1)}, bf16[256,512]{1,0:T(8,128)(2,1)S(1)}, u32[]{:S(2)}, u32[]{:S(2)}) collective-permute-start(bf16[256,512]{1,0:T(8,128)(2,1)S(1)} %get-tuple-element.69), channel_id=1, source_target_pairs={{0,2},{1,7},{2,4},{3,1},{4,6},{5,3},{6,0},{7,5},{8,10},{9,15},{10,... | collective-permute-start | bytes 786440 | tf_op jit(solution)/shard_map/ppermute | solution.py:355
  89.0 9.6 %collective-permute-start.19 = (bf16[256,512]{1,0:T(8,128)(2,1)S(1)}, bf16[256,512]{1,0:T(8,128)(2,1)S(1)}, u32[]{:S(2)}, u32[]{:S(2)}) collective-permute-start(bf16[256,512]{1,0:T(8,128)(2,1)S(1)} %get-tuple-element.70), channel_id=1, source_target_pairs={{0,6},{1,3},{2,0},{3,5},{4,2},{5,7},{6,4},{7,1},{8,14},{9,11},{10,... | collective-permute-start | bytes 786440 | tf_op jit(solution)/shard_map/ppermute | solution.py:355
where the time goes:
time: 99.7 us; the launch traced here: 99.4 us
  waiting for transfers between devices  49.2 us (49%)
  starting transfers between devices  24.4 us (24%)
  Pallas kernels  22.3 us (22%)
  local copies, waits for them, and re-layouts  1.83 us (2%)
  other arithmetic  1.6 us (2%)
    ppermute x4, waiting for transfers between devices, swap_y(): return lax.ppermute(a, ('seq', 'tp'), pairs)  20 us
    ppermute x4, waiting for transfers between devices, along_z(): lax.ppermute(a, 'seq', [(i, (i // ny + d) % nz * ny + i % ny) for i in ra...  17.3 us
    ppermute x6, waiting for transfers between devices, along_x(): lax.ppermute(a, 'tp', [(i, (i // 2 + (d if i % 2 == 0 else -d)) % nx * 2...  10.6 us
    ppermute x6, starting transfers between devices, along_x(): lax.ppermute(a, 'tp', [(i, (i // 2 + (d if i % 2 == 0 else -d)) % nx * 2...  9.91 us
    pallas_call x2, Pallas kernels, stage(): pl.pallas_call(functools.partial(stage_kernel, plan, len(arrays)), in_spe...  6.59 us
    pallas_call x3, Pallas kernels, out_project(): pl.pallas_call(functools.partial(out_kernel, targets), in_specs=[vm] * 4,...  6.33 us
    ppermute x4, starting transfers between devices, along_z(): lax.ppermute(a, 'seq', [(i, (i // ny + d) % nz * ny + i % ny) for i in ra...  6.14 us
    ppermute x6, starting transfers between devices, sibling(): return lax.ppermute(a, 'tp', [(i, i ^ 1) for i in range(tps)])  5.49 us
  transfers between devices with their start and end apart: 20, of which 13 were waited for; matrix products, arithmetic and copies ran while one was open for 2% of the time, Pallas kernels for 19%

commit v1 on v0

--- a/solution.py
+++ b/solution.py
@@ -13,11 +13,11 @@
 BF = jnp.bfloat16
 F32 = jnp.float32
 VMEM = pltpu.VMEM
-VLIMIT = 24 * 1024 * 1024
-
-
-def params():
-    return pltpu.CompilerParams(vmem_limit_bytes=VLIMIT)
+MIB = 1024 * 1024
+
+
+def params(limit=10):
+    return pltpu.CompilerParams(vmem_limit_bytes=limit * MIB)
 
 
 def doc_tables(doc_lengths, token_index):
@@ -86,6 +86,26 @@
 FLAG = (8, 128)
 
 
+def fetch_kernel(src, out, flag, sem):
+    copy = pltpu.make_async_copy(src, out, sem)
+    copy.start()
+    flag[...] = jnp.zeros_like(flag)
+    copy.wait()
+
+
+def fetch(a):
+    vm = pl.BlockSpec(memory_space=VMEM)
+    return pl.pallas_call(
+        fetch_kernel,
+        in_specs=[pl.BlockSpec(memory_space=pl.ANY)],
+        out_specs=[vm, vm],
+        out_shape=[VMEM(a.shape, a.dtype), jax.ShapeDtypeStruct(FLAG, F32)],
+        scratch_shapes=[pltpu.SemaphoreType.DMA],
+        compiler_params=params(),
+        name="fetch",
+    )(a)
+
+
 def stage(arrays, plan, shapes, name):
     vm = pl.BlockSpec(memory_space=VMEM)
     return pl.pallas_call(
@@ -94,7 +114,7 @@
         out_specs=[vm] * (len(shapes) + 1),
         out_shape=[VMEM(shape, BF) for shape in shapes] + [jax.ShapeDtypeStruct(FLAG, F32)],
         scratch_shapes=[pltpu.SemaphoreType.DMA((len(plan),))],
-        compiler_params=params(),
+        compiler_params=params(14),
         cost_estimate=pl.CostEstimate(
             flops=0, bytes_accessed=sum(4 * math.prod(shape) for shape in shapes), transcendentals=0
         ),
@@ -105,6 +125,22 @@
 def after(flags, *arrays):
     out = lax.optimization_barrier((*arrays, *flags))
     return (*out[: len(arrays)], list(out[len(arrays) :]))
+
+
+def hold_kernel(*refs):
+    refs[-1][...] = jnp.zeros(FLAG, F32)
+
+
+def hold(*arrays):
+    return pl.pallas_call(
+        hold_kernel,
+        in_specs=[pl.BlockSpec(memory_space=pl.ANY)] * len(arrays),
+        out_specs=pl.BlockSpec(memory_space=VMEM),
+        out_shape=jax.ShapeDtypeStruct(FLAG, F32),
+        compiler_params=params(),
+        cost_estimate=pl.CostEstimate(flops=2 * 10**10, bytes_accessed=4096, transcendentals=0),
+        name="hold",
+    )(*arrays)
 
 
 def pack_kernel(pieces, tok, count, *refs):
@@ -201,7 +237,7 @@
         in_specs=[vm] * len(args) + [pl.BlockSpec(memory_space=pl.ANY)] * len(flags),
         out_specs=[vm, vm] if last else vm,
         out_shape=shape,
-        compiler_params=params(),
+        compiler_params=params(16),
         cost_estimate=pl.CostEstimate(
             flops=4 * rows * depth * count * width,
             bytes_accessed=2 * depth * count * width,
@@ -318,7 +354,7 @@
             transcendentals=0,
         ),
         name="out_project",
-    )(a, b, w_own, pltpu.with_memory_space_constraint(w_sib, VMEM))
+    )(a, b, w_own, w_sib)
 
 
 def sum_kernel(mine, a, b, c, out):
@@ -398,57 +434,55 @@
     a1, a3, a2 = along_x(own, 1), along_x(own, nx - 1), along_x(own, 2)
     b0 = sibling(own)
     acc = project([own, b0], w_in, 0)
-    a1, flags = after([flag_in], a1)
+    a1, flags = after([flag_in, flag_out], a1)
     b1 = sibling(a1)
     a3, acc, _ = after([], a3, acc)
     b3 = sibling(a3)
-    a2, cos, sin, start_col, index_col, more = after(
-        [flag_out], a2, cos, sin, start_col, index_col
-    )
+    a2, cos, sin, start_col, index_col, _ = after([], a2, cos, sin, start_col, index_col)
     b2 = sibling(a2)
     acc = project([a1, a3, b1, b3], w_in, 2, acc, flags=flags)
     queries, kv = project(
-        [a2, b2], w_in, 6, acc, last=(cos, sin, q_gain[None, :], k_gain[None, :]), flags=more
-    )
-    w_send, kv = lax.optimization_barrier((w_send, kv))
-    w_sib = sibling(w_send)
-
+        [a2, b2], w_in, 6, acc, last=(cos, sin, q_gain[None, :], k_gain[None, :])
+    )
     attn = (start, queries, start_col, index_col)
     r0 = kv
     r1 = along_z(r0, 1)
     r4 = along_z(r0, 4)
     r2 = along_z(r1, 1)
-    r3 = along_z(r1, 2)
-    x01, _ = pack([r0, r1], [(0, 0), (1, 0)], tok)
-    s01 = swap_y(x01, 0)
-    o, flag_a = attend(*attn, [(r0, [(0, 0)]), (r1, [(1, 0)])])
-    x_near, flag_n = pack([r1, s01], [(0, 0), (1, 1)], tok)
+    r3 = along_z(r2, 1)
+    x012, _ = pack([r0, r1, r2], [(0, 0), (1, 0), (2, 0)], tok)
+    s012 = swap_y(x012, 0)
+    o, _ = attend(*attn, [(r0, [(0, 0)]), (r1, [(1, 0)])])
+    x34, flag_34 = pack([r3, r4], [(0, 0), (1, 0)], tok)
+    s34 = swap_y(x34, 0)
+    x_near, flag_n = pack(
+        [r1, r2, s012], [(0, 0), (1, 0), (2, 1), (2, 2)], tok, flags=[hold(r3, r4), flag_34]
+    )
     near = swap_y(x_near, 1)
-    x234, _ = pack([r2, r3, r4], [(0, 0), (1, 0), (2, 0)], tok, flags=[flag_a, flag_n])
-    s234 = swap_y(x234, 0)
-    o, flag_b = attend(
-        *attn,
-        [(s01, [(0, 1), (1, 1)]), (r2, [(2, 0)]), (r3, [(3, 0)]), (r4, [(4, 0)])],
-        o,
-    )
+    w_send, flags = after([flag_n], w_send)
+    w_sib = sibling(w_send)
+    o, flag_b = attend(*attn, [(r2, [(2, 0)]), (s012, [(0, 1), (1, 1), (2, 1)])], o, flags=flags)
     x_last, flag_l = pack(
-        [r2, r3, s234, r0, r4, s01],
-        [(0, 0), (1, 0), (2, 0), (2, 1), (0, (3, 0), (4, 0)), (1, (5, 0), (2, 2))],
+        [r3, s34, r0, r4, s012],
+        [(0, 0), (1, 0), (0, (2, 0), (3, 0)), (1, (4, 0), (1, 1))],
         tok,
-        flags=[flag_b, near],
+        flags=[flag_b, hold(s34), near],
     )
     last = swap_y(x_last, 1)
+    w_sib, flag_w = fetch(w_sib)
     o, _ = attend(
         *attn,
-        [(near, [(1, 2), (1, 3)]), (s234, [(2, 1), (3, 1), (4, 1)])],
+        [
+            (near, [(1, 2), (2, 2), (1, 3), (2, 3)]),
+            (r3, [(3, 0)]),
+            (r4, [(4, 0)]),
+            (s34, [(3, 1), (4, 1)]),
+        ],
         o,
-        flags=[flag_l],
+        flags=[flag_l, flag_w],
     )
     attended, _ = attend(
-        *attn,
-        [(last, [(2, 2), (3, 2), (2, 3), (3, 3), (None, 2), (None, 3)])],
-        o,
-        final=True,
+        *attn, [(last, [(3, 2), (3, 3), (None, 2), (None, 3)])], o, final=True
     )
 
     attended_sib = sibling(attended)

time: 99.7 us -> 95.4 us (0.957)
  the two profiles are of different devices: /device:TPU:1 before, /device:TPU:121 now
where the time goes in v1:
time: 95.4 us; the launch traced here: 95.3 us
  waiting for transfers between devices  37.3 us (39%)
  starting transfers between devices  36 us (38%)
  Pallas kernels  19.2 us (20%)
  other arithmetic  1.6 us (2%)
    ppermute x4, waiting for transfers between devices, swap_y(): return lax.ppermute(a, ('seq', 'tp'), pairs)  16 us
    ppermute x6, starting transfers between devices, sibling(): return lax.ppermute(a, 'tp', [(i, i ^ 1) for i in range(tps)])  15.8 us
    ppermute x6, waiting for transfers between devices, along_x(): lax.ppermute(a, 'tp', [(i, (i // 2 + (d if i % 2 == 0 else -d)) % nx * 2...  12.3 us
    ppermute x4, starting transfers between devices, along_z(): lax.ppermute(a, 'seq', [(i, (i // ny + d) % nz * ny + i % ny) for i in ra...  11 us
    ppermute x6, starting transfers between devices, along_x(): lax.ppermute(a, 'tp', [(i, (i // 2 + (d if i % 2 == 0 else -d)) % nx * 2...  7.89 us
    pallas_call x4, Pallas kernels, attend(): pl.pallas_call(functools.partial(attend_kernel, layout, first, final, len...  7.33 us
    ppermute x4, waiting for transfers between devices, along_z(): lax.ppermute(a, 'seq', [(i, (i // ny + d) % nz * ny + i % ny) for i in ra...  7.08 us
    pallas_call x2, Pallas kernels, stage(): pl.pallas_call(functools.partial(stage_kernel, plan, len(arrays)), in_spe...  6.01 us
  transfers between devices with their start and end apart: 20, of which 12 were waited for; matrix products, arithmetic and copies ran while one was open for 3% of the time, Pallas kernels for 15%

profile of v1, /device:TPU:121, one launch (start us, length us, event | category | flops | bytes accessed | tf_op | source)
XLA Modules:
  0.0 95.3 jit_solution(17394987369744244931)
XLA Ops:
  0.0 2.7 %collective-permute-start = (bf16[256,512]{1,0:T(8,128)(2,1)}, bf16[256,512]{1,0:T(8,128)(2,1)S(1)}, u32[]{:S(2)}, u32[]{:S(2)}) collective-permute-start(bf16[256,512]{1,0:T(8,128)(2,1)} %refs_0_.5), channel_id=1, source_target_pairs={{0,4},{1,5},{2,6},{3,7},{4,0},{5,1},{6,2},{7,3},{8,12},{9,13},{10,... | collective-permute-start | bytes 786440 | tf_op jit(solution)/shard_map/ppermute | solution.py:391
  2.7 0.9 collective-permute-start.2
  3.6 0.7 collective-permute-start.4
  4.3 0.0 collective-permute-start.3
  4.3 0.7 copy.15
  5.1 0.1 reduce
  5.2 0.7 select_reduce_fusion.start_s
  5.9 2.3 %stage_out.1 = (bf16[4,512,512]{2,1,0:T(8,128)(2,1)S(1)}, bf16[4,512,512]{2,1,0:T(8,128)(2,1)S(1)}, f32[8,128]{1,0:T(8,128)S(1)}) custom-call(bf16[512,4096]{1,0:T(8,128)(2,1)} %refs_0_.4), custom_call_target="tpu_custom_call" | custom-call | bytes 8388608 | tf_op jit(solution)/shard_map/stage_out/pallas_call | solution.py:111
  8.2 0.0 copy-start
  8.2 3.7 %stage_in.1 = (bf16[8,512,768]{2,1,0:T(8,128)(2,1)S(1)}, f32[8,128]{1,0:T(8,128)S(1)}) custom-call(bf16[4096,512]{1,0:T(8,128)(2,1)} %refs_0_.3, bf16[4096,128]{1,0:T(8,128)(2,1)} %refs_1_.1, bf16[4096,128]{1,0:T(8,128)(2,1)} %refs_2_.1), custom_call_target="tpu_custom_call" | custom-call | bytes 12582912 | tf_op jit(solution)/shard_map/stage_in/pallas_call | solution.py:111
  12.0 0.5 fusion
  12.6 2.2 %collective-permute-done.2.refs_0_ = bf16[256,512]{1,0:T(8,128)(2,1)S(1)} collective-permute-done((bf16[256,512]{1,0:T(8,128)(2,1)}, bf16[256,512]{1,0:T(8,128)(2,1)S(1)}, u32[]{:S(2)}, u32[]{:S(2)}) %collective-permute-start.2) | collective-permute-done | bytes 262176 | tf_op jit(solution)/shard_map/ppermute | solution.py:391
  14.7 1.3 %collective-permute-start.5 = (bf16[256,512]{1,0:T(8,128)(2,1)S(1)}, bf16[256,512]{1,0:T(8,128)(2,1)S(1)}, u32[]{:S(2)}, u32[]{:S(2)}) collective-permute-start(bf16[256,512]{1,0:T(8,128)(2,1)S(1)} %collective-permute-done.2.refs_0_), channel_id=1, source_target_pairs={{0,1},{1,0},{2,3},{3,2},{4,5},{5,4},{6,7},{7,6},{8,9},{9,8},{10,11... | collective-permute-start | bytes 786440 | tf_op jit(solution)/shard_map/ppermute | solution.py:388
  16.0 0.0 collective-permute-done.4.refs_1_
  16.1 0.6 project.3.refs_5_
  16.6 0.0 collective-permute-done.3.refs_1_
  16.6 0.1 collective-permute-start.6
  16.8 0.1 pad_maximum_fusion
  16.9 0.0 collective-permute-done.refs_0_
  16.9 0.0 copy-start.1
  16.9 0.0 copy-start.2
  16.9 0.6 collective-permute-start.1
  17.5 0.0 collective-permute-done.5.refs_2_
  17.5 0.7 collective-permute-done.6.refs_3_
  18.3 1.0 %project.4.refs_3_ = f32[256,768]{1,0:T(8,128)S(1)} custom-call(bf16[256,512]{1,0:T(8,128)(2,1)S(1)} %collective-permute-done.2.refs_0_, bf16[256,512]{1,0:T(8,128)(2,1)S(1)} %collective-permute-done.3.refs_1_, bf16[256,512]{1,0:T(8,128)(2,1)S(1)} %collective-permute-done.5.refs_2_, bf16[256,512]{1,0:T(8,128)(2,1)S(1)} %collective-permute-done.6.refs_3_, ...), custom_call_target="tpu_custom_call" | custom-call | flops 1610612736 | bytes 3145728 | tf_op jit(solution)/shard_map/project/pallas_call | solution.py:233
  19.2 0.0 collective-permute-done.1.refs_1_
  19.3 1.0 %project.5 = (bf16[1024,128]{1,0:T(8,128)(2,1)S(1)}, bf16[256,256]{1,0:T(8,128)(2,1)S(1)}) custom-call(bf16[256,512]{1,0:T(8,128)(2,1)S(1)} %collective-permute-done.refs_0_, bf16[256,512]{1,0:T(8,128)(2,1)S(1)} %collective-permute-done.1.refs_1_, bf16[8,512,768]{2,1,0:T(8,128)(2,1)S(1)} %get-tuple-element.41.refs_2_.refs_4_, ...), custom_call_target="tpu_custom_call" | custom-call | flops 805306368 | bytes 1572864 | tf_op jit(solution)/shard_map/project/pallas_call | solution.py:233
  20.3 2.9 %collective-permute-start.7 = (bf16[256,256]{1,0:T(8,128)(2,1)S(1)}, bf16[256,256]{1,0:T(8,128)(2,1)S(1)}, u32[]{:S(2)}, u32[]{:S(2)}) collective-permute-start(bf16[256,256]{1,0:T(8,128)(2,1)S(1)} %get-tuple-element.54.refs_0_.refs_3_.refs_2_), channel_id=1, source_target_pairs={{0,32},{8,40},{16,48},{24,56},{32,64},{40,72},{48,80},{56,88},{64,... | collective-permute-start | bytes 393224 | tf_op jit(solution)/shard_map/ppermute | solution.py:401
  23.2 2.8 %collective-permute-done.7.refs_1_.refs_4_.refs_0_ = bf16[256,256]{1,0:T(8,128)(2,1)S(1)} collective-permute-done((bf16[256,256]{1,0:T(8,128)(2,1)S(1)}, bf16[256,256]{1,0:T(8,128)(2,1)S(1)}, u32[]{:S(2)}, u32[]{:S(2)}) %collective-permute-start.7) | collective-permute-done | bytes 131104 | tf_op jit(solution)/shard_map/ppermute | solution.py:401
  26.0 3.4 %collective-permute-start.8 = (bf16[256,256]{1,0:T(8,128)(2,1)S(1)}, bf16[256,256]{1,0:T(8,128)(2,1)S(1)}, u32[]{:S(2)}, u32[]{:S(2)}) collective-permute-start(bf16[256,256]{1,0:T(8,128)(2,1)S(1)} %collective-permute-done.7.refs_1_.refs_4_.refs_0_), channel_id=1, source_target_pairs={{0,32},{8,40},{16,48},{24,56},{32,64},{40,72},{48,80},{56,88},{64,... | collective-permute-start | bytes 393224 | tf_op jit(solution)/shard_map/ppermute | solution.py:401
  29.4 1.6 %collective-permute-start.10 = (bf16[256,256]{1,0:T(8,128)(2,1)S(1)}, bf16[256,256]{1,0:T(8,128)(2,1)S(1)}, u32[]{:S(2)}, u32[]{:S(2)}) collective-permute-start(bf16[256,256]{1,0:T(8,128)(2,1)S(1)} %get-tuple-element.54.refs_0_.refs_3_.refs_2_), channel_id=1, source_target_pairs={{0,128},{8,136},{16,144},{24,152},{32,160},{40,168},{48,176},{56,1... | collective-permute-start | bytes 393224 | tf_op jit(solution)/shard_map/ppermute | solution.py:401
  31.0 0.3 collective-permute-done.8.refs_2_.refs_1_.refs_3_
  31.3 3.1 %collective-permute-start.9 = (bf16[256,256]{1,0:T(8,128)(2,1)S(1)}, bf16[256,256]{1,0:T(8,128)(2,1)S(1)}, u32[]{:S(2)}, u32[]{:S(2)}) collective-permute-start(bf16[256,256]{1,0:T(8,128)(2,1)S(1)} %collective-permute-done.8.refs_2_.refs_1_.refs_3_), channel_id=1, source_target_pairs={{0,32},{8,40},{16,48},{24,56},{32,64},{40,72},{48,80},{56,88},{64,... | collective-permute-start | bytes 393224 | tf_op jit(solution)/shard_map/ppermute | solution.py:401
  34.4 0.1 copy.19.refs_1_
  34.6 1.7 %attend.4 = (f32[1024,256]{1,0:T(8,128)S(1)}, f32[8,128]{1,0:T(8,128)}) custom-call(s32[256]{0:T(256)S(1)} %select_reduce_fusion.start_s, bf16[1024,128]{1,0:T(8,128)(2,1)S(1)} %get-tuple-element.51.refs_0_, s32[256,1]{1,0:T(8,128)S(1)} %copy.19.refs_1_, s32[256,1]{1,0:T(8,128)S(1)} %iota_add_fusion.refs_2_, ...), custom_call_target="tpu_custom_call" | custom-call | flops 536870912 | bytes 2097152 | tf_op jit(solution)/shard_map/attend/pallas_call | solution.py:316
  36.3 0.6 pack.5
  36.9 0.0 collective-permute-start.12
  36.9 4.0 %collective-permute-done.10.refs_1_.refs_3_.refs_5_ = bf16[256,256]{1,0:T(8,128)(2,1)S(1)} collective-permute-done((bf16[256,256]{1,0:T(8,128)(2,1)S(1)}, bf16[256,256]{1,0:T(8,128)(2,1)S(1)}, u32[]{:S(2)}, u32[]{:S(2)}) %collective-permute-start.10) | collective-permute-done | bytes 131104 | tf_op jit(solution)/shard_map/ppermute | solution.py:401
  40.9 0.0 collective-permute-done.9.refs_0_.refs_4_
  40.9 0.3 collective-permute-start.11
  41.2 3.5 %collective-permute-done.12.refs_2_.refs_4_ = bf16[768,256]{1,0:T(8,128)(2,1)S(1)} collective-permute-done((bf16[768,256]{1,0:T(8,128)(2,1)S(1)}, bf16[768,256]{1,0:T(8,128)(2,1)S(1)}, u32[]{:S(2)}, u32[]{:S(2)}) %collective-permute-start.12) | collective-permute-done | bytes 393248 | tf_op jit(solution)/shard_map/ppermute | solution.py:410
  44.8 8.9 %collective-permute-start.15 = (bf16[4,512,512]{2,1,0:T(8,128)(2,1)S(1)}, bf16[4,512,512]{2,1,0:T(8,128)(2,1)S(1)}, u32[]{:S(2)}, u32[]{:S(2)}) collective-permute-start(bf16[4,512,512]{2,1,0:T(8,128)(2,1)S(1)} %copy-done.4), channel_id=1, source_target_pairs={{0,1},{1,0},{2,3},{3,2},{4,5},{5,4},{6,7},{7,6},{8,9},{9,8},{10,11... | collective-permute-start | bytes 6291464 | tf_op jit(solution)/shard_map/ppermute | solution.py:388
  53.7 0.5 collective-permute-start.13
  54.2 0.0 collective-permute-done.11.refs_0_.refs_1_.refs_6_
  54.2 1.8 %attend.5 = (f32[1024,256]{1,0:T(8,128)S(1)}, f32[8,128]{1,0:T(8,128)S(1)}) custom-call(s32[256]{0:T(256)S(1)} %select_reduce_fusion.start_s, bf16[1024,128]{1,0:T(8,128)(2,1)S(1)} %get-tuple-element.51.refs_0_, s32[256,1]{1,0:T(8,128)S(1)} %copy.19.refs_1_, s32[256,1]{1,0:T(8,128)S(1)} %iota_add_fusion.refs_2_, ...), custom_call_target="tpu_custom_call" | custom-call | flops 1073741824 | bytes 2097152 | tf_op jit(solution)/shard_map/attend/pallas_call | solution.py:316
  56.0 6.0 %collective-permute-done.13.refs_7_.refs_3_ = bf16[1024,256]{1,0:T(8,128)(2,1)S(1)} collective-permute-done((bf16[1024,256]{1,0:T(8,128)(2,1)S(1)}, bf16[1024,256]{1,0:T(8,128)(2,1)S(1)}, u32[]{:S(2)}, u32[]{:S(2)}) %collective-permute-start.13) | collective-permute-done | bytes 524320 | tf_op jit(solution)/shard_map/ppermute | solution.py:410
  62.1 0.5 collective-permute-start.14
  62.6 0.0 collective-permute-done.15.src
  62.6 0.2 fetch.1
  62.8 1.2 %attend.6 = (f32[1024,256]{1,0:T(8,128)S(1)}, f32[8,128]{1,0:T(8,128)}) custom-call(s32[256]{0:T(256)S(1)} %select_reduce_fusion.start_s, bf16[1024,128]{1,0:T(8,128)(2,1)S(1)} %get-tuple-element.51.refs_0_, s32[256,1]{1,0:T(8,128)S(1)} %copy.19.refs_1_, s32[256,1]{1,0:T(8,128)S(1)} %iota_add_fusion.refs_2_, ...), custom_call_target="tpu_custom_call" | custom-call | flops 2147483648 | bytes 2097152 | tf_op jit(solution)/shard_map/attend/pallas_call | solution.py:316
  64.0 6.5 %collective-permute-done.14.refs_3_ = bf16[1024,256]{1,0:T(8,128)(2,1)S(1)} collective-permute-done((bf16[1024,256]{1,0:T(8,128)(2,1)S(1)}, bf16[1024,256]{1,0:T(8,128)(2,1)S(1)}, u32[]{:S(2)}, u32[]{:S(2)}) %collective-permute-start.14) | collective-permute-done | bytes 524320 | tf_op jit(solution)/shard_map/ppermute | solution.py:410
  70.5 2.6 %attend.7 = (bf16[256,512]{1,0:T(8,128)(2,1)S(1)}, f32[8,128]{1,0:T(8,128)}) custom-call(s32[256]{0:T(256)S(1)} %select_reduce_fusion.start_s, bf16[1024,128]{1,0:T(8,128)(2,1)S(1)} %get-tuple-element.51.refs_0_, s32[256,1]{1,0:T(8,128)S(1)} %copy.19.refs_1_, s32[256,1]{1,0:T(8,128)S(1)} %iota_add_fusion.refs_2_, ...), custom_call_target="tpu_custom_call" | custom-call | flops 1073741824 | bytes 2097152 | tf_op jit(solution)/shard_map/attend/pallas_call | solution.py:316
  73.1 4.2 %collective-permute-start.16 = (bf16[256,512]{1,0:T(8,128)(2,1)S(1)}, bf16[256,512]{1,0:T(8,128)(2,1)S(1)}, u32[]{:S(2)}, u32[]{:S(2)}) collective-permute-start(bf16[256,512]{1,0:T(8,128)(2,1)S(1)} %get-tuple-element.70.a_ref), channel_id=1, source_target_pairs={{0,1},{1,0},{2,3},{3,2},{4,5},{5,4},{6,7},{7,6},{8,9},{9,8},{10,11... | collective-permute-start | bytes 786440 | tf_op jit(solution)/shard_map/ppermute | solution.py:388
  77.3 1.2 %collective-permute-done.16.b_ref = bf16[256,512]{1,0:T(8,128)(2,1)S(1)} collective-permute-done((bf16[256,512]{1,0:T(8,128)(2,1)S(1)}, bf16[256,512]{1,0:T(8,128)(2,1)S(1)}, u32[]{:S(2)}, u32[]{:S(2)}) %collective-permute-start.16) | collective-permute-done | bytes 262176 | tf_op jit(solution)/shard_map/ppermute | solution.py:388
  78.5 0.4 out_project.5
  78.9 2.7 %collective-permute-start.18 = (bf16[256,512]{1,0:T(8,128)(2,1)S(1)}, bf16[256,512]{1,0:T(8,128)(2,1)S(1)}, u32[]{:S(2)}, u32[]{:S(2)}) collective-permute-start(bf16[256,512]{1,0:T(8,128)(2,1)S(1)} %out_project.5), channel_id=1, source_target_pairs={{0,4},{1,5},{2,6},{3,7},{4,0},{5,1},{6,2},{7,3},{8,12},{9,13},{10,... | collective-permute-start | bytes 786440 | tf_op jit(solution)/shard_map/ppermute | solution.py:391
  81.7 0.7 out_project.4
  82.4 1.1 %collective-permute-start.17 = (bf16[256,512]{1,0:T(8,128)(2,1)S(1)}, bf16[256,512]{1,0:T(8,128)(2,1)S(1)}, u32[]{:S(2)}, u32[]{:S(2)}) collective-permute-start(bf16[256,512]{1,0:T(8,128)(2,1)S(1)} %get-tuple-element.73), channel_id=1, source_target_pairs={{0,2},{1,7},{2,4},{3,1},{4,6},{5,3},{6,0},{7,5},{8,10},{9,15},{10,... | collective-permute-start | bytes 786440 | tf_op jit(solution)/shard_map/ppermute | solution.py:391
  83.5 0.4 collective-permute-start.19
  83.9 0.4 out_project.3.mine
  84.4 3.7 %collective-permute-done.18.b = bf16[256,512]{1,0:T(8,128)(2,1)S(1)} collective-permute-done((bf16[256,512]{1,0:T(8,128)(2,1)S(1)}, bf16[256,512]{1,0:T(8,128)(2,1)S(1)}, u32[]{:S(2)}, u32[]{:S(2)}) %collective-permute-start.18) | collective-permute-done | bytes 262176 | tf_op jit(solution)/shard_map/ppermute | solution.py:391
  88.0 5.1 %collective-permute-done.17.a = bf16[256,512]{1,0:T(8,128)(2,1)S(1)} collective-permute-done((bf16[256,512]{1,0:T(8,128)(2,1)S(1)}, bf16[256,512]{1,0:T(8,128)(2,1)S(1)}, u32[]{:S(2)}, u32[]{:S(2)}) %collective-permute-start.17) | collective-permute-done | bytes 262176 | tf_op jit(solution)/shard_map/ppermute | solution.py:391
  93.1 1.3 %collective-permute-done.19.c = bf16[256,512]{1,0:T(8,128)(2,1)S(1)} collective-permute-done((bf16[256,512]{1,0:T(8,128)(2,1)S(1)}, bf16[256,512]{1,0:T(8,128)(2,1)S(1)}, u32[]{:S(2)}, u32[]{:S(2)}) %collective-permute-start.19) | collective-permute-done | bytes 262176 | tf_op jit(solution)/shard_map/ppermute | solution.py:391
  94.4 0.8 add_up.1
  (17 shorter events, 0.2 us)
Async XLA Ops:
  0.0 16.9 %collective-permute-start = (bf16[256,512]{1,0:T(8,128)(2,1)}, bf16[256,512]{1,0:T(8,128)(2,1)S(1)}, u32[]{:S(2)}, u32[]{:S(2)}) collective-permute-start(bf16[256,512]{1,0:T(8,128)(2,1)} %refs_0_.5), channel_id=1, source_target_pairs={{0,4},{1,5},{2,6},{3,7},{4,0},{5,1},{6,2},{7,3},{8,12},{9,13},{10,... | collective-permute-start | bytes 786440 | tf_op jit(solution)/shard_map/ppermute | solution.py:391
  2.7 12.0 %collective-permute-start.2 = (bf16[256,512]{1,0:T(8,128)(2,1)}, bf16[256,512]{1,0:T(8,128)(2,1)S(1)}, u32[]{:S(2)}, u32[]{:S(2)}) collective-permute-start(bf16[256,512]{1,0:T(8,128)(2,1)} %refs_0_.5), channel_id=1, source_target_pairs={{0,2},{1,7},{2,4},{3,1},{4,6},{5,3},{6,0},{7,5},{8,10},{9,15},{10,... | collective-permute-start | bytes 786440 | tf_op jit(solution)/shard_map/ppermute | solution.py:391
  3.6 12.4 %collective-permute-start.4 = (bf16[256,512]{1,0:T(8,128)(2,1)}, bf16[256,512]{1,0:T(8,128)(2,1)S(1)}, u32[]{:S(2)}, u32[]{:S(2)}) collective-permute-start(bf16[256,512]{1,0:T(8,128)(2,1)} %refs_0_.5), channel_id=1, source_target_pairs={{0,1},{1,0},{2,3},{3,2},{4,5},{5,4},{6,7},{7,6},{8,9},{9,8},{10,11... | collective-permute-start | bytes 786440 | tf_op jit(solution)/shard_map/ppermute | solution.py:388
  4.3 12.3 %collective-permute-start.3 = (bf16[256,512]{1,0:T(8,128)(2,1)}, bf16[256,512]{1,0:T(8,128)(2,1)S(1)}, u32[]{:S(2)}, u32[]{:S(2)}) collective-permute-start(bf16[256,512]{1,0:T(8,128)(2,1)} %refs_0_.5), channel_id=1, source_target_pairs={{0,6},{1,3},{2,0},{3,5},{4,2},{5,7},{6,4},{7,1},{8,14},{9,11},{10,... | collective-permute-start | bytes 786440 | tf_op jit(solution)/shard_map/ppermute | solution.py:391
  8.2 3.8 %copy-start.3 = (bf16[4,512,512]{2,1,0:T(8,128)(2,1)}, bf16[4,512,512]{2,1,0:T(8,128)(2,1)S(1)}, u32[]{:S(2)}) copy-start(bf16[4,512,512]{2,1,0:T(8,128)(2,1)S(1)} %get-tuple-element.67) | copy-start | bytes 6291460
  8.2 7.8 %copy-start = (bf16[256,512]{1,0:T(8,128)(2,1)S(1)}, bf16[256,512]{1,0:T(8,128)(2,1)}, u32[]{:S(2)}) copy-start(bf16[256,512]{1,0:T(8,128)(2,1)} %refs_0_.5) | copy-start | bytes 786436
  14.7 2.8 %collective-permute-start.5 = (bf16[256,512]{1,0:T(8,128)(2,1)S(1)}, bf16[256,512]{1,0:T(8,128)(2,1)S(1)}, u32[]{:S(2)}, u32[]{:S(2)}) collective-permute-start(bf16[256,512]{1,0:T(8,128)(2,1)S(1)} %collective-permute-done.2.refs_0_), channel_id=1, source_target_pairs={{0,1},{1,0},{2,3},{3,2},{4,5},{5,4},{6,7},{7,6},{8,9},{9,8},{10,11... | collective-permute-start | bytes 786440 | tf_op jit(solution)/shard_map/ppermute | solution.py:388
  16.6 1.6 %collective-permute-start.6 = (bf16[256,512]{1,0:T(8,128)(2,1)S(1)}, bf16[256,512]{1,0:T(8,128)(2,1)S(1)}, u32[]{:S(2)}, u32[]{:S(2)}) collective-permute-start(bf16[256,512]{1,0:T(8,128)(2,1)S(1)} %collective-permute-done.3.refs_1_), channel_id=1, source_target_pairs={{0,1},{1,0},{2,3},{3,2},{4,5},{5,4},{6,7},{7,6},{8,9},{9,8},{10,11... | collective-permute-start | bytes 786440 | tf_op jit(solution)/shard_map/ppermute | solution.py:388
  16.9 2.4 %copy-start.1 = (f32[128]{0:T(128)S(1)}, f32[128]{0:T(128)}, u32[]{:S(2)}) copy-start(f32[128]{0:T(128)} %param.12) | copy-start | bytes 1540
  16.9 2.3 %copy-start.2 = (f32[128]{0:T(128)S(1)}, f32[128]{0:T(128)}, u32[]{:S(2)}) copy-start(f32[128]{0:T(128)} %param.13) | copy-start | bytes 1540
  16.9 2.3 %collective-permute-start.1 = (bf16[256,512]{1,0:T(8,128)(2,1)S(1)}, bf16[256,512]{1,0:T(8,128)(2,1)S(1)}, u32[]{:S(2)}, u32[]{:S(2)}) collective-permute-start(bf16[256,512]{1,0:T(8,128)(2,1)S(1)} %collective-permute-done.refs_0_), channel_id=1, source_target_pairs={{0,1},{1,0},{2,3},{3,2},{4,5},{5,4},{6,7},{7,6},{8,9},{9,8},{10,11... | collective-permute-start | bytes 786440 | tf_op jit(solution)/shard_map/ppermute | solution.py:388
  20.3 5.7 %collective-permute-start.7 = (bf16[256,256]{1,0:T(8,128)(2,1)S(1)}, bf16[256,256]{1,0:T(8,128)(2,1)S(1)}, u32[]{:S(2)}, u32[]{:S(2)}) collective-permute-start(bf16[256,256]{1,0:T(8,128)(2,1)S(1)} %get-tuple-element.54.refs_0_.refs_3_.refs_2_), channel_id=1, source_target_pairs={{0,32},{8,40},{16,48},{24,56},{32,64},{40,72},{48,80},{56,88},{64,... | collective-permute-start | bytes 393224 | tf_op jit(solution)/shard_map/ppermute | solution.py:401
  26.0 5.4 %collective-permute-start.8 = (bf16[256,256]{1,0:T(8,128)(2,1)S(1)}, bf16[256,256]{1,0:T(8,128)(2,1)S(1)}, u32[]{:S(2)}, u32[]{:S(2)}) collective-permute-start(bf16[256,256]{1,0:T(8,128)(2,1)S(1)} %collective-permute-done.7.refs_1_.refs_4_.refs_0_), channel_id=1, source_target_pairs={{0,32},{8,40},{16,48},{24,56},{32,64},{40,72},{48,80},{56,88},{64,... | collective-permute-start | bytes 393224 | tf_op jit(solution)/shard_map/ppermute | solution.py:401
  29.4 11.5 %collective-permute-start.10 = (bf16[256,256]{1,0:T(8,128)(2,1)S(1)}, bf16[256,256]{1,0:T(8,128)(2,1)S(1)}, u32[]{:S(2)}, u32[]{:S(2)}) collective-permute-start(bf16[256,256]{1,0:T(8,128)(2,1)S(1)} %get-tuple-element.54.refs_0_.refs_3_.refs_2_), channel_id=1, source_target_pairs={{0,128},{8,136},{16,144},{24,152},{32,160},{40,168},{48,176},{56,1... | collective-permute-start | bytes 393224 | tf_op jit(solution)/shard_map/ppermute | solution.py:401
  31.3 9.5 %collective-permute-start.9 = (bf16[256,256]{1,0:T(8,128)(2,1)S(1)}, bf16[256,256]{1,0:T(8,128)(2,1)S(1)}, u32[]{:S(2)}, u32[]{:S(2)}) collective-permute-start(bf16[256,256]{1,0:T(8,128)(2,1)S(1)} %collective-permute-done.8.refs_2_.refs_1_.refs_3_), channel_id=1, source_target_pairs={{0,32},{8,40},{16,48},{24,56},{32,64},{40,72},{48,80},{56,88},{64,... | collective-permute-start | bytes 393224 | tf_op jit(solution)/shard_map/ppermute | solution.py:401
  36.9 7.8 %collective-permute-start.12 = (bf16[768,256]{1,0:T(8,128)(2,1)S(1)}, bf16[768,256]{1,0:T(8,128)(2,1)S(1)}, u32[]{:S(2)}, u32[]{:S(2)}) collective-permute-start(bf16[768,256]{1,0:T(8,128)(2,1)S(1)} %get-tuple-element.56), channel_id=1, source_target_pairs={{0,8},{1,25},{2,10},{3,27},{4,12},{5,29},{6,14},{7,31},{8,0},{9,17... | collective-permute-start | bytes 1179656 | tf_op jit(solution)/shard_map/ppermute | solution.py:410
  40.9 3.9 %copy-start.4 = (bf16[4,512,512]{2,1,0:T(8,128)(2,1)S(1)}, bf16[4,512,512]{2,1,0:T(8,128)(2,1)}, u32[]{:S(2)}) copy-start(bf16[4,512,512]{2,1,0:T(8,128)(2,1)} %copy-done.3) | copy-start | bytes 6291460
  40.9 13.3 %collective-permute-start.11 = (bf16[512,256]{1,0:T(8,128)(2,1)S(1)}, bf16[512,256]{1,0:T(8,128)(2,1)S(1)}, u32[]{:S(2)}, u32[]{:S(2)}) collective-permute-start(bf16[512,256]{1,0:T(8,128)(2,1)S(1)} %get-tuple-element.55), channel_id=1, source_target_pairs={{0,8},{1,25},{2,10},{3,27},{4,12},{5,29},{6,14},{7,31},{8,0},{9,17... | collective-permute-start | bytes 786440 | tf_op jit(solution)/shard_map/ppermute | solution.py:410
  44.8 17.9 %collective-permute-start.15 = (bf16[4,512,512]{2,1,0:T(8,128)(2,1)S(1)}, bf16[4,512,512]{2,1,0:T(8,128)(2,1)S(1)}, u32[]{:S(2)}, u32[]{:S(2)}) collective-permute-start(bf16[4,512,512]{2,1,0:T(8,128)(2,1)S(1)} %copy-done.4), channel_id=1, source_target_pairs={{0,1},{1,0},{2,3},{3,2},{4,5},{5,4},{6,7},{7,6},{8,9},{9,8},{10,11... | collective-permute-start | bytes 6291464 | tf_op jit(solution)/shard_map/ppermute | solution.py:388
  53.7 8.3 %collective-permute-start.13 = (bf16[1024,256]{1,0:T(8,128)(2,1)S(1)}, bf16[1024,256]{1,0:T(8,128)(2,1)S(1)}, u32[]{:S(2)}, u32[]{:S(2)}) collective-permute-start(bf16[1024,256]{1,0:T(8,128)(2,1)S(1)} %get-tuple-element.63), channel_id=1, source_target_pairs={{0,24},{1,9},{2,26},{3,11},{4,28},{5,13},{6,30},{7,15},{8,16},{9,1... | collective-permute-start | bytes 1572872 | tf_op jit(solution)/shard_map/ppermute | solution.py:410
  62.1 8.4 %collective-permute-start.14 = (bf16[1024,256]{1,0:T(8,128)(2,1)S(1)}, bf16[1024,256]{1,0:T(8,128)(2,1)S(1)}, u32[]{:S(2)}, u32[]{:S(2)}) collective-permute-start(bf16[1024,256]{1,0:T(8,128)(2,1)S(1)} %get-tuple-element.64), channel_id=1, source_target_pairs={{0,24},{1,9},{2,26},{3,11},{4,28},{5,13},{6,30},{7,15},{8,16},{9,1... | collective-permute-start | bytes 1572872 | tf_op jit(solution)/shard_map/ppermute | solution.py:410
  73.1 5.4 %collective-permute-start.16 = (bf16[256,512]{1,0:T(8,128)(2,1)S(1)}, bf16[256,512]{1,0:T(8,128)(2,1)S(1)}, u32[]{:S(2)}, u32[]{:S(2)}) collective-permute-start(bf16[256,512]{1,0:T(8,128)(2,1)S(1)} %get-tuple-element.70.a_ref), channel_id=1, source_target_pairs={{0,1},{1,0},{2,3},{3,2},{4,5},{5,4},{6,7},{7,6},{8,9},{9,8},{10,11... | collective-permute-start | bytes 786440 | tf_op jit(solution)/shard_map/ppermute | solution.py:388
  78.9 9.1 %collective-permute-start.18 = (bf16[256,512]{1,0:T(8,128)(2,1)S(1)}, bf16[256,512]{1,0:T(8,128)(2,1)S(1)}, u32[]{:S(2)}, u32[]{:S(2)}) collective-permute-start(bf16[256,512]{1,0:T(8,128)(2,1)S(1)} %out_project.5), channel_id=1, source_target_pairs={{0,4},{1,5},{2,6},{3,7},{4,0},{5,1},{6,2},{7,3},{8,12},{9,13},{10,... | collective-permute-start | bytes 786440 | tf_op jit(solution)/shard_map/ppermute | solution.py:391
  82.4 10.7 %collective-permute-start.17 = (bf16[256,512]{1,0:T(8,128)(2,1)S(1)}, bf16[256,512]{1,0:T(8,128)(2,1)S(1)}, u32[]{:S(2)}, u32[]{:S(2)}) collective-permute-start(bf16[256,512]{1,0:T(8,128)(2,1)S(1)} %get-tuple-element.73), channel_id=1, source_target_pairs={{0,2},{1,7},{2,4},{3,1},{4,6},{5,3},{6,0},{7,5},{8,10},{9,15},{10,... | collective-permute-start | bytes 786440 | tf_op jit(solution)/shard_map/ppermute | solution.py:391
  83.5 11.0 %collective-permute-start.19 = (bf16[256,512]{1,0:T(8,128)(2,1)S(1)}, bf16[256,512]{1,0:T(8,128)(2,1)S(1)}, u32[]{:S(2)}, u32[]{:S(2)}) collective-permute-start(bf16[256,512]{1,0:T(8,128)(2,1)S(1)} %get-tuple-element.74), channel_id=1, source_target_pairs={{0,6},{1,3},{2,0},{3,5},{4,2},{5,7},{6,4},{7,1},{8,14},{9,11},{10,... | collective-permute-start | bytes 786440 | tf_op jit(solution)/shard_map/ppermute | solution.py:391

commit v2 on v1

--- a/solution.py
+++ b/solution.py
@@ -447,43 +447,41 @@
     attn = (start, queries, start_col, index_col)
     r0 = kv
     r1 = along_z(r0, 1)
-    r4 = along_z(r0, 4)
     r2 = along_z(r1, 1)
     r3 = along_z(r2, 1)
-    x012, _ = pack([r0, r1, r2], [(0, 0), (1, 0), (2, 0)], tok)
-    s012 = swap_y(x012, 0)
-    o, _ = attend(*attn, [(r0, [(0, 0)]), (r1, [(1, 0)])])
-    x34, flag_34 = pack([r3, r4], [(0, 0), (1, 0)], tok)
-    s34 = swap_y(x34, 0)
-    x_near, flag_n = pack(
-        [r1, r2, s012], [(0, 0), (1, 0), (2, 1), (2, 2)], tok, flags=[hold(r3, r4), flag_34]
-    )
-    near = swap_y(x_near, 1)
-    w_send, flags = after([flag_n], w_send)
-    w_sib = sibling(w_send)
-    o, flag_b = attend(*attn, [(r2, [(2, 0)]), (s012, [(0, 1), (1, 1), (2, 1)])], o, flags=flags)
+    r4 = along_z(r3, 1)
+    x01, flag_01 = pack([r0, r1], [(0, 0), (1, 0)], tok)
+    s01 = swap_y(x01, 0)
+    o, flag_a = attend(*attn, [(r0, [(0, 0)]), (r1, [(1, 0)])], flags=[flag_01])
+    x_one, flag_1 = pack([r1, s01], [(0, 0), (1, 1)], tok)
+    near_one = swap_y(x_one, 1)
+    o, flag_b = attend(*attn, [(s01, [(0, 1), (1, 1)]), (r2, [(2, 0)])], o, flags=[flag_1])
+    x23, flag_23 = pack([r2, r3], [(0, 0), (1, 0)], tok)
+    s23 = swap_y(x23, 0)
+    s4 = swap_y(r4, 0)
+    x_two, flag_2 = pack(
+        [r2, s23, r3], [(0, 0), (1, 0), (2, 0), (1, 1)], tok, flags=[hold(r4)]
+    )
+    near_two = swap_y(x_two, 1)
+    o, flag_c = attend(
+        *attn,
+        [(near_one, [(1, 2), (1, 3)]), (r3, [(3, 0)]), (s23, [(2, 1), (3, 1)])],
+        o,
+        flags=[flag_2],
+    )
     x_last, flag_l = pack(
-        [r3, s34, r0, r4, s012],
-        [(0, 0), (1, 0), (0, (2, 0), (3, 0)), (1, (4, 0), (1, 1))],
-        tok,
-        flags=[flag_b, hold(s34), near],
+        [r0, r4, s01, s4], [(0, (0, 0), (1, 0)), (1, (2, 0), (3, 0))], tok, flags=[hold(s4)]
     )
     last = swap_y(x_last, 1)
-    w_sib, flag_w = fetch(w_sib)
+    w_send, _ = after([flag_l], w_send)
+    w_sib, flag_w = fetch(sibling(w_send))
     o, _ = attend(
         *attn,
-        [
-            (near, [(1, 2), (2, 2), (1, 3), (2, 3)]),
-            (r3, [(3, 0)]),
-            (r4, [(4, 0)]),
-            (s34, [(3, 1), (4, 1)]),
-        ],
+        [(near_two, [(2, 2), (2, 3), (3, 2), (3, 3)]), (r4, [(4, 0)]), (s4, [(4, 1)])],
         o,
-        flags=[flag_l, flag_w],
-    )
-    attended, _ = attend(
-        *attn, [(last, [(3, 2), (3, 3), (None, 2), (None, 3)])], o, final=True
-    )
+        flags=[flag_l, flag_w, hold(near_two)],
+    )
+    attended, _ = attend(*attn, [(last, [(None, 2), (None, 3)])], o, final=True)
 
     attended_sib = sibling(attended)
     (p2,) = out_project((0,), (BF,), attended, attended_sib, w_own, w_sib)

time: 95.4 us -> 87.9 us (0.921)
  the two profiles are of different devices: /device:TPU:121 before, /device:TPU:1 now
where the time goes in v2:
time: 87.9 us; the launch traced here: 86.7 us
  waiting for transfers between devices  35.2 us (40%)
  starting transfers between devices  29.7 us (34%)
  Pallas kernels  19.1 us (22%)
  other arithmetic  1.6 us (2%)
  local copies, waits for them, and re-layouts  0.89 us (1%)
    ppermute x4, waiting for transfers between devices, along_z(): lax.ppermute(a, 'seq', [(i, (i // ny + d) % nz * ny + i % ny) for i in ra...  15.7 us
    ppermute x6, waiting for transfers between devices, along_x(): lax.ppermute(a, 'tp', [(i, (i // 2 + (d if i % 2 == 0 else -d)) % nx * 2...  11 us
    ppermute x6, starting transfers between devices, swap_y(): return lax.ppermute(a, ('seq', 'tp'), pairs)  10.3 us
    ppermute x6, starting transfers between devices, along_x(): lax.ppermute(a, 'tp', [(i, (i // 2 + (d if i % 2 == 0 else -d)) % nx * 2...  10 us
    ppermute x6, starting transfers between devices, sibling(): return lax.ppermute(a, 'tp', [(i, i ^ 1) for i in range(tps)])  7.68 us
    pallas_call x5, Pallas kernels, attend(): pl.pallas_call(functools.partial(attend_kernel, layout, first, final, len...  6.57 us
    ppermute x6, waiting for transfers between devices, swap_y(): return lax.ppermute(a, ('seq', 'tp'), pairs)  6.56 us
    pallas_call x2, Pallas kernels, stage(): pl.pallas_call(functools.partial(stage_kernel, plan, len(arrays)), in_spe...  6.01 us
  transfers between devices with their start and end apart: 22, of which 13 were waited for; matrix products, arithmetic and copies ran while one was open for 3% of the time, Pallas kernels for 18%

profile of v2, /device:TPU:1, one launch (start us, length us, event | category | flops | bytes accessed | tf_op | source)
XLA Modules:
  0.0 86.7 jit_solution(5789670579313298806)
XLA Ops:
  0.0 3.6 %collective-permute-start = (bf16[256,512]{1,0:T(8,128)(2,1)}, bf16[256,512]{1,0:T(8,128)(2,1)S(1)}, u32[]{:S(2)}, u32[]{:S(2)}) collective-permute-start(bf16[256,512]{1,0:T(8,128)(2,1)} %refs_0_.5), channel_id=1, source_target_pairs={{0,4},{1,5},{2,6},{3,7},{4,0},{5,1},{6,2},{7,3},{8,12},{9,13},{10,... | collective-permute-start | bytes 786440 | tf_op jit(solution)/shard_map/ppermute | solution.py:391
  3.6 0.9 collective-permute-start.2
  4.4 0.7 collective-permute-start.4
  5.1 1.3 %collective-permute-start.3 = (bf16[256,512]{1,0:T(8,128)(2,1)}, bf16[256,512]{1,0:T(8,128)(2,1)S(1)}, u32[]{:S(2)}, u32[]{:S(2)}) collective-permute-start(bf16[256,512]{1,0:T(8,128)(2,1)} %refs_0_.5), channel_id=1, source_target_pairs={{0,6},{1,3},{2,0},{3,5},{4,2},{5,7},{6,4},{7,1},{8,14},{9,11},{10,... | collective-permute-start | bytes 786440 | tf_op jit(solution)/shard_map/ppermute | solution.py:391
  6.5 0.7 copy.16
  7.2 0.1 reduce
  7.3 0.7 select_reduce_fusion.start_s
  8.1 2.3 %stage_out.1 = (bf16[4,512,512]{2,1,0:T(8,128)(2,1)S(1)}, bf16[4,512,512]{2,1,0:T(8,128)(2,1)S(1)}, f32[8,128]{1,0:T(8,128)S(1)}) custom-call(bf16[512,4096]{1,0:T(8,128)(2,1)} %refs_0_.4), custom_call_target="tpu_custom_call" | custom-call | bytes 8388608 | tf_op jit(solution)/shard_map/stage_out/pallas_call | solution.py:111
  10.4 0.0 copy-start
  10.4 3.7 %stage_in.1 = (bf16[8,512,768]{2,1,0:T(8,128)(2,1)S(1)}, f32[8,128]{1,0:T(8,128)S(1)}) custom-call(bf16[4096,512]{1,0:T(8,128)(2,1)} %refs_0_.3, bf16[4096,128]{1,0:T(8,128)(2,1)} %refs_1_.1, bf16[4096,128]{1,0:T(8,128)(2,1)} %refs_2_.1), custom_call_target="tpu_custom_call" | custom-call | bytes 12582912 | tf_op jit(solution)/shard_map/stage_in/pallas_call | solution.py:111
  14.2 0.5 fusion
  14.7 0.9 collective-permute-done.2.refs_0_
  15.6 1.4 %collective-permute-start.5 = (bf16[256,512]{1,0:T(8,128)(2,1)S(1)}, bf16[256,512]{1,0:T(8,128)(2,1)S(1)}, u32[]{:S(2)}, u32[]{:S(2)}) collective-permute-start(bf16[256,512]{1,0:T(8,128)(2,1)S(1)} %collective-permute-done.2.refs_0_), channel_id=1, source_target_pairs={{0,1},{1,0},{2,3},{3,2},{4,5},{5,4},{6,7},{7,6},{8,9},{9,8},{10,11... | collective-permute-start | bytes 786440 | tf_op jit(solution)/shard_map/ppermute | solution.py:388
  16.9 0.0 collective-permute-done.4.refs_1_
  16.9 0.6 project.3.refs_5_
  17.5 0.0 collective-permute-done.3.refs_1_
  17.5 0.1 collective-permute-start.6
  17.6 0.1 pad_maximum_fusion
  17.8 0.0 copy-start.1
  17.8 0.0 copy-start.2
  17.8 0.6 collective-permute-start.1
  18.4 0.0 collective-permute-done.5.refs_2_
  18.4 0.7 collective-permute-done.6.refs_3_
  19.1 1.0 %project.4.refs_3_ = f32[256,768]{1,0:T(8,128)S(1)} custom-call(bf16[256,512]{1,0:T(8,128)(2,1)S(1)} %collective-permute-done.2.refs_0_, bf16[256,512]{1,0:T(8,128)(2,1)S(1)} %collective-permute-done.3.refs_1_, bf16[256,512]{1,0:T(8,128)(2,1)S(1)} %collective-permute-done.5.refs_2_, bf16[256,512]{1,0:T(8,128)(2,1)S(1)} %collective-permute-done.6.refs_3_, ...), custom_call_target="tpu_custom_call" | custom-call | flops 1610612736 | bytes 3145728 | tf_op jit(solution)/shard_map/project/pallas_call | solution.py:233
  20.1 0.0 collective-permute-done.1.refs_1_
  20.2 1.0 %project.5 = (bf16[1024,128]{1,0:T(8,128)(2,1)S(1)}, bf16[256,256]{1,0:T(8,128)(2,1)S(1)}) custom-call(bf16[256,512]{1,0:T(8,128)(2,1)S(1)} %collective-permute-done.refs_0_, bf16[256,512]{1,0:T(8,128)(2,1)S(1)} %collective-permute-done.1.refs_1_, bf16[8,512,768]{2,1,0:T(8,128)(2,1)S(1)} %get-tuple-element.42.refs_2_.refs_4_, ...), custom_call_target="tpu_custom_call" | custom-call | flops 805306368 | bytes 1572864 | tf_op jit(solution)/shard_map/project/pallas_call | solution.py:233
  21.2 1.7 %collective-permute-start.7 = (bf16[256,256]{1,0:T(8,128)(2,1)S(1)}, bf16[256,256]{1,0:T(8,128)(2,1)S(1)}, u32[]{:S(2)}, u32[]{:S(2)}) collective-permute-start(bf16[256,256]{1,0:T(8,128)(2,1)S(1)} %get-tuple-element.55.refs_0_.refs_3_), channel_id=1, source_target_pairs={{0,32},{8,40},{16,48},{24,56},{32,64},{40,72},{48,80},{56,88},{64,... | collective-permute-start | bytes 393224 | tf_op jit(solution)/shard_map/ppermute | solution.py:401
  22.9 7.7 %collective-permute-done.7.refs_1_.refs_0_.refs_4_ = bf16[256,256]{1,0:T(8,128)(2,1)S(1)} collective-permute-done((bf16[256,256]{1,0:T(8,128)(2,1)S(1)}, bf16[256,256]{1,0:T(8,128)(2,1)S(1)}, u32[]{:S(2)}, u32[]{:S(2)}) %collective-permute-start.7) | collective-permute-done | bytes 131104 | tf_op jit(solution)/shard_map/ppermute | solution.py:401
  30.5 0.0 collective-permute-start.8
  30.5 0.7 pack.5
  31.3 2.7 %collective-permute-start.11 = (bf16[512,256]{1,0:T(8,128)(2,1)}, bf16[512,256]{1,0:T(8,128)(2,1)S(1)}, u32[]{:S(2)}, u32[]{:S(2)}) collective-permute-start(bf16[512,256]{1,0:T(8,128)(2,1)} %get-tuple-element.56), channel_id=1, source_target_pairs={{0,8},{1,25},{2,10},{3,27},{4,12},{5,29},{6,14},{7,31},{8,0},{9,17... | collective-permute-start | bytes 786440 | tf_op jit(solution)/shard_map/ppermute | solution.py:410
  34.0 2.1 %collective-permute-done.8.refs_0_.refs_4_ = bf16[256,256]{1,0:T(8,128)(2,1)S(1)} collective-permute-done((bf16[256,256]{1,0:T(8,128)(2,1)S(1)}, bf16[256,256]{1,0:T(8,128)(2,1)S(1)}, u32[]{:S(2)}, u32[]{:S(2)}) %collective-permute-start.8) | collective-permute-done | bytes 131104 | tf_op jit(solution)/shard_map/ppermute | solution.py:401
  36.1 5.0 %collective-permute-done.9.refs_1_.refs_2_.refs_4_ = bf16[256,256]{1,0:T(8,128)(2,1)S(1)} collective-permute-done((bf16[256,256]{1,0:T(8,128)(2,1)S(1)}, bf16[256,256]{1,0:T(8,128)(2,1)S(1)}, u32[]{:S(2)}, u32[]{:S(2)}) %collective-permute-start.9) | collective-permute-done | bytes 131104 | tf_op jit(solution)/shard_map/ppermute | solution.py:401
  41.1 0.0 collective-permute-start.10
  41.1 0.1 copy.21.refs_1_
  41.3 1.4 %collective-permute-start.16 = (bf16[512,256]{1,0:T(8,128)(2,1)S(1)}, bf16[512,256]{1,0:T(8,128)(2,1)S(1)}, u32[]{:S(2)}, u32[]{:S(2)}) collective-permute-start(bf16[512,256]{1,0:T(8,128)(2,1)S(1)} %get-tuple-element.60), channel_id=1, source_target_pairs={{0,24},{1,9},{2,26},{3,11},{4,28},{5,13},{6,30},{7,15},{8,16},{9,1... | collective-permute-start | bytes 786440 | tf_op jit(solution)/shard_map/ppermute | solution.py:410
  42.7 0.6 pack.7
  43.3 1.9 %collective-permute-start.14 = (bf16[512,256]{1,0:T(8,128)(2,1)S(1)}, bf16[512,256]{1,0:T(8,128)(2,1)S(1)}, u32[]{:S(2)}, u32[]{:S(2)}) collective-permute-start(bf16[512,256]{1,0:T(8,128)(2,1)S(1)} %get-tuple-element.58), channel_id=1, source_target_pairs={{0,8},{1,25},{2,10},{3,27},{4,12},{5,29},{6,14},{7,31},{8,0},{9,17... | collective-permute-start | bytes 786440 | tf_op jit(solution)/shard_map/ppermute | solution.py:410
  45.2 1.0 %collective-permute-done.10.refs_1_.refs_0_.refs_4_ = bf16[256,256]{1,0:T(8,128)(2,1)S(1)} collective-permute-done((bf16[256,256]{1,0:T(8,128)(2,1)S(1)}, bf16[256,256]{1,0:T(8,128)(2,1)S(1)}, u32[]{:S(2)}, u32[]{:S(2)}) %collective-permute-start.10) | collective-permute-done | bytes 131104 | tf_op jit(solution)/shard_map/ppermute | solution.py:401
  46.1 2.7 %collective-permute-start.12 = (bf16[256,256]{1,0:T(8,128)(2,1)S(1)}, bf16[256,256]{1,0:T(8,128)(2,1)S(1)}, u32[]{:S(2)}, u32[]{:S(2)}) collective-permute-start(bf16[256,256]{1,0:T(8,128)(2,1)S(1)} %collective-permute-done.10.refs_1_.refs_0_.refs_4_), channel_id=1, source_target_pairs={{0,8},{1,25},{2,10},{3,27},{4,12},{5,29},{6,14},{7,31},{8,0},{9,17... | collective-permute-start | bytes 393224 | tf_op jit(solution)/shard_map/ppermute | solution.py:410
  48.9 2.6 %collective-permute-done.14.refs_1_.refs_5_ = bf16[512,256]{1,0:T(8,128)(2,1)S(1)} collective-permute-done((bf16[512,256]{1,0:T(8,128)(2,1)S(1)}, bf16[512,256]{1,0:T(8,128)(2,1)S(1)}, u32[]{:S(2)}, u32[]{:S(2)}) %collective-permute-start.14) | collective-permute-done | bytes 262176 | tf_op jit(solution)/shard_map/ppermute | solution.py:410
  51.5 0.1 collective-permute-start.15
  51.6 2.5 %collective-permute-done.12.refs_0_.refs_3_.refs_5_ = bf16[256,256]{1,0:T(8,128)(2,1)S(1)} collective-permute-done((bf16[256,256]{1,0:T(8,128)(2,1)S(1)}, bf16[256,256]{1,0:T(8,128)(2,1)S(1)}, u32[]{:S(2)}, u32[]{:S(2)}) %collective-permute-start.12) | collective-permute-done | bytes 131104 | tf_op jit(solution)/shard_map/ppermute | solution.py:410
  54.2 2.2 %collective-permute-start.17 = (bf16[4,512,512]{2,1,0:T(8,128)(2,1)S(1)}, bf16[4,512,512]{2,1,0:T(8,128)(2,1)S(1)}, u32[]{:S(2)}, u32[]{:S(2)}) collective-permute-start(bf16[4,512,512]{2,1,0:T(8,128)(2,1)S(1)} %copy-done.4), channel_id=1, source_target_pairs={{0,1},{1,0},{2,3},{3,2},{4,5},{5,4},{6,7},{7,6},{8,9},{9,8},{10,11... | collective-permute-start | bytes 6291464 | tf_op jit(solution)/shard_map/ppermute | solution.py:388
  56.4 1.7 %attend.5 = (f32[1024,256]{1,0:T(8,128)S(1)}, f32[8,128]{1,0:T(8,128)}) custom-call(s32[256]{0:T(256)S(1)} %select_reduce_fusion.start_s, bf16[1024,128]{1,0:T(8,128)(2,1)S(1)} %get-tuple-element.52.refs_0_, s32[256,1]{1,0:T(8,128)S(1)} %copy.21.refs_1_, s32[256,1]{1,0:T(8,128)S(1)} %iota_add_fusion.refs_2_, ...), custom_call_target="tpu_custom_call" | custom-call | flops 536870912 | bytes 2097152 | tf_op jit(solution)/shard_map/attend/pallas_call | solution.py:316
  58.0 1.2 %attend.6 = (f32[1024,256]{1,0:T(8,128)S(1)}, f32[8,128]{1,0:T(8,128)}) custom-call(s32[256]{0:T(256)S(1)} %select_reduce_fusion.start_s, bf16[1024,128]{1,0:T(8,128)(2,1)S(1)} %get-tuple-element.52.refs_0_, s32[256,1]{1,0:T(8,128)S(1)} %copy.21.refs_1_, s32[256,1]{1,0:T(8,128)S(1)} %iota_add_fusion.refs_2_, ...), custom_call_target="tpu_custom_call" | custom-call | flops 805306368 | bytes 2097152 | tf_op jit(solution)/shard_map/attend/pallas_call | solution.py:316
  59.3 1.5 %collective-permute-start.13 = (bf16[512,256]{1,0:T(8,128)(2,1)S(1)}, bf16[512,256]{1,0:T(8,128)(2,1)S(1)}, u32[]{:S(2)}, u32[]{:S(2)}) collective-permute-start(bf16[512,256]{1,0:T(8,128)(2,1)S(1)} %get-tuple-element.57), channel_id=1, source_target_pairs={{0,24},{1,9},{2,26},{3,11},{4,28},{5,13},{6,30},{7,15},{8,16},{9,1... | collective-permute-start | bytes 786440 | tf_op jit(solution)/shard_map/ppermute | solution.py:410
  60.7 1.2 %attend.7 = (f32[1024,256]{1,0:T(8,128)S(1)}, f32[8,128]{1,0:T(8,128)}) custom-call(s32[256]{0:T(256)S(1)} %select_reduce_fusion.start_s, bf16[1024,128]{1,0:T(8,128)(2,1)S(1)} %get-tuple-element.52.refs_0_, s32[256,1]{1,0:T(8,128)S(1)} %copy.21.refs_1_, s32[256,1]{1,0:T(8,128)S(1)} %iota_add_fusion.refs_2_, ...), custom_call_target="tpu_custom_call" | custom-call | flops 1342177280 | bytes 2097152 | tf_op jit(solution)/shard_map/attend/pallas_call | solution.py:316
  62.0 0.2 fetch.1
  62.1 1.2 %attend.8 = (f32[1024,256]{1,0:T(8,128)S(1)}, f32[8,128]{1,0:T(8,128)}) custom-call(s32[256]{0:T(256)S(1)} %select_reduce_fusion.start_s, bf16[1024,128]{1,0:T(8,128)(2,1)S(1)} %get-tuple-element.52.refs_0_, s32[256,1]{1,0:T(8,128)S(1)} %copy.21.refs_1_, s32[256,1]{1,0:T(8,128)S(1)} %iota_add_fusion.refs_2_, ...), custom_call_target="tpu_custom_call" | custom-call | flops 1610612736 | bytes 2097152 | tf_op jit(solution)/shard_map/attend/pallas_call | solution.py:316
  63.4 1.4 %collective-permute-done.13.refs_3_ = bf16[512,256]{1,0:T(8,128)(2,1)S(1)} collective-permute-done((bf16[512,256]{1,0:T(8,128)(2,1)S(1)}, bf16[512,256]{1,0:T(8,128)(2,1)S(1)}, u32[]{:S(2)}, u32[]{:S(2)}) %collective-permute-start.13) | collective-permute-done | bytes 262176 | tf_op jit(solution)/shard_map/ppermute | solution.py:410
  64.8 1.2 %attend.9 = (bf16[256,512]{1,0:T(8,128)(2,1)S(1)}, f32[8,128]{1,0:T(8,128)}) custom-call(s32[256]{0:T(256)S(1)} %select_reduce_fusion.start_s, bf16[1024,128]{1,0:T(8,128)(2,1)S(1)} %get-tuple-element.52.refs_0_, s32[256,1]{1,0:T(8,128)S(1)} %copy.21.refs_1_, s32[256,1]{1,0:T(8,128)S(1)} %iota_add_fusion.refs_2_, ...), custom_call_target="tpu_custom_call" | custom-call | flops 536870912 | bytes 2097152 | tf_op jit(solution)/shard_map/attend/pallas_call | solution.py:316
  66.0 2.8 %collective-permute-start.18 = (bf16[256,512]{1,0:T(8,128)(2,1)S(1)}, bf16[256,512]{1,0:T(8,128)(2,1)S(1)}, u32[]{:S(2)}, u32[]{:S(2)}) collective-permute-start(bf16[256,512]{1,0:T(8,128)(2,1)S(1)} %get-tuple-element.72.a_ref), channel_id=1, source_target_pairs={{0,1},{1,0},{2,3},{3,2},{4,5},{5,4},{6,7},{7,6},{8,9},{9,8},{10,11... | collective-permute-start | bytes 786440 | tf_op jit(solution)/shard_map/ppermute | solution.py:388
  68.8 1.2 %collective-permute-done.18.b_ref = bf16[256,512]{1,0:T(8,128)(2,1)S(1)} collective-permute-done((bf16[256,512]{1,0:T(8,128)(2,1)S(1)}, bf16[256,512]{1,0:T(8,128)(2,1)S(1)}, u32[]{:S(2)}, u32[]{:S(2)}) %collective-permute-start.18) | collective-permute-done | bytes 262176 | tf_op jit(solution)/shard_map/ppermute | solution.py:388
  69.9 0.4 out_project.5
  70.4 2.7 %collective-permute-start.20 = (bf16[256,512]{1,0:T(8,128)(2,1)S(1)}, bf16[256,512]{1,0:T(8,128)(2,1)S(1)}, u32[]{:S(2)}, u32[]{:S(2)}) collective-permute-start(bf16[256,512]{1,0:T(8,128)(2,1)S(1)} %out_project.5), channel_id=1, source_target_pairs={{0,4},{1,5},{2,6},{3,7},{4,0},{5,1},{6,2},{7,3},{8,12},{9,13},{10,... | collective-permute-start | bytes 786440 | tf_op jit(solution)/shard_map/ppermute | solution.py:391
  73.1 0.7 out_project.4
  73.8 1.1 %collective-permute-start.19 = (bf16[256,512]{1,0:T(8,128)(2,1)S(1)}, bf16[256,512]{1,0:T(8,128)(2,1)S(1)}, u32[]{:S(2)}, u32[]{:S(2)}) collective-permute-start(bf16[256,512]{1,0:T(8,128)(2,1)S(1)} %get-tuple-element.75), channel_id=1, source_target_pairs={{0,2},{1,7},{2,4},{3,1},{4,6},{5,3},{6,0},{7,5},{8,10},{9,15},{10,... | collective-permute-start | bytes 786440 | tf_op jit(solution)/shard_map/ppermute | solution.py:391
  74.9 0.4 collective-permute-start.21
  75.4 0.4 out_project.3.mine
  75.8 3.7 %collective-permute-done.20.b = bf16[256,512]{1,0:T(8,128)(2,1)S(1)} collective-permute-done((bf16[256,512]{1,0:T(8,128)(2,1)S(1)}, bf16[256,512]{1,0:T(8,128)(2,1)S(1)}, u32[]{:S(2)}, u32[]{:S(2)}) %collective-permute-start.20) | collective-permute-done | bytes 262176 | tf_op jit(solution)/shard_map/ppermute | solution.py:391
  79.5 5.3 %collective-permute-done.19.a = bf16[256,512]{1,0:T(8,128)(2,1)S(1)} collective-permute-done((bf16[256,512]{1,0:T(8,128)(2,1)S(1)}, bf16[256,512]{1,0:T(8,128)(2,1)S(1)}, u32[]{:S(2)}, u32[]{:S(2)}) %collective-permute-start.19) | collective-permute-done | bytes 262176 | tf_op jit(solution)/shard_map/ppermute | solution.py:391
  84.8 1.1 %collective-permute-done.21.c = bf16[256,512]{1,0:T(8,128)(2,1)S(1)} collective-permute-done((bf16[256,512]{1,0:T(8,128)(2,1)S(1)}, bf16[256,512]{1,0:T(8,128)(2,1)S(1)}, u32[]{:S(2)}, u32[]{:S(2)}) %collective-permute-start.21) | collective-permute-done | bytes 262176 | tf_op jit(solution)/shard_map/ppermute | solution.py:391
  85.9 0.8 add_up.1
  (24 shorter events, 0.2 us)
Async XLA Ops:
  0.0 17.8 %collective-permute-start = (bf16[256,512]{1,0:T(8,128)(2,1)}, bf16[256,512]{1,0:T(8,128)(2,1)S(1)}, u32[]{:S(2)}, u32[]{:S(2)}) collective-permute-start(bf16[256,512]{1,0:T(8,128)(2,1)} %refs_0_.5), channel_id=1, source_target_pairs={{0,4},{1,5},{2,6},{3,7},{4,0},{5,1},{6,2},{7,3},{8,12},{9,13},{10,... | collective-permute-start | bytes 786440 | tf_op jit(solution)/shard_map/ppermute | solution.py:391
  3.6 12.0 %collective-permute-start.2 = (bf16[256,512]{1,0:T(8,128)(2,1)}, bf16[256,512]{1,0:T(8,128)(2,1)S(1)}, u32[]{:S(2)}, u32[]{:S(2)}) collective-permute-start(bf16[256,512]{1,0:T(8,128)(2,1)} %refs_0_.5), channel_id=1, source_target_pairs={{0,2},{1,7},{2,4},{3,1},{4,6},{5,3},{6,0},{7,5},{8,10},{9,15},{10,... | collective-permute-start | bytes 786440 | tf_op jit(solution)/shard_map/ppermute | solution.py:391
  4.4 12.5 %collective-permute-start.4 = (bf16[256,512]{1,0:T(8,128)(2,1)}, bf16[256,512]{1,0:T(8,128)(2,1)S(1)}, u32[]{:S(2)}, u32[]{:S(2)}) collective-permute-start(bf16[256,512]{1,0:T(8,128)(2,1)} %refs_0_.5), channel_id=1, source_target_pairs={{0,1},{1,0},{2,3},{3,2},{4,5},{5,4},{6,7},{7,6},{8,9},{9,8},{10,11... | collective-permute-start | bytes 786440 | tf_op jit(solution)/shard_map/ppermute | solution.py:388
  5.1 12.4 %collective-permute-start.3 = (bf16[256,512]{1,0:T(8,128)(2,1)}, bf16[256,512]{1,0:T(8,128)(2,1)S(1)}, u32[]{:S(2)}, u32[]{:S(2)}) collective-permute-start(bf16[256,512]{1,0:T(8,128)(2,1)} %refs_0_.5), channel_id=1, source_target_pairs={{0,6},{1,3},{2,0},{3,5},{4,2},{5,7},{6,4},{7,1},{8,14},{9,11},{10,... | collective-permute-start | bytes 786440 | tf_op jit(solution)/shard_map/ppermute | solution.py:391
  10.4 3.8 %copy-start.3 = (bf16[4,512,512]{2,1,0:T(8,128)(2,1)}, bf16[4,512,512]{2,1,0:T(8,128)(2,1)S(1)}, u32[]{:S(2)}) copy-start(bf16[4,512,512]{2,1,0:T(8,128)(2,1)S(1)} %get-tuple-element.69) | copy-start | bytes 6291460
  10.4 6.6 %copy-start = (bf16[256,512]{1,0:T(8,128)(2,1)S(1)}, bf16[256,512]{1,0:T(8,128)(2,1)}, u32[]{:S(2)}) copy-start(bf16[256,512]{1,0:T(8,128)(2,1)} %refs_0_.5) | copy-start | bytes 786436
  15.6 2.8 %collective-permute-start.5 = (bf16[256,512]{1,0:T(8,128)(2,1)S(1)}, bf16[256,512]{1,0:T(8,128)(2,1)S(1)}, u32[]{:S(2)}, u32[]{:S(2)}) collective-permute-start(bf16[256,512]{1,0:T(8,128)(2,1)S(1)} %collective-permute-done.2.refs_0_), channel_id=1, source_target_pairs={{0,1},{1,0},{2,3},{3,2},{4,5},{5,4},{6,7},{7,6},{8,9},{9,8},{10,11... | collective-permute-start | bytes 786440 | tf_op jit(solution)/shard_map/ppermute | solution.py:388
  17.5 1.6 %collective-permute-start.6 = (bf16[256,512]{1,0:T(8,128)(2,1)S(1)}, bf16[256,512]{1,0:T(8,128)(2,1)S(1)}, u32[]{:S(2)}, u32[]{:S(2)}) collective-permute-start(bf16[256,512]{1,0:T(8,128)(2,1)S(1)} %collective-permute-done.3.refs_1_), channel_id=1, source_target_pairs={{0,1},{1,0},{2,3},{3,2},{4,5},{5,4},{6,7},{7,6},{8,9},{9,8},{10,11... | collective-permute-start | bytes 786440 | tf_op jit(solution)/shard_map/ppermute | solution.py:388
  17.8 2.4 %copy-start.1 = (f32[128]{0:T(128)S(1)}, f32[128]{0:T(128)}, u32[]{:S(2)}) copy-start(f32[128]{0:T(128)} %param.12) | copy-start | bytes 1540
  17.8 2.3 %copy-start.2 = (f32[128]{0:T(128)S(1)}, f32[128]{0:T(128)}, u32[]{:S(2)}) copy-start(f32[128]{0:T(128)} %param.13) | copy-start | bytes 1540
  17.8 2.3 %collective-permute-start.1 = (bf16[256,512]{1,0:T(8,128)(2,1)S(1)}, bf16[256,512]{1,0:T(8,128)(2,1)S(1)}, u32[]{:S(2)}, u32[]{:S(2)}) collective-permute-start(bf16[256,512]{1,0:T(8,128)(2,1)S(1)} %collective-permute-done.refs_0_), channel_id=1, source_target_pairs={{0,1},{1,0},{2,3},{3,2},{4,5},{5,4},{6,7},{7,6},{8,9},{9,8},{10,11... | collective-permute-start | bytes 786440 | tf_op jit(solution)/shard_map/ppermute | solution.py:388
  21.2 9.3 %collective-permute-start.7 = (bf16[256,256]{1,0:T(8,128)(2,1)S(1)}, bf16[256,256]{1,0:T(8,128)(2,1)S(1)}, u32[]{:S(2)}, u32[]{:S(2)}) collective-permute-start(bf16[256,256]{1,0:T(8,128)(2,1)S(1)} %get-tuple-element.55.refs_0_.refs_3_), channel_id=1, source_target_pairs={{0,32},{8,40},{16,48},{24,56},{32,64},{40,72},{48,80},{56,88},{64,... | collective-permute-start | bytes 393224 | tf_op jit(solution)/shard_map/ppermute | solution.py:401
  30.5 5.5 %collective-permute-start.8 = (bf16[256,256]{1,0:T(8,128)(2,1)S(1)}, bf16[256,256]{1,0:T(8,128)(2,1)S(1)}, u32[]{:S(2)}, u32[]{:S(2)}) collective-permute-start(bf16[256,256]{1,0:T(8,128)(2,1)S(1)} %collective-permute-done.7.refs_1_.refs_0_.refs_4_), channel_id=1, source_target_pairs={{0,32},{8,40},{16,48},{24,56},{32,64},{40,72},{48,80},{56,88},{64,... | collective-permute-start | bytes 393224 | tf_op jit(solution)/shard_map/ppermute | solution.py:401
  31.3 10.0 %collective-permute-start.11 = (bf16[512,256]{1,0:T(8,128)(2,1)}, bf16[512,256]{1,0:T(8,128)(2,1)S(1)}, u32[]{:S(2)}, u32[]{:S(2)}) collective-permute-start(bf16[512,256]{1,0:T(8,128)(2,1)} %get-tuple-element.56), channel_id=1, source_target_pairs={{0,8},{1,25},{2,10},{3,27},{4,12},{5,29},{6,14},{7,31},{8,0},{9,17... | collective-permute-start | bytes 786440 | tf_op jit(solution)/shard_map/ppermute | solution.py:410
  36.1 5.0 %collective-permute-start.9 = (bf16[256,256]{1,0:T(8,128)(2,1)S(1)}, bf16[256,256]{1,0:T(8,128)(2,1)S(1)}, u32[]{:S(2)}, u32[]{:S(2)}) collective-permute-start(bf16[256,256]{1,0:T(8,128)(2,1)S(1)} %collective-permute-done.8.refs_0_.refs_4_), channel_id=1, source_target_pairs={{0,32},{8,40},{16,48},{24,56},{32,64},{40,72},{48,80},{56,88},{64,... | collective-permute-start | bytes 393224 | tf_op jit(solution)/shard_map/ppermute | solution.py:401
  41.1 5.0 %collective-permute-start.10 = (bf16[256,256]{1,0:T(8,128)(2,1)S(1)}, bf16[256,256]{1,0:T(8,128)(2,1)S(1)}, u32[]{:S(2)}, u32[]{:S(2)}) collective-permute-start(bf16[256,256]{1,0:T(8,128)(2,1)S(1)} %collective-permute-done.9.refs_1_.refs_2_.refs_4_), channel_id=1, source_target_pairs={{0,32},{8,40},{16,48},{24,56},{32,64},{40,72},{48,80},{56,88},{64,... | collective-permute-start | bytes 393224 | tf_op jit(solution)/shard_map/ppermute | solution.py:401
  41.3 19.5 %collective-permute-start.16 = (bf16[512,256]{1,0:T(8,128)(2,1)S(1)}, bf16[512,256]{1,0:T(8,128)(2,1)S(1)}, u32[]{:S(2)}, u32[]{:S(2)}) collective-permute-start(bf16[512,256]{1,0:T(8,128)(2,1)S(1)} %get-tuple-element.60), channel_id=1, source_target_pairs={{0,24},{1,9},{2,26},{3,11},{4,28},{5,13},{6,30},{7,15},{8,16},{9,1... | collective-permute-start | bytes 786440 | tf_op jit(solution)/shard_map/ppermute | solution.py:410
  43.3 8.2 %collective-permute-start.14 = (bf16[512,256]{1,0:T(8,128)(2,1)S(1)}, bf16[512,256]{1,0:T(8,128)(2,1)S(1)}, u32[]{:S(2)}, u32[]{:S(2)}) collective-permute-start(bf16[512,256]{1,0:T(8,128)(2,1)S(1)} %get-tuple-element.58), channel_id=1, source_target_pairs={{0,8},{1,25},{2,10},{3,27},{4,12},{5,29},{6,14},{7,31},{8,0},{9,17... | collective-permute-start | bytes 786440 | tf_op jit(solution)/shard_map/ppermute | solution.py:410
  46.1 8.0 %collective-permute-start.12 = (bf16[256,256]{1,0:T(8,128)(2,1)S(1)}, bf16[256,256]{1,0:T(8,128)(2,1)S(1)}, u32[]{:S(2)}, u32[]{:S(2)}) collective-permute-start(bf16[256,256]{1,0:T(8,128)(2,1)S(1)} %collective-permute-done.10.refs_1_.refs_0_.refs_4_), channel_id=1, source_target_pairs={{0,8},{1,25},{2,10},{3,27},{4,12},{5,29},{6,14},{7,31},{8,0},{9,17... | collective-permute-start | bytes 393224 | tf_op jit(solution)/shard_map/ppermute | solution.py:410
  51.5 2.7 %copy-start.4 = (bf16[4,512,512]{2,1,0:T(8,128)(2,1)S(1)}, bf16[4,512,512]{2,1,0:T(8,128)(2,1)}, u32[]{:S(2)}) copy-start(bf16[4,512,512]{2,1,0:T(8,128)(2,1)} %copy-done.3) | copy-start | bytes 6291460
  51.5 10.4 %collective-permute-start.15 = (bf16[1024,256]{1,0:T(8,128)(2,1)S(1)}, bf16[1024,256]{1,0:T(8,128)(2,1)S(1)}, u32[]{:S(2)}, u32[]{:S(2)}) collective-permute-start(bf16[1024,256]{1,0:T(8,128)(2,1)S(1)} %get-tuple-element.59), channel_id=1, source_target_pairs={{0,24},{1,9},{2,26},{3,11},{4,28},{5,13},{6,30},{7,15},{8,16},{9,1... | collective-permute-start | bytes 1572872 | tf_op jit(solution)/shard_map/ppermute | solution.py:410
  54.2 7.8 %collective-permute-start.17 = (bf16[4,512,512]{2,1,0:T(8,128)(2,1)S(1)}, bf16[4,512,512]{2,1,0:T(8,128)(2,1)S(1)}, u32[]{:S(2)}, u32[]{:S(2)}) collective-permute-start(bf16[4,512,512]{2,1,0:T(8,128)(2,1)S(1)} %copy-done.4), channel_id=1, source_target_pairs={{0,1},{1,0},{2,3},{3,2},{4,5},{5,4},{6,7},{7,6},{8,9},{9,8},{10,11... | collective-permute-start | bytes 6291464 | tf_op jit(solution)/shard_map/ppermute | solution.py:388
  59.3 5.5 %collective-permute-start.13 = (bf16[512,256]{1,0:T(8,128)(2,1)S(1)}, bf16[512,256]{1,0:T(8,128)(2,1)S(1)}, u32[]{:S(2)}, u32[]{:S(2)}) collective-permute-start(bf16[512,256]{1,0:T(8,128)(2,1)S(1)} %get-tuple-element.57), channel_id=1, source_target_pairs={{0,24},{1,9},{2,26},{3,11},{4,28},{5,13},{6,30},{7,15},{8,16},{9,1... | collective-permute-start | bytes 786440 | tf_op jit(solution)/shard_map/ppermute | solution.py:410
  66.0 3.9 %collective-permute-start.18 = (bf16[256,512]{1,0:T(8,128)(2,1)S(1)}, bf16[256,512]{1,0:T(8,128)(2,1)S(1)}, u32[]{:S(2)}, u32[]{:S(2)}) collective-permute-start(bf16[256,512]{1,0:T(8,128)(2,1)S(1)} %get-tuple-element.72.a_ref), channel_id=1, source_target_pairs={{0,1},{1,0},{2,3},{3,2},{4,5},{5,4},{6,7},{7,6},{8,9},{9,8},{10,11... | collective-permute-start | bytes 786440 | tf_op jit(solution)/shard_map/ppermute | solution.py:388
  70.4 9.1 %collective-permute-start.20 = (bf16[256,512]{1,0:T(8,128)(2,1)S(1)}, bf16[256,512]{1,0:T(8,128)(2,1)S(1)}, u32[]{:S(2)}, u32[]{:S(2)}) collective-permute-start(bf16[256,512]{1,0:T(8,128)(2,1)S(1)} %out_project.5), channel_id=1, source_target_pairs={{0,4},{1,5},{2,6},{3,7},{4,0},{5,1},{6,2},{7,3},{8,12},{9,13},{10,... | collective-permute-start | bytes 786440 | tf_op jit(solution)/shard_map/ppermute | solution.py:391
  73.8 10.9 %collective-permute-start.19 = (bf16[256,512]{1,0:T(8,128)(2,1)S(1)}, bf16[256,512]{1,0:T(8,128)(2,1)S(1)}, u32[]{:S(2)}, u32[]{:S(2)}) collective-permute-start(bf16[256,512]{1,0:T(8,128)(2,1)S(1)} %get-tuple-element.75), channel_id=1, source_target_pairs={{0,2},{1,7},{2,4},{3,1},{4,6},{5,3},{6,0},{7,5},{8,10},{9,15},{10,... | collective-permute-start | bytes 786440 | tf_op jit(solution)/shard_map/ppermute | solution.py:391
  74.9 11.0 %collective-permute-start.21 = (bf16[256,512]{1,0:T(8,128)(2,1)S(1)}, bf16[256,512]{1,0:T(8,128)(2,1)S(1)}, u32[]{:S(2)}, u32[]{:S(2)}) collective-permute-start(bf16[256,512]{1,0:T(8,128)(2,1)S(1)} %get-tuple-element.76), channel_id=1, source_target_pairs={{0,6},{1,3},{2,0},{3,5},{4,2},{5,7},{6,4},{7,1},{8,14},{9,11},{10,... | collective-permute-start | bytes 786440 | tf_op jit(solution)/shard_map/ppermute | solution.py:391

commit v3 on v2

--- a/solution.py
+++ b/solution.py
@@ -59,9 +59,11 @@
 
     def base(self, block, tok):
         back, who = block
-        y = (self.y, self.y1, self.y2, self.y3)[who]
         if back is None:
-            back = jnp.where(self.y > y, 0, 4)
+            wraps = self.y < who
+            back, y = jnp.where(wraps, 4, 0), self.y - who + jnp.where(wraps, NY, 0)
+        else:
+            y = (self.y, self.y1, self.y2, self.y3)[who]
         return ((self.z - back) * NY + y) * tok
 
 
@@ -86,24 +88,25 @@
 FLAG = (8, 128)
 
 
-def fetch_kernel(src, out, flag, sem):
+def fetch_kernel(src, *refs):
+    out, flag, sem = refs[-3:]
     copy = pltpu.make_async_copy(src, out, sem)
     copy.start()
     flag[...] = jnp.zeros_like(flag)
     copy.wait()
 
 
-def fetch(a):
+def fetch(a, flags=()):
     vm = pl.BlockSpec(memory_space=VMEM)
     return pl.pallas_call(
         fetch_kernel,
-        in_specs=[pl.BlockSpec(memory_space=pl.ANY)],
+        in_specs=[pl.BlockSpec(memory_space=pl.ANY)] * (1 + len(flags)),
         out_specs=[vm, vm],
         out_shape=[VMEM(a.shape, a.dtype), jax.ShapeDtypeStruct(FLAG, F32)],
         scratch_shapes=[pltpu.SemaphoreType.DMA],
         compiler_params=params(),
         name="fetch",
-    )(a)
+    )(a, *flags)
 
 
 def stage(arrays, plan, shapes, name):
@@ -131,14 +134,14 @@
     refs[-1][...] = jnp.zeros(FLAG, F32)
 
 
-def hold(*arrays):
+def hold(*arrays, cost=20):
     return pl.pallas_call(
         hold_kernel,
         in_specs=[pl.BlockSpec(memory_space=pl.ANY)] * len(arrays),
         out_specs=pl.BlockSpec(memory_space=VMEM),
         out_shape=jax.ShapeDtypeStruct(FLAG, F32),
         compiler_params=params(),
-        cost_estimate=pl.CostEstimate(flops=2 * 10**10, bytes_accessed=4096, transcendentals=0),
+        cost_estimate=pl.CostEstimate(flops=cost * 10**9, bytes_accessed=4096, transcendentals=0),
         name="hold",
     )(*arrays)
 
@@ -146,22 +149,10 @@
 def pack_kernel(pieces, tok, count, *refs):
     ins, out, flag = refs[:count], refs[-2], refs[-1]
     flag[...] = jnp.zeros_like(flag)
-    place = Place()
-    here = (place.y, place.y1)
     for n, piece in enumerate(pieces):
         to = slice(n * tok, (n + 1) * tok)
-        if len(piece) == 2:
-            src, at = piece
-            out[to, :] = ins[src][at * tok : (at + 1) * tok, :]
-        else:
-            who, one, two = piece
-            later = place.y2 > here[who]
-
-            def put(src, at, to=to):
-                out[to, :] = ins[src][at * tok : (at + 1) * tok, :]
-
-            pl.when(later)(functools.partial(put, *one))
-            pl.when(jnp.logical_not(later))(functools.partial(put, *two))
+        src, at = piece
+        out[to, :] = ins[src][at * tok : (at + 1) * tok, :]
 
 
 def pack(arrays, pieces, tok, flags=()):
@@ -178,6 +169,32 @@
         compiler_params=params(),
         name="pack",
     )(*arrays, *flags)
+
+
+def mix_kernel(own, far, *refs):
+    outs, flag = refs[-NY:-1], refs[-1]
+    flag[...] = jnp.zeros_like(flag)
+    place = Place()
+    for e, out in enumerate(outs, 1):
+        here = place.y + e < NY
+
+        def put(src, out=out):
+            out[...] = src[...]
+
+        pl.when(here)(functools.partial(put, own))
+        pl.when(jnp.logical_not(here))(functools.partial(put, far))
+
+
+def mixes(own, far, flags=()):
+    vm = pl.BlockSpec(memory_space=VMEM)
+    return pl.pallas_call(
+        mix_kernel,
+        in_specs=[vm] * 2 + [pl.BlockSpec(memory_space=pl.ANY)] * len(flags),
+        out_specs=[vm] * NY,
+        out_shape=[VMEM(own.shape, BF)] * (NY - 1) + [jax.ShapeDtypeStruct(FLAG, F32)],
+        compiler_params=params(),
+        name="mixes",
+    )(own, far, *flags)
 
 
 def project_kernel(count, at, head, first, last, flags, *refs):
@@ -397,6 +414,9 @@
     def along_y(a, d):
         return lax.ppermute(a, "seq", [(i, i // ny * ny + (i + d) % ny) for i in range(seqs)])
 
+    def along_y(a, d):
+        return lax.ppermute(a, "seq", [(i, i // ny * ny + (i + d) % ny) for i in range(seqs)])
+
     def along_z(a, d):
         return lax.ppermute(a, "seq", [(i, (i // ny + d) % nz * ny + i % ny) for i in range(seqs)])
 
@@ -450,38 +470,36 @@
     r2 = along_z(r1, 1)
     r3 = along_z(r2, 1)
     r4 = along_z(r3, 1)
-    x01, flag_01 = pack([r0, r1], [(0, 0), (1, 0)], tok)
-    s01 = swap_y(x01, 0)
-    o, flag_a = attend(*attn, [(r0, [(0, 0)]), (r1, [(1, 0)])], flags=[flag_01])
-    x_one, flag_1 = pack([r1, s01], [(0, 0), (1, 1)], tok)
+    s1, s2, s3 = swap_y(r1, 0), swap_y(r2, 0), swap_y(r3, 0)
+    w_sib = sibling(w_send)
+    got = hold(w_sib, cost=0)
+    o, flag_a = attend(*attn, [(r0, [(0, 0)])])
+    x_one, flag_1 = pack([r1, s1], [(0, 0), (1, 0)], tok)
     near_one = swap_y(x_one, 1)
-    o, flag_b = attend(*attn, [(s01, [(0, 1), (1, 1)]), (r2, [(2, 0)])], o, flags=[flag_1])
-    x23, flag_23 = pack([r2, r3], [(0, 0), (1, 0)], tok)
-    s23 = swap_y(x23, 0)
-    s4 = swap_y(r4, 0)
-    x_two, flag_2 = pack(
-        [r2, s23, r3], [(0, 0), (1, 0), (2, 0), (1, 1)], tok, flags=[hold(r4)]
-    )
+    o, flag_b = attend(*attn, [(r1, [(1, 0)]), (r2, [(2, 0)])], o, flags=[flag_1])
+    x_two, flag_2 = pack([r2, s2], [(0, 0), (1, 0)], tok, flags=[hold(r3), got, flag_b])
     near_two = swap_y(x_two, 1)
+    x1, x2, x3, flag_m = mixes(r0, r4, flags=[hold(r4), flag_2])
+    mixed = [(along_y((x1, x2, x3)[e - 1], e), [(None, e)]) for e in (2, 1, 3)]
+    x_three, flag_3 = pack([r3, s3], [(0, 0), (1, 0)], tok, flags=[flag_m])
+    near_three = swap_y(x_three, 1)
     o, flag_c = attend(
         *attn,
-        [(near_one, [(1, 2), (1, 3)]), (r3, [(3, 0)]), (s23, [(2, 1), (3, 1)])],
+        [(s1, [(1, 1)]), (s2, [(2, 1)]), (near_one, [(1, 2), (1, 3)]), (r3, [(3, 0)])],
         o,
-        flags=[flag_2],
-    )
-    x_last, flag_l = pack(
-        [r0, r4, s01, s4], [(0, (0, 0), (1, 0)), (1, (2, 0), (3, 0))], tok, flags=[hold(s4)]
-    )
-    last = swap_y(x_last, 1)
-    w_send, _ = after([flag_l], w_send)
-    w_sib, flag_w = fetch(sibling(w_send))
-    o, _ = attend(
+        flags=[flag_3],
+    )
+    w_sib, flag_w = fetch(w_sib, [flag_3])
+    o, flag_d = attend(
+        *attn, [(near_two, [(2, 2), (2, 3)]), (s3, [(3, 1)]), (r4, [(4, 0)])], o
+    )
+    attended, _ = attend(
         *attn,
-        [(near_two, [(2, 2), (2, 3), (3, 2), (3, 3)]), (r4, [(4, 0)]), (s4, [(4, 1)])],
+        [(near_three, [(3, 2), (3, 3)]), *mixed],
         o,
-        flags=[flag_l, flag_w, hold(near_two)],
-    )
-    attended, _ = attend(*attn, [(last, [(None, 2), (None, 3)])], o, final=True)
+        final=True,
+        flags=[flag_w, hold(*[m for m, _ in mixed], flag_d, cost=2)],
+    )
 
     attended_sib = sibling(attended)
     (p2,) = out_project((0,), (BF,), attended, attended_sib, w_own, w_sib)

time: 87.9 us -> 83.8 us (0.953); the launches traced: 86.7 us -> 83.7 us
  waiting for transfers between devices: 35.2 us -> 29.6 us
  starting transfers between devices: 29.7 us -> 32.3 us
    ppermute x0 -> x3, starting transfers between devices: none -> 4.59 us  [along_y(): lax.ppermute(a, 'seq', [(i, i // ny * ny + (i + d) % ny) for i in range(s...]
    ppermute x4, waiting for transfers between devices: 15.7 us -> 11.6 us  [along_z(): lax.ppermute(a, 'seq', [(i, (i // ny + d) % nz * ny + i % ny) for i in ra...]
    ppermute x6, waiting for transfers between devices: 6.56 us -> 2.62 us  [swap_y(): return lax.ppermute(a, ('seq', 'tp'), pairs)]
    ppermute x0 -> x3, waiting for transfers between devices: none -> 3.08 us  [along_y(): lax.ppermute(a, 'seq', [(i, i // ny * ny + (i + d) % ny) for i in range(s...]
    ppermute x6, starting transfers between devices: 10.3 us -> 8.13 us  [swap_y(): return lax.ppermute(a, ('seq', 'tp'), pairs)]
    pallas_call x1, Pallas kernels: 0.15 us -> 1.6 us  [fetch(): pl.pallas_call(fetch_kernel, in_specs=[pl.BlockSpec(memory_space=pl.ANY)]...]
    pallas_call x5 -> x3, Pallas kernels: 1.41 us -> 0.06 us  [pack(): pl.pallas_call(functools.partial(pack_kernel, tuple(pieces), tok, count),...]
    pallas_call x5, Pallas kernels: 6.57 us -> 5.67 us  [attend(): pl.pallas_call(functools.partial(attend_kernel, layout, first, final, len...]
  transfers between devices with their start and end apart: 22 -> 25, of which waited for: 13 -> 12; matrix products, arithmetic and copies ran while one was open for 3% -> 3% of each run, Pallas kernels for 18% -> 18%
where the time goes in v3:
time: 83.8 us; the launch traced here: 83.7 us
  starting transfers between devices  32.3 us (39%)
  waiting for transfers between devices  29.6 us (35%)
  Pallas kernels  18.9 us (23%)
  other arithmetic  1.6 us (2%)
  local copies, waits for them, and re-layouts  0.88 us (1%)
    ppermute x4, waiting for transfers between devices, along_z(): lax.ppermute(a, 'seq', [(i, (i // ny + d) % nz * ny + i % ny) for i in ra...  11.6 us
    ppermute x6, waiting for transfers between devices, along_x(): lax.ppermute(a, 'tp', [(i, (i // 2 + (d if i % 2 == 0 else -d)) % nx * 2...  10.4 us
    ppermute x6, starting transfers between devices, along_x(): lax.ppermute(a, 'tp', [(i, (i // 2 + (d if i % 2 == 0 else -d)) % nx * 2...  10 us
    ppermute x6, starting transfers between devices, swap_y(): return lax.ppermute(a, ('seq', 'tp'), pairs)  8.13 us
    ppermute x6, starting transfers between devices, sibling(): return lax.ppermute(a, 'tp', [(i, i ^ 1) for i in range(tps)])  7.83 us
    pallas_call x2, Pallas kernels, stage(): pl.pallas_call(functools.partial(stage_kernel, plan, len(arrays)), in_spe...  6.62 us
    pallas_call x5, Pallas kernels, attend(): pl.pallas_call(functools.partial(attend_kernel, layout, first, final, len...  5.67 us
    ppermute x3, starting transfers between devices, along_y(): lax.ppermute(a, 'seq', [(i, i // ny * ny + (i + d) % ny) for i in range(s...  4.59 us
  transfers between devices with their start and end apart: 25, of which 12 were waited for; matrix products, arithmetic and copies ran while one was open for 3% of the time, Pallas kernels for 18%

profile of v3, /device:TPU:1, one launch (start us, length us, event | category | flops | bytes accessed | tf_op | source)
XLA Modules:
  0.0 83.7 jit_solution(14661779567394663155)
XLA Ops:
  0.0 3.6 %collective-permute-start = (bf16[256,512]{1,0:T(8,128)(2,1)}, bf16[256,512]{1,0:T(8,128)(2,1)S(1)}, u32[]{:S(2)}, u32[]{:S(2)}) collective-permute-start(bf16[256,512]{1,0:T(8,128)(2,1)} %refs_0_.5), channel_id=1, source_target_pairs={{0,4},{1,5},{2,6},{3,7},{4,0},{5,1},{6,2},{7,3},{8,12},{9,13},{10,... | collective-permute-start | bytes 786440 | tf_op jit(solution)/shard_map/ppermute | solution.py:408
  3.6 0.9 %collective-permute-start.2 = (bf16[256,512]{1,0:T(8,128)(2,1)}, bf16[256,512]{1,0:T(8,128)(2,1)S(1)}, u32[]{:S(2)}, u32[]{:S(2)}) collective-permute-start(bf16[256,512]{1,0:T(8,128)(2,1)} %refs_0_.5), channel_id=1, source_target_pairs={{0,2},{1,7},{2,4},{3,1},{4,6},{5,3},{6,0},{7,5},{8,10},{9,15},{10,... | collective-permute-start | bytes 786440 | tf_op jit(solution)/shard_map/ppermute | solution.py:408
  4.4 0.7 collective-permute-start.4
  5.1 1.3 %collective-permute-start.3 = (bf16[256,512]{1,0:T(8,128)(2,1)}, bf16[256,512]{1,0:T(8,128)(2,1)S(1)}, u32[]{:S(2)}, u32[]{:S(2)}) collective-permute-start(bf16[256,512]{1,0:T(8,128)(2,1)} %refs_0_.5), channel_id=1, source_target_pairs={{0,6},{1,3},{2,0},{3,5},{4,2},{5,7},{6,4},{7,1},{8,14},{9,11},{10,... | collective-permute-start | bytes 786440 | tf_op jit(solution)/shard_map/ppermute | solution.py:408
  6.5 0.7 copy.16
  7.2 0.1 reduce
  7.3 0.7 select_reduce_fusion.start_s
  8.1 3.6 %stage_out.1 = (bf16[4,512,512]{2,1,0:T(8,128)(2,1)S(1)}, bf16[4,512,512]{2,1,0:T(8,128)(2,1)}, f32[8,128]{1,0:T(8,128)S(1)}) custom-call(bf16[512,4096]{1,0:T(8,128)(2,1)} %refs_0_.4), custom_call_target="tpu_custom_call" | custom-call | bytes 8388608 | tf_op jit(solution)/shard_map/stage_out/pallas_call | solution.py:114
  11.7 0.0 copy-start
  11.7 3.0 %stage_in.1 = (bf16[8,512,768]{2,1,0:T(8,128)(2,1)S(1)}, f32[8,128]{1,0:T(8,128)S(1)}) custom-call(bf16[4096,512]{1,0:T(8,128)(2,1)} %refs_0_.3, bf16[4096,128]{1,0:T(8,128)(2,1)} %refs_1_.1, bf16[4096,128]{1,0:T(8,128)(2,1)} %refs_2_.1), custom_call_target="tpu_custom_call" | custom-call | bytes 12582912 | tf_op jit(solution)/shard_map/stage_in/pallas_call | solution.py:114
  14.8 0.5 fusion
  15.3 0.3 collective-permute-done.2.refs_0_
  15.6 1.4 %collective-permute-start.5 = (bf16[256,512]{1,0:T(8,128)(2,1)S(1)}, bf16[256,512]{1,0:T(8,128)(2,1)S(1)}, u32[]{:S(2)}, u32[]{:S(2)}) collective-permute-start(bf16[256,512]{1,0:T(8,128)(2,1)S(1)} %collective-permute-done.2.refs_0_), channel_id=1, source_target_pairs={{0,1},{1,0},{2,3},{3,2},{4,5},{5,4},{6,7},{7,6},{8,9},{9,8},{10,11... | collective-permute-start | bytes 786440 | tf_op jit(solution)/shard_map/ppermute | solution.py:405
  16.9 0.6 project.3.refs_5_
  17.5 0.1 collective-permute-start.6
  17.6 0.1 pad_maximum_fusion
  17.8 0.0 collective-permute-done.refs_0_
  17.8 0.0 copy-start.1
  17.8 0.0 copy-start.2
  17.8 0.6 collective-permute-start.1
  18.4 0.7 collective-permute-done.6.refs_3_
  19.1 1.0 %project.4.refs_3_ = f32[256,768]{1,0:T(8,128)S(1)} custom-call(bf16[256,512]{1,0:T(8,128)(2,1)S(1)} %collective-permute-done.2.refs_0_, bf16[256,512]{1,0:T(8,128)(2,1)S(1)} %collective-permute-done.3.refs_1_, bf16[256,512]{1,0:T(8,128)(2,1)S(1)} %collective-permute-done.5.refs_2_, bf16[256,512]{1,0:T(8,128)(2,1)S(1)} %collective-permute-done.6.refs_3_, ...), custom_call_target="tpu_custom_call" | custom-call | flops 1610612736 | bytes 3145728 | tf_op jit(solution)/shard_map/project/pallas_call | solution.py:250
  20.2 1.0 %project.5 = (bf16[1024,128]{1,0:T(8,128)(2,1)S(1)}, bf16[256,256]{1,0:T(8,128)(2,1)S(1)}) custom-call(bf16[256,512]{1,0:T(8,128)(2,1)S(1)} %collective-permute-done.refs_0_, bf16[256,512]{1,0:T(8,128)(2,1)S(1)} %collective-permute-done.1.refs_1_, bf16[8,512,768]{2,1,0:T(8,128)(2,1)S(1)} %get-tuple-element.44.refs_2_.refs_4_, ...), custom_call_target="tpu_custom_call" | custom-call | flops 805306368 | bytes 1572864 | tf_op jit(solution)/shard_map/project/pallas_call | solution.py:250
  21.2 1.7 %collective-permute-start.7 = (bf16[256,256]{1,0:T(8,128)(2,1)S(1)}, bf16[256,256]{1,0:T(8,128)(2,1)S(1)}, u32[]{:S(2)}, u32[]{:S(2)}) collective-permute-start(bf16[256,256]{1,0:T(8,128)(2,1)S(1)} %get-tuple-element.57.refs_3_.own), channel_id=1, source_target_pairs={{0,32},{8,40},{16,48},{24,56},{32,64},{40,72},{48,80},{56,88},{64,... | collective-permute-start | bytes 393224 | tf_op jit(solution)/shard_map/ppermute | solution.py:421
  22.9 7.7 %collective-permute-done.7.refs_0_.refs_3_ = bf16[256,256]{1,0:T(8,128)(2,1)S(1)} collective-permute-done((bf16[256,256]{1,0:T(8,128)(2,1)S(1)}, bf16[256,256]{1,0:T(8,128)(2,1)S(1)}, u32[]{:S(2)}, u32[]{:S(2)}) %collective-permute-start.7) | collective-permute-done | bytes 131104 | tf_op jit(solution)/shard_map/ppermute | solution.py:421
  30.5 0.0 collective-permute-start.8
  30.5 0.7 collective-permute-start.13
  31.2 2.7 %collective-permute-start.14 = (bf16[256,256]{1,0:T(8,128)(2,1)S(1)}, bf16[256,256]{1,0:T(8,128)(2,1)S(1)}, u32[]{:S(2)}, u32[]{:S(2)}) collective-permute-start(bf16[256,256]{1,0:T(8,128)(2,1)S(1)} %collective-permute-done.7.refs_0_.refs_3_), channel_id=1, source_target_pairs={{0,8},{1,25},{2,10},{3,27},{4,12},{5,29},{6,14},{7,31},{8,0},{9,17... | collective-permute-start | bytes 393224 | tf_op jit(solution)/shard_map/ppermute | solution.py:430
  34.0 2.1 %collective-permute-done.8.refs_4_.refs_0_ = bf16[256,256]{1,0:T(8,128)(2,1)S(1)} collective-permute-done((bf16[256,256]{1,0:T(8,128)(2,1)S(1)}, bf16[256,256]{1,0:T(8,128)(2,1)S(1)}, u32[]{:S(2)}, u32[]{:S(2)}) %collective-permute-start.8) | collective-permute-done | bytes 131104 | tf_op jit(solution)/shard_map/ppermute | solution.py:421
  36.1 0.0 collective-permute-start.9
  36.1 0.1 copy.21.refs_1_
  36.2 1.6 %attend.5 = (f32[1024,256]{1,0:T(8,128)S(1)}, f32[8,128]{1,0:T(8,128)}) custom-call(s32[256]{0:T(256)S(1)} %select_reduce_fusion.start_s, bf16[1024,128]{1,0:T(8,128)(2,1)S(1)} %get-tuple-element.54.refs_0_, s32[256,1]{1,0:T(8,128)S(1)} %copy.21.refs_1_, s32[256,1]{1,0:T(8,128)S(1)} %iota_add_fusion.refs_2_, bf16[256,256]{1,0:T(8,128)(2,1)S(1)} %get-tuple-element.57.refs_3_.own), custom_call_target="tpu_custom_call" | custom-call | flops 268435456 | bytes 2097152 | tf_op jit(solution)/shard_map/attend/pallas_call | solution.py:333
  37.8 1.4 %collective-permute-start.20 = (bf16[512,256]{1,0:T(8,128)(2,1)S(1)}, bf16[512,256]{1,0:T(8,128)(2,1)S(1)}, u32[]{:S(2)}, u32[]{:S(2)}) collective-permute-start(bf16[512,256]{1,0:T(8,128)(2,1)S(1)} %get-tuple-element.69), channel_id=1, source_target_pairs={{0,24},{1,9},{2,26},{3,11},{4,28},{5,13},{6,30},{7,15},{8,16},{9,1... | collective-permute-start | bytes 786440 | tf_op jit(solution)/shard_map/ppermute | solution.py:430
  39.2 1.9 %collective-permute-start.12 = (bf16[256,256]{1,0:T(8,128)(2,1)S(1)}, bf16[256,256]{1,0:T(8,128)(2,1)S(1)}, u32[]{:S(2)}, u32[]{:S(2)}) collective-permute-start(bf16[256,256]{1,0:T(8,128)(2,1)S(1)} %collective-permute-done.8.refs_4_.refs_0_), channel_id=1, source_target_pairs={{0,8},{1,25},{2,10},{3,27},{4,12},{5,29},{6,14},{7,31},{8,0},{9,17... | collective-permute-start | bytes 393224 | tf_op jit(solution)/shard_map/ppermute | solution.py:430
  41.1 0.7 attend.6
  41.8 0.0 collective-permute-done.9.refs_0_.refs_6_
  41.8 0.1 collective-permute-start.11
  41.9 1.9 %collective-permute-start.10 = (bf16[256,256]{1,0:T(8,128)(2,1)S(1)}, bf16[256,256]{1,0:T(8,128)(2,1)S(1)}, u32[]{:S(2)}, u32[]{:S(2)}) collective-permute-start(bf16[256,256]{1,0:T(8,128)(2,1)S(1)} %collective-permute-done.9.refs_0_.refs_6_), channel_id=1, source_target_pairs={{0,8},{1,25},{2,10},{3,27},{4,12},{5,29},{6,14},{7,31},{8,0},{9,17... | collective-permute-start | bytes 393224 | tf_op jit(solution)/shard_map/ppermute | solution.py:430
  43.8 0.0 collective-permute-done.13.refs_0_.src
  43.8 1.4 %collective-permute-done.12.refs_1_.refs_4_ = bf16[256,256]{1,0:T(8,128)(2,1)S(1)} collective-permute-done((bf16[256,256]{1,0:T(8,128)(2,1)S(1)}, bf16[256,256]{1,0:T(8,128)(2,1)S(1)}, u32[]{:S(2)}, u32[]{:S(2)}) %collective-permute-start.12) | collective-permute-done | bytes 131104 | tf_op jit(solution)/shard_map/ppermute | solution.py:430
  45.2 0.1 collective-permute-start.19
  45.3 1.9 %collective-permute-done.11.refs_0_.far.refs_5_ = bf16[256,256]{1,0:T(8,128)(2,1)S(1)} collective-permute-done((bf16[256,256]{1,0:T(8,128)(2,1)S(1)}, bf16[256,256]{1,0:T(8,128)(2,1)S(1)}, u32[]{:S(2)}, u32[]{:S(2)}) %collective-permute-start.11) | collective-permute-done | bytes 131104 | tf_op jit(solution)/shard_map/ppermute | solution.py:421
  47.3 1.9 %collective-permute-start.16 = (bf16[256,256]{1,0:T(8,128)(2,1)S(1)}, bf16[256,256]{1,0:T(8,128)(2,1)S(1)}, u32[]{:S(2)}, u32[]{:S(2)}) collective-permute-start(bf16[256,256]{1,0:T(8,128)(2,1)S(1)} %get-tuple-element.65), channel_id=1, source_target_pairs={{0,16},{8,24},{16,0},{24,8},{32,48},{40,56},{48,32},{56,40},{64,80... | collective-permute-start | bytes 393224 | tf_op jit(solution)/shard_map/ppermute | solution.py:418
  49.2 0.7 collective-permute-start.17
  49.9 2.0 %collective-permute-start.18 = (bf16[256,256]{1,0:T(8,128)(2,1)S(1)}, bf16[256,256]{1,0:T(8,128)(2,1)S(1)}, u32[]{:S(2)}, u32[]{:S(2)}) collective-permute-start(bf16[256,256]{1,0:T(8,128)(2,1)S(1)} %get-tuple-element.67), channel_id=1, source_target_pairs={{0,24},{8,0},{16,8},{24,16},{32,56},{40,32},{48,40},{56,48},{64,88... | collective-permute-start | bytes 393224 | tf_op jit(solution)/shard_map/ppermute | solution.py:418
  51.9 0.1 collective-permute-start.15
  52.0 1.2 %attend.7 = (f32[1024,256]{1,0:T(8,128)S(1)}, f32[8,128]{1,0:T(8,128)}) custom-call(s32[256]{0:T(256)S(1)} %select_reduce_fusion.start_s, bf16[1024,128]{1,0:T(8,128)(2,1)S(1)} %get-tuple-element.54.refs_0_, s32[256,1]{1,0:T(8,128)S(1)} %copy.21.refs_1_, s32[256,1]{1,0:T(8,128)S(1)} %iota_add_fusion.refs_2_, ...), custom_call_target="tpu_custom_call" | custom-call | flops 1342177280 | bytes 2097152 | tf_op jit(solution)/shard_map/attend/pallas_call | solution.py:333
  53.2 1.6 %fetch.1 = (bf16[4,512,512]{2,1,0:T(8,128)(2,1)S(1)}, f32[8,128]{1,0:T(8,128)S(1)}) custom-call(bf16[4,512,512]{2,1,0:T(8,128)(2,1)} %collective-permute-done.13.refs_0_.src, f32[8,128]{1,0:T(8,128)S(1)} %get-tuple-element.71.refs_8_.refs_0_), custom_call_target="tpu_custom_call" | custom-call | tf_op jit(solution)/shard_map/fetch/pallas_call | solution.py:101
  54.8 0.7 attend.8
  55.6 3.1 %collective-permute-done.17.refs_1_.refs_5_ = bf16[256,256]{1,0:T(8,128)(2,1)S(1)} collective-permute-done((bf16[256,256]{1,0:T(8,128)(2,1)S(1)}, bf16[256,256]{1,0:T(8,128)(2,1)S(1)}, u32[]{:S(2)}, u32[]{:S(2)}) %collective-permute-start.17) | collective-permute-done | bytes 131104 | tf_op jit(solution)/shard_map/ppermute | solution.py:418
  58.7 1.2 %collective-permute-done.15.refs_3_ = bf16[512,256]{1,0:T(8,128)(2,1)S(1)} collective-permute-done((bf16[512,256]{1,0:T(8,128)(2,1)S(1)}, bf16[512,256]{1,0:T(8,128)(2,1)S(1)}, u32[]{:S(2)}, u32[]{:S(2)}) %collective-permute-start.15) | collective-permute-done | bytes 262176 | tf_op jit(solution)/shard_map/ppermute | solution.py:430
  59.9 1.5 %attend.9 = (bf16[256,512]{1,0:T(8,128)(2,1)S(1)}, f32[8,128]{1,0:T(8,128)}) custom-call(s32[256]{0:T(256)S(1)} %select_reduce_fusion.start_s, bf16[1024,128]{1,0:T(8,128)(2,1)S(1)} %get-tuple-element.54.refs_0_, s32[256,1]{1,0:T(8,128)S(1)} %copy.21.refs_1_, s32[256,1]{1,0:T(8,128)S(1)} %iota_add_fusion.refs_2_, ...), custom_call_target="tpu_custom_call" | custom-call | flops 1342177280 | bytes 2097152 | tf_op jit(solution)/shard_map/attend/pallas_call | solution.py:333
  61.4 4.4 %collective-permute-start.21 = (bf16[256,512]{1,0:T(8,128)(2,1)S(1)}, bf16[256,512]{1,0:T(8,128)(2,1)S(1)}, u32[]{:S(2)}, u32[]{:S(2)}) collective-permute-start(bf16[256,512]{1,0:T(8,128)(2,1)S(1)} %get-tuple-element.76.a_ref), channel_id=1, source_target_pairs={{0,1},{1,0},{2,3},{3,2},{4,5},{5,4},{6,7},{7,6},{8,9},{9,8},{10,11... | collective-permute-start | bytes 786440 | tf_op jit(solution)/shard_map/ppermute | solution.py:405
  65.7 1.2 %collective-permute-done.21.b_ref = bf16[256,512]{1,0:T(8,128)(2,1)S(1)} collective-permute-done((bf16[256,512]{1,0:T(8,128)(2,1)S(1)}, bf16[256,512]{1,0:T(8,128)(2,1)S(1)}, u32[]{:S(2)}, u32[]{:S(2)}) %collective-permute-start.21) | collective-permute-done | bytes 262176 | tf_op jit(solution)/shard_map/ppermute | solution.py:405
  66.9 0.4 out_project.5
  67.3 2.7 %collective-permute-start.23 = (bf16[256,512]{1,0:T(8,128)(2,1)S(1)}, bf16[256,512]{1,0:T(8,128)(2,1)S(1)}, u32[]{:S(2)}, u32[]{:S(2)}) collective-permute-start(bf16[256,512]{1,0:T(8,128)(2,1)S(1)} %out_project.5), channel_id=1, source_target_pairs={{0,4},{1,5},{2,6},{3,7},{4,0},{5,1},{6,2},{7,3},{8,12},{9,13},{10,... | collective-permute-start | bytes 786440 | tf_op jit(solution)/shard_map/ppermute | solution.py:408
  70.1 0.7 out_project.4
  70.8 1.1 %collective-permute-start.22 = (bf16[256,512]{1,0:T(8,128)(2,1)S(1)}, bf16[256,512]{1,0:T(8,128)(2,1)S(1)}, u32[]{:S(2)}, u32[]{:S(2)}) collective-permute-start(bf16[256,512]{1,0:T(8,128)(2,1)S(1)} %get-tuple-element.79), channel_id=1, source_target_pairs={{0,2},{1,7},{2,4},{3,1},{4,6},{5,3},{6,0},{7,5},{8,10},{9,15},{10,... | collective-permute-start | bytes 786440 | tf_op jit(solution)/shard_map/ppermute | solution.py:408
  71.9 0.4 collective-permute-start.24
  72.3 0.4 out_project.3.mine
  72.8 3.7 %collective-permute-done.23.b = bf16[256,512]{1,0:T(8,128)(2,1)S(1)} collective-permute-done((bf16[256,512]{1,0:T(8,128)(2,1)S(1)}, bf16[256,512]{1,0:T(8,128)(2,1)S(1)}, u32[]{:S(2)}, u32[]{:S(2)}) %collective-permute-start.23) | collective-permute-done | bytes 262176 | tf_op jit(solution)/shard_map/ppermute | solution.py:408
  76.5 5.2 %collective-permute-done.22.a = bf16[256,512]{1,0:T(8,128)(2,1)S(1)} collective-permute-done((bf16[256,512]{1,0:T(8,128)(2,1)S(1)}, bf16[256,512]{1,0:T(8,128)(2,1)S(1)}, u32[]{:S(2)}, u32[]{:S(2)}) %collective-permute-start.22) | collective-permute-done | bytes 262176 | tf_op jit(solution)/shard_map/ppermute | solution.py:408
  81.7 1.2 %collective-permute-done.24.c = bf16[256,512]{1,0:T(8,128)(2,1)S(1)} collective-permute-done((bf16[256,512]{1,0:T(8,128)(2,1)S(1)}, bf16[256,512]{1,0:T(8,128)(2,1)S(1)}, u32[]{:S(2)}, u32[]{:S(2)}) %collective-permute-start.24) | collective-permute-done | bytes 262176 | tf_op jit(solution)/shard_map/ppermute | solution.py:408
  82.9 0.8 add_up.1
  (26 shorter events, 0.2 us)
Async XLA Ops:
  0.0 17.8 %collective-permute-start = (bf16[256,512]{1,0:T(8,128)(2,1)}, bf16[256,512]{1,0:T(8,128)(2,1)S(1)}, u32[]{:S(2)}, u32[]{:S(2)}) collective-permute-start(bf16[256,512]{1,0:T(8,128)(2,1)} %refs_0_.5), channel_id=1, source_target_pairs={{0,4},{1,5},{2,6},{3,7},{4,0},{5,1},{6,2},{7,3},{8,12},{9,13},{10,... | collective-permute-start | bytes 786440 | tf_op jit(solution)/shard_map/ppermute | solution.py:408
  3.6 12.0 %collective-permute-start.2 = (bf16[256,512]{1,0:T(8,128)(2,1)}, bf16[256,512]{1,0:T(8,128)(2,1)S(1)}, u32[]{:S(2)}, u32[]{:S(2)}) collective-permute-start(bf16[256,512]{1,0:T(8,128)(2,1)} %refs_0_.5), channel_id=1, source_target_pairs={{0,2},{1,7},{2,4},{3,1},{4,6},{5,3},{6,0},{7,5},{8,10},{9,15},{10,... | collective-permute-start | bytes 786440 | tf_op jit(solution)/shard_map/ppermute | solution.py:408
  4.4 12.5 %collective-permute-start.4 = (bf16[256,512]{1,0:T(8,128)(2,1)}, bf16[256,512]{1,0:T(8,128)(2,1)S(1)}, u32[]{:S(2)}, u32[]{:S(2)}) collective-permute-start(bf16[256,512]{1,0:T(8,128)(2,1)} %refs_0_.5), channel_id=1, source_target_pairs={{0,1},{1,0},{2,3},{3,2},{4,5},{5,4},{6,7},{7,6},{8,9},{9,8},{10,11... | collective-permute-start | bytes 786440 | tf_op jit(solution)/shard_map/ppermute | solution.py:405
  5.1 12.4 %collective-permute-start.3 = (bf16[256,512]{1,0:T(8,128)(2,1)}, bf16[256,512]{1,0:T(8,128)(2,1)S(1)}, u32[]{:S(2)}, u32[]{:S(2)}) collective-permute-start(bf16[256,512]{1,0:T(8,128)(2,1)} %refs_0_.5), channel_id=1, source_target_pairs={{0,6},{1,3},{2,0},{3,5},{4,2},{5,7},{6,4},{7,1},{8,14},{9,11},{10,... | collective-permute-start | bytes 786440 | tf_op jit(solution)/shard_map/ppermute | solution.py:408
  11.7 5.2 %copy-start = (bf16[256,512]{1,0:T(8,128)(2,1)S(1)}, bf16[256,512]{1,0:T(8,128)(2,1)}, u32[]{:S(2)}) copy-start(bf16[256,512]{1,0:T(8,128)(2,1)} %refs_0_.5) | copy-start | bytes 786436
  15.6 2.8 %collective-permute-start.5 = (bf16[256,512]{1,0:T(8,128)(2,1)S(1)}, bf16[256,512]{1,0:T(8,128)(2,1)S(1)}, u32[]{:S(2)}, u32[]{:S(2)}) collective-permute-start(bf16[256,512]{1,0:T(8,128)(2,1)S(1)} %collective-permute-done.2.refs_0_), channel_id=1, source_target_pairs={{0,1},{1,0},{2,3},{3,2},{4,5},{5,4},{6,7},{7,6},{8,9},{9,8},{10,11... | collective-permute-start | bytes 786440 | tf_op jit(solution)/shard_map/ppermute | solution.py:405
  17.5 1.6 %collective-permute-start.6 = (bf16[256,512]{1,0:T(8,128)(2,1)S(1)}, bf16[256,512]{1,0:T(8,128)(2,1)S(1)}, u32[]{:S(2)}, u32[]{:S(2)}) collective-permute-start(bf16[256,512]{1,0:T(8,128)(2,1)S(1)} %collective-permute-done.3.refs_1_), channel_id=1, source_target_pairs={{0,1},{1,0},{2,3},{3,2},{4,5},{5,4},{6,7},{7,6},{8,9},{9,8},{10,11... | collective-permute-start | bytes 786440 | tf_op jit(solution)/shard_map/ppermute | solution.py:405
  17.8 2.4 %copy-start.1 = (f32[128]{0:T(128)S(1)}, f32[128]{0:T(128)}, u32[]{:S(2)}) copy-start(f32[128]{0:T(128)} %param.12) | copy-start | bytes 1540
  17.8 2.3 %copy-start.2 = (f32[128]{0:T(128)S(1)}, f32[128]{0:T(128)}, u32[]{:S(2)}) copy-start(f32[128]{0:T(128)} %param.13) | copy-start | bytes 1540
  17.8 2.3 %collective-permute-start.1 = (bf16[256,512]{1,0:T(8,128)(2,1)S(1)}, bf16[256,512]{1,0:T(8,128)(2,1)S(1)}, u32[]{:S(2)}, u32[]{:S(2)}) collective-permute-start(bf16[256,512]{1,0:T(8,128)(2,1)S(1)} %collective-permute-done.refs_0_), channel_id=1, source_target_pairs={{0,1},{1,0},{2,3},{3,2},{4,5},{5,4},{6,7},{7,6},{8,9},{9,8},{10,11... | collective-permute-start | bytes 786440 | tf_op jit(solution)/shard_map/ppermute | solution.py:405
  21.2 9.3 %collective-permute-start.7 = (bf16[256,256]{1,0:T(8,128)(2,1)S(1)}, bf16[256,256]{1,0:T(8,128)(2,1)S(1)}, u32[]{:S(2)}, u32[]{:S(2)}) collective-permute-start(bf16[256,256]{1,0:T(8,128)(2,1)S(1)} %get-tuple-element.57.refs_3_.own), channel_id=1, source_target_pairs={{0,32},{8,40},{16,48},{24,56},{32,64},{40,72},{48,80},{56,88},{64,... | collective-permute-start | bytes 393224 | tf_op jit(solution)/shard_map/ppermute | solution.py:421
  30.5 5.5 %collective-permute-start.8 = (bf16[256,256]{1,0:T(8,128)(2,1)S(1)}, bf16[256,256]{1,0:T(8,128)(2,1)S(1)}, u32[]{:S(2)}, u32[]{:S(2)}) collective-permute-start(bf16[256,256]{1,0:T(8,128)(2,1)S(1)} %collective-permute-done.7.refs_0_.refs_3_), channel_id=1, source_target_pairs={{0,32},{8,40},{16,48},{24,56},{32,64},{40,72},{48,80},{56,88},{64,... | collective-permute-start | bytes 393224 | tf_op jit(solution)/shard_map/ppermute | solution.py:421
  30.5 13.3 %collective-permute-start.13 = (bf16[4,512,512]{2,1,0:T(8,128)(2,1)}, bf16[4,512,512]{2,1,0:T(8,128)(2,1)}, u32[]{:S(2)}, u32[]{:S(2)}) collective-permute-start(bf16[4,512,512]{2,1,0:T(8,128)(2,1)} %get-tuple-element.58), channel_id=1, source_target_pairs={{0,1},{1,0},{2,3},{3,2},{4,5},{5,4},{6,7},{7,6},{8,9},{9,8},{10,11... | collective-permute-start | bytes 6291464 | tf_op jit(solution)/shard_map/ppermute | solution.py:405
  31.2 6.5 %collective-permute-start.14 = (bf16[256,256]{1,0:T(8,128)(2,1)S(1)}, bf16[256,256]{1,0:T(8,128)(2,1)S(1)}, u32[]{:S(2)}, u32[]{:S(2)}) collective-permute-start(bf16[256,256]{1,0:T(8,128)(2,1)S(1)} %collective-permute-done.7.refs_0_.refs_3_), channel_id=1, source_target_pairs={{0,8},{1,25},{2,10},{3,27},{4,12},{5,29},{6,14},{7,31},{8,0},{9,17... | collective-permute-start | bytes 393224 | tf_op jit(solution)/shard_map/ppermute | solution.py:430
  36.1 5.7 %collective-permute-start.9 = (bf16[256,256]{1,0:T(8,128)(2,1)S(1)}, bf16[256,256]{1,0:T(8,128)(2,1)S(1)}, u32[]{:S(2)}, u32[]{:S(2)}) collective-permute-start(bf16[256,256]{1,0:T(8,128)(2,1)S(1)} %collective-permute-done.8.refs_4_.refs_0_), channel_id=1, source_target_pairs={{0,32},{8,40},{16,48},{24,56},{32,64},{40,72},{48,80},{56,88},{64,... | collective-permute-start | bytes 393224 | tf_op jit(solution)/shard_map/ppermute | solution.py:421
  37.8 14.1 %collective-permute-start.20 = (bf16[512,256]{1,0:T(8,128)(2,1)S(1)}, bf16[512,256]{1,0:T(8,128)(2,1)S(1)}, u32[]{:S(2)}, u32[]{:S(2)}) collective-permute-start(bf16[512,256]{1,0:T(8,128)(2,1)S(1)} %get-tuple-element.69), channel_id=1, source_target_pairs={{0,24},{1,9},{2,26},{3,11},{4,28},{5,13},{6,30},{7,15},{8,16},{9,1... | collective-permute-start | bytes 786440 | tf_op jit(solution)/shard_map/ppermute | solution.py:430
  39.2 6.0 %collective-permute-start.12 = (bf16[256,256]{1,0:T(8,128)(2,1)S(1)}, bf16[256,256]{1,0:T(8,128)(2,1)S(1)}, u32[]{:S(2)}, u32[]{:S(2)}) collective-permute-start(bf16[256,256]{1,0:T(8,128)(2,1)S(1)} %collective-permute-done.8.refs_4_.refs_0_), channel_id=1, source_target_pairs={{0,8},{1,25},{2,10},{3,27},{4,12},{5,29},{6,14},{7,31},{8,0},{9,17... | collective-permute-start | bytes 393224 | tf_op jit(solution)/shard_map/ppermute | solution.py:430
  41.8 5.4 %collective-permute-start.11 = (bf16[256,256]{1,0:T(8,128)(2,1)S(1)}, bf16[256,256]{1,0:T(8,128)(2,1)S(1)}, u32[]{:S(2)}, u32[]{:S(2)}) collective-permute-start(bf16[256,256]{1,0:T(8,128)(2,1)S(1)} %collective-permute-done.9.refs_0_.refs_6_), channel_id=1, source_target_pairs={{0,32},{8,40},{16,48},{24,56},{32,64},{40,72},{48,80},{56,88},{64,... | collective-permute-start | bytes 393224 | tf_op jit(solution)/shard_map/ppermute | solution.py:421
  41.9 8.0 %collective-permute-start.10 = (bf16[256,256]{1,0:T(8,128)(2,1)S(1)}, bf16[256,256]{1,0:T(8,128)(2,1)S(1)}, u32[]{:S(2)}, u32[]{:S(2)}) collective-permute-start(bf16[256,256]{1,0:T(8,128)(2,1)S(1)} %collective-permute-done.9.refs_0_.refs_6_), channel_id=1, source_target_pairs={{0,8},{1,25},{2,10},{3,27},{4,12},{5,29},{6,14},{7,31},{8,0},{9,17... | collective-permute-start | bytes 393224 | tf_op jit(solution)/shard_map/ppermute | solution.py:430
  45.2 9.6 %collective-permute-start.19 = (bf16[512,256]{1,0:T(8,128)(2,1)S(1)}, bf16[512,256]{1,0:T(8,128)(2,1)S(1)}, u32[]{:S(2)}, u32[]{:S(2)}) collective-permute-start(bf16[512,256]{1,0:T(8,128)(2,1)S(1)} %get-tuple-element.68), channel_id=1, source_target_pairs={{0,24},{1,9},{2,26},{3,11},{4,28},{5,13},{6,30},{7,15},{8,16},{9,1... | collective-permute-start | bytes 786440 | tf_op jit(solution)/shard_map/ppermute | solution.py:430
  47.3 8.3 %collective-permute-start.16 = (bf16[256,256]{1,0:T(8,128)(2,1)S(1)}, bf16[256,256]{1,0:T(8,128)(2,1)S(1)}, u32[]{:S(2)}, u32[]{:S(2)}) collective-permute-start(bf16[256,256]{1,0:T(8,128)(2,1)S(1)} %get-tuple-element.65), channel_id=1, source_target_pairs={{0,16},{8,24},{16,0},{24,8},{32,48},{40,56},{48,32},{56,40},{64,80... | collective-permute-start | bytes 393224 | tf_op jit(solution)/shard_map/ppermute | solution.py:418
  49.2 9.5 %collective-permute-start.17 = (bf16[256,256]{1,0:T(8,128)(2,1)S(1)}, bf16[256,256]{1,0:T(8,128)(2,1)S(1)}, u32[]{:S(2)}, u32[]{:S(2)}) collective-permute-start(bf16[256,256]{1,0:T(8,128)(2,1)S(1)} %get-tuple-element.66), channel_id=1, source_target_pairs={{0,8},{8,16},{16,24},{24,0},{32,40},{40,48},{48,56},{56,32},{64,72... | collective-permute-start | bytes 393224 | tf_op jit(solution)/shard_map/ppermute | solution.py:418
  49.9 8.8 %collective-permute-start.18 = (bf16[256,256]{1,0:T(8,128)(2,1)S(1)}, bf16[256,256]{1,0:T(8,128)(2,1)S(1)}, u32[]{:S(2)}, u32[]{:S(2)}) collective-permute-start(bf16[256,256]{1,0:T(8,128)(2,1)S(1)} %get-tuple-element.67), channel_id=1, source_target_pairs={{0,24},{8,0},{16,8},{24,16},{32,56},{40,32},{48,40},{56,48},{64,88... | collective-permute-start | bytes 393224 | tf_op jit(solution)/shard_map/ppermute | solution.py:418
  51.9 8.0 %collective-permute-start.15 = (bf16[512,256]{1,0:T(8,128)(2,1)S(1)}, bf16[512,256]{1,0:T(8,128)(2,1)S(1)}, u32[]{:S(2)}, u32[]{:S(2)}) collective-permute-start(bf16[512,256]{1,0:T(8,128)(2,1)S(1)} %get-tuple-element.64), channel_id=1, source_target_pairs={{0,24},{1,9},{2,26},{3,11},{4,28},{5,13},{6,30},{7,15},{8,16},{9,1... | collective-permute-start | bytes 786440 | tf_op jit(solution)/shard_map/ppermute | solution.py:430
  61.4 5.5 %collective-permute-start.21 = (bf16[256,512]{1,0:T(8,128)(2,1)S(1)}, bf16[256,512]{1,0:T(8,128)(2,1)S(1)}, u32[]{:S(2)}, u32[]{:S(2)}) collective-permute-start(bf16[256,512]{1,0:T(8,128)(2,1)S(1)} %get-tuple-element.76.a_ref), channel_id=1, source_target_pairs={{0,1},{1,0},{2,3},{3,2},{4,5},{5,4},{6,7},{7,6},{8,9},{9,8},{10,11... | collective-permute-start | bytes 786440 | tf_op jit(solution)/shard_map/ppermute | solution.py:405
  67.3 9.1 %collective-permute-start.23 = (bf16[256,512]{1,0:T(8,128)(2,1)S(1)}, bf16[256,512]{1,0:T(8,128)(2,1)S(1)}, u32[]{:S(2)}, u32[]{:S(2)}) collective-permute-start(bf16[256,512]{1,0:T(8,128)(2,1)S(1)} %out_project.5), channel_id=1, source_target_pairs={{0,4},{1,5},{2,6},{3,7},{4,0},{5,1},{6,2},{7,3},{8,12},{9,13},{10,... | collective-permute-start | bytes 786440 | tf_op jit(solution)/shard_map/ppermute | solution.py:408
  70.8 10.9 %collective-permute-start.22 = (bf16[256,512]{1,0:T(8,128)(2,1)S(1)}, bf16[256,512]{1,0:T(8,128)(2,1)S(1)}, u32[]{:S(2)}, u32[]{:S(2)}) collective-permute-start(bf16[256,512]{1,0:T(8,128)(2,1)S(1)} %get-tuple-element.79), channel_id=1, source_target_pairs={{0,2},{1,7},{2,4},{3,1},{4,6},{5,3},{6,0},{7,5},{8,10},{9,15},{10,... | collective-permute-start | bytes 786440 | tf_op jit(solution)/shard_map/ppermute | solution.py:408
  71.9 11.0 %collective-permute-start.24 = (bf16[256,512]{1,0:T(8,128)(2,1)S(1)}, bf16[256,512]{1,0:T(8,128)(2,1)S(1)}, u32[]{:S(2)}, u32[]{:S(2)}) collective-permute-start(bf16[256,512]{1,0:T(8,128)(2,1)S(1)} %get-tuple-element.80), channel_id=1, source_target_pairs={{0,6},{1,3},{2,0},{3,5},{4,2},{5,7},{6,4},{7,1},{8,14},{9,11},{10,... | collective-permute-start | bytes 786440 | tf_op jit(solution)/shard_map/ppermute | solution.py:408

commit v4 on v3

--- a/solution.py
+++ b/solution.py
@@ -438,13 +438,6 @@
     w_in, flag_in = stage(
         [w_query, w_key, w_value], tuple(plan), [(tps, part, nq + 2 * nk)], "stage_in"
     )
-    cols = w_out.shape[1] // tps
-    plan = [(0, 1, cols, (d, 0), 0, k, 0, cols) for k, d in enumerate((2, 1, -1, 0))]
-    plan += [(0, 1, cols, (d, 1), 1, k, 0, cols) for k, d in enumerate((2, -1, 1, 0))]
-    w_own, w_send, flag_out = stage(
-        [w_out], tuple(plan), [(nx, w_out.shape[0], cols)] * 2, "stage_out"
-    )
-
     token_index = my_seq * tok + jnp.arange(tok, dtype=jnp.int32)
     start = doc_tables(doc_lengths, token_index)
     cos, sin = rope_tables(token_index - start, head)
@@ -454,7 +447,7 @@
     a1, a3, a2 = along_x(own, 1), along_x(own, nx - 1), along_x(own, 2)
     b0 = sibling(own)
     acc = project([own, b0], w_in, 0)
-    a1, flags = after([flag_in, flag_out], a1)
+    a1, flags = after([flag_in], a1)
     b1 = sibling(a1)
     a3, acc, _ = after([], a3, acc)
     b3 = sibling(a3)
@@ -464,35 +457,44 @@
     queries, kv = project(
         [a2, b2], w_in, 6, acc, last=(cos, sin, q_gain[None, :], k_gain[None, :])
     )
+    w_late, kv = lax.optimization_barrier((w_out, kv))
+    cols = w_out.shape[1] // tps
+    plan = [(0, 1, cols, (d, 0), 0, k, 0, cols) for k, d in enumerate((2, 1, -1, 0))]
+    plan += [(0, 1, cols, (d, 1), 1, k, 0, cols) for k, d in enumerate((2, -1, 1, 0))]
+    w_own, w_send, flag_out = stage(
+        [w_late], tuple(plan), [(nx, w_out.shape[0], cols)] * 2, "stage_out"
+    )
+
     attn = (start, queries, start_col, index_col)
     r0 = kv
     r1 = along_z(r0, 1)
+    r1, staged = after([flag_out], r1)
     r2 = along_z(r1, 1)
+    o, flag_a = attend(*attn, [(r0, [(0, 0)])])
+    r2, first = after([flag_a], r2)
     r3 = along_z(r2, 1)
     r4 = along_z(r3, 1)
     s1, s2, s3 = swap_y(r1, 0), swap_y(r2, 0), swap_y(r3, 0)
     w_sib = sibling(w_send)
     got = hold(w_sib, cost=0)
-    o, flag_a = attend(*attn, [(r0, [(0, 0)])])
-    x_one, flag_1 = pack([r1, s1], [(0, 0), (1, 0)], tok)
+    x_one, flag_1 = pack([r1, s1], [(0, 0), (1, 0)], tok, flags=staged)
     near_one = swap_y(x_one, 1)
-    o, flag_b = attend(*attn, [(r1, [(1, 0)]), (r2, [(2, 0)])], o, flags=[flag_1])
-    x_two, flag_2 = pack([r2, s2], [(0, 0), (1, 0)], tok, flags=[hold(r3), got, flag_b])
+    x_two, flag_2 = pack([r2, s2], [(0, 0), (1, 0)], tok, flags=[*first, hold(r3), got])
     near_two = swap_y(x_two, 1)
     x1, x2, x3, flag_m = mixes(r0, r4, flags=[hold(r4), flag_2])
-    mixed = [(along_y((x1, x2, x3)[e - 1], e), [(None, e)]) for e in (2, 1, 3)]
+    mixed = [(along_y((x1, x2, x3)[e - 1], e), [(None, e)]) for e in (1, 3, 2)]
     x_three, flag_3 = pack([r3, s3], [(0, 0), (1, 0)], tok, flags=[flag_m])
     near_three = swap_y(x_three, 1)
     o, flag_c = attend(
         *attn,
-        [(s1, [(1, 1)]), (s2, [(2, 1)]), (near_one, [(1, 2), (1, 3)]), (r3, [(3, 0)])],
+        [(r1, [(1, 0)]), (r2, [(2, 0)]), (s1, [(1, 1)]), (s2, [(2, 1)]), (near_one, [(1, 2), (1, 3)]), (r3, [(3, 0)])],
         o,
         flags=[flag_3],
     )
-    w_sib, flag_w = fetch(w_sib, [flag_3])
     o, flag_d = attend(
         *attn, [(near_two, [(2, 2), (2, 3)]), (s3, [(3, 1)]), (r4, [(4, 0)])], o
     )
+    w_sib, flag_w = fetch(w_sib, [flag_d])
     attended, _ = attend(
         *attn,
         [(near_three, [(3, 2), (3, 3)]), *mixed],

time: 83.8 us -> 82.6 us (0.986)
  waiting for transfers between devices: 29.6 us -> 26.7 us
  starting transfers between devices: 32.3 us -> 34.7 us
    ppermute x3, waiting for transfers between devices: 3.08 us -> 0.01 us  [along_y(): lax.ppermute(a, 'seq', [(i, i // ny * ny + (i + d) % ny) for i in range(s...]
    ppermute x4, waiting for transfers between devices: 11.6 us -> 8.66 us  [along_z(): lax.ppermute(a, 'seq', [(i, (i // ny + d) % nz * ny + i % ny) for i in ra...]
    ppermute x6, waiting for transfers between devices: 10.4 us -> 12.9 us  [along_x(): lax.ppermute(a, 'tp', [(i, (i // 2 + (d if i % 2 == 0 else -d)) % nx * 2...]
    ppermute x6, starting transfers between devices: 7.83 us -> 9.25 us  [sibling(): return lax.ppermute(a, 'tp', [(i, i ^ 1) for i in range(tps)])]
    pallas_call x5 -> x4, Pallas kernels: 5.67 us -> 4.51 us  [attend(): pl.pallas_call(functools.partial(attend_kernel, layout, first, final, len...]
    ppermute x6, starting transfers between devices: 8.13 us -> 9.16 us  [swap_y(): return lax.ppermute(a, ('seq', 'tp'), pairs)]
where the time goes in v4:
time: 82.6 us; the launch traced here: 82.4 us
  starting transfers between devices  34.7 us (42%)
  waiting for transfers between devices  26.7 us (32%)
  Pallas kernels  18.4 us (22%)
  other arithmetic  1.6 us (2%)
  local copies, waits for them, and re-layouts  0.88 us (1%)
    ppermute x6, waiting for transfers between devices, along_x(): lax.ppermute(a, 'tp', [(i, (i // 2 + (d if i % 2 == 0 else -d)) % nx * 2...  12.9 us
    ppermute x6, starting transfers between devices, along_x(): lax.ppermute(a, 'tp', [(i, (i // 2 + (d if i % 2 == 0 else -d)) % nx * 2...  10.6 us
    ppermute x6, starting transfers between devices, sibling(): return lax.ppermute(a, 'tp', [(i, i ^ 1) for i in range(tps)])  9.25 us
    ppermute x6, starting transfers between devices, swap_y(): return lax.ppermute(a, ('seq', 'tp'), pairs)  9.16 us
    ppermute x4, waiting for transfers between devices, along_z(): lax.ppermute(a, 'seq', [(i, (i // ny + d) % nz * ny + i % ny) for i in ra...  8.66 us
    pallas_call x2, Pallas kernels, stage(): pl.pallas_call(functools.partial(stage_kernel, plan, len(arrays)), in_spe...  6.61 us
    pallas_call x4, Pallas kernels, attend(): pl.pallas_call(functools.partial(attend_kernel, layout, first, final, len...  4.51 us
    ppermute x3, starting transfers between devices, along_y(): lax.ppermute(a, 'seq', [(i, i // ny * ny + (i + d) % ny) for i in range(s...  3.92 us
  transfers between devices with their start and end apart: 25, of which 12 were waited for; matrix products, arithmetic and copies ran while one was open for 3% of the time, Pallas kernels for 18%

profile of v4, /device:TPU:1, one launch (start us, length us, event | category | flops | bytes accessed | tf_op | source)
XLA Modules:
  0.0 82.4 jit_solution(5056007773685372122)
XLA Ops:
  0.0 3.6 %collective-permute-start = (bf16[256,512]{1,0:T(8,128)(2,1)}, bf16[256,512]{1,0:T(8,128)(2,1)S(1)}, u32[]{:S(2)}, u32[]{:S(2)}) collective-permute-start(bf16[256,512]{1,0:T(8,128)(2,1)} %refs_0_.3), channel_id=1, source_target_pairs={{0,4},{1,5},{2,6},{3,7},{4,0},{5,1},{6,2},{7,3},{8,12},{9,13},{10,... | collective-permute-start | bytes 786440 | tf_op jit(solution)/shard_map/ppermute | solution.py:408
  3.6 1.0 %collective-permute-start.4 = (bf16[256,512]{1,0:T(8,128)(2,1)}, bf16[256,512]{1,0:T(8,128)(2,1)S(1)}, u32[]{:S(2)}, u32[]{:S(2)}) collective-permute-start(bf16[256,512]{1,0:T(8,128)(2,1)} %refs_0_.3), channel_id=1, source_target_pairs={{0,1},{1,0},{2,3},{3,2},{4,5},{5,4},{6,7},{7,6},{8,9},{9,8},{10,11... | collective-permute-start | bytes 786440 | tf_op jit(solution)/shard_map/ppermute | solution.py:405
  4.5 0.3 collective-permute-start.3
  4.8 2.4 %collective-permute-start.2 = (bf16[256,512]{1,0:T(8,128)(2,1)}, bf16[256,512]{1,0:T(8,128)(2,1)S(1)}, u32[]{:S(2)}, u32[]{:S(2)}) collective-permute-start(bf16[256,512]{1,0:T(8,128)(2,1)} %refs_0_.3), channel_id=1, source_target_pairs={{0,2},{1,7},{2,4},{3,1},{4,6},{5,3},{6,0},{7,5},{8,10},{9,15},{10,... | collective-permute-start | bytes 786440 | tf_op jit(solution)/shard_map/ppermute | solution.py:408
  7.2 0.7 copy.15
  8.0 0.1 reduce
  8.1 0.7 select_reduce_fusion.start_s
  8.9 3.0 %stage_in.1 = (bf16[8,512,768]{2,1,0:T(8,128)(2,1)S(1)}, f32[8,128]{1,0:T(8,128)S(1)}) custom-call(bf16[4096,512]{1,0:T(8,128)(2,1)} %refs_0_.2, bf16[4096,128]{1,0:T(8,128)(2,1)} %refs_1_.1, bf16[4096,128]{1,0:T(8,128)(2,1)} %refs_2_.1), custom_call_target="tpu_custom_call" | custom-call | bytes 12582912 | tf_op jit(solution)/shard_map/stage_in/pallas_call | solution.py:114
  11.9 0.5 fusion
  12.4 0.0 collective-permute-done.4.refs_1_
  12.5 0.6 project.3.refs_5_
  13.0 2.9 %collective-permute-done.3.refs_1_ = bf16[256,512]{1,0:T(8,128)(2,1)S(1)} collective-permute-done((bf16[256,512]{1,0:T(8,128)(2,1)}, bf16[256,512]{1,0:T(8,128)(2,1)S(1)}, u32[]{:S(2)}, u32[]{:S(2)}) %collective-permute-start.3) | collective-permute-done | bytes 262176 | tf_op jit(solution)/shard_map/ppermute | solution.py:408
  15.9 1.1 %collective-permute-start.6 = (bf16[256,512]{1,0:T(8,128)(2,1)S(1)}, bf16[256,512]{1,0:T(8,128)(2,1)S(1)}, u32[]{:S(2)}, u32[]{:S(2)}) collective-permute-start(bf16[256,512]{1,0:T(8,128)(2,1)S(1)} %collective-permute-done.3.refs_1_), channel_id=1, source_target_pairs={{0,1},{1,0},{2,3},{3,2},{4,5},{5,4},{6,7},{7,6},{8,9},{9,8},{10,11... | collective-permute-start | bytes 786440 | tf_op jit(solution)/shard_map/ppermute | solution.py:405
  17.0 0.0 collective-permute-done.2.refs_0_
  17.0 0.2 collective-permute-start.5
  17.2 0.1 pad_maximum_fusion
  17.4 0.0 copy-start.1
  17.4 0.0 copy-start.2
  17.4 0.4 collective-permute-start.1
  17.8 0.4 collective-permute-done.6.refs_3_
  18.2 0.4 collective-permute-done.5.refs_2_
  18.6 1.0 %project.4.refs_3_ = f32[256,768]{1,0:T(8,128)S(1)} custom-call(bf16[256,512]{1,0:T(8,128)(2,1)S(1)} %collective-permute-done.2.refs_0_, bf16[256,512]{1,0:T(8,128)(2,1)S(1)} %collective-permute-done.3.refs_1_, bf16[256,512]{1,0:T(8,128)(2,1)S(1)} %collective-permute-done.5.refs_2_, bf16[256,512]{1,0:T(8,128)(2,1)S(1)} %collective-permute-done.6.refs_3_, ...), custom_call_target="tpu_custom_call" | custom-call | flops 1610612736 | bytes 3145728 | tf_op jit(solution)/shard_map/project/pallas_call | solution.py:250
  19.5 0.0 collective-permute-done.1.refs_1_
  19.6 1.0 %project.5 = (bf16[1024,128]{1,0:T(8,128)(2,1)S(1)}, bf16[256,256]{1,0:T(8,128)(2,1)S(1)}) custom-call(bf16[256,512]{1,0:T(8,128)(2,1)S(1)} %collective-permute-done.refs_0_, bf16[256,512]{1,0:T(8,128)(2,1)S(1)} %collective-permute-done.1.refs_1_, bf16[8,512,768]{2,1,0:T(8,128)(2,1)S(1)} %get-tuple-element.47.refs_2_.refs_4_, ...), custom_call_target="tpu_custom_call" | custom-call | flops 805306368 | bytes 1572864 | tf_op jit(solution)/shard_map/project/pallas_call | solution.py:250
  20.6 1.7 %collective-permute-start.7 = (bf16[256,256]{1,0:T(8,128)(2,1)S(1)}, bf16[256,256]{1,0:T(8,128)(2,1)S(1)}, u32[]{:S(2)}, u32[]{:S(2)}) collective-permute-start(bf16[256,256]{1,0:T(8,128)(2,1)S(1)} %get-tuple-element.59.refs_3_.own), channel_id=1, source_target_pairs={{0,32},{8,40},{16,48},{24,56},{32,64},{40,72},{48,80},{56,88},{64,... | collective-permute-start | bytes 393224 | tf_op jit(solution)/shard_map/ppermute | solution.py:421
  22.3 3.6 %stage_out.1 = (bf16[4,512,512]{2,1,0:T(8,128)(2,1)S(1)}, bf16[4,512,512]{2,1,0:T(8,128)(2,1)}, f32[8,128]{1,0:T(8,128)S(1)}) custom-call(bf16[512,4096]{1,0:T(8,128)(2,1)} %refs_0_.4), custom_call_target="tpu_custom_call" | custom-call | bytes 8388608 | tf_op jit(solution)/shard_map/stage_out/pallas_call | solution.py:114
  25.9 3.9 %collective-permute-done.7.refs_0_.refs_3_ = bf16[256,256]{1,0:T(8,128)(2,1)S(1)} collective-permute-done((bf16[256,256]{1,0:T(8,128)(2,1)S(1)}, bf16[256,256]{1,0:T(8,128)(2,1)S(1)}, u32[]{:S(2)}, u32[]{:S(2)}) %collective-permute-start.7) | collective-permute-done | bytes 131104 | tf_op jit(solution)/shard_map/ppermute | solution.py:421
  29.8 0.0 collective-permute-start.8
  29.8 0.9 %collective-permute-start.13 = (bf16[4,512,512]{2,1,0:T(8,128)(2,1)}, bf16[4,512,512]{2,1,0:T(8,128)(2,1)}, u32[]{:S(2)}, u32[]{:S(2)}) collective-permute-start(bf16[4,512,512]{2,1,0:T(8,128)(2,1)} %get-tuple-element.66), channel_id=1, source_target_pairs={{0,1},{1,0},{2,3},{3,2},{4,5},{5,4},{6,7},{7,6},{8,9},{9,8},{10,11... | collective-permute-start | bytes 6291464 | tf_op jit(solution)/shard_map/ppermute | solution.py:405
  30.7 0.1 copy.19.refs_1_
  30.9 1.1 %attend.4 = (f32[1024,256]{1,0:T(8,128)S(1)}, f32[8,128]{1,0:T(8,128)S(1)}) custom-call(s32[256]{0:T(256)S(1)} %select_reduce_fusion.start_s, bf16[1024,128]{1,0:T(8,128)(2,1)S(1)} %get-tuple-element.55.refs_0_, s32[256,1]{1,0:T(8,128)S(1)} %copy.19.refs_1_, s32[256,1]{1,0:T(8,128)S(1)} %iota_add_fusion.refs_2_, ...), custom_call_target="tpu_custom_call" | custom-call | flops 268435456 | bytes 2097152 | tf_op jit(solution)/shard_map/attend/pallas_call | solution.py:333
  32.0 2.8 %collective-permute-start.19 = (bf16[256,256]{1,0:T(8,128)(2,1)S(1)}, bf16[256,256]{1,0:T(8,128)(2,1)S(1)}, u32[]{:S(2)}, u32[]{:S(2)}) collective-permute-start(bf16[256,256]{1,0:T(8,128)(2,1)S(1)} %collective-permute-done.7.refs_0_.refs_3_), channel_id=1, source_target_pairs={{0,8},{1,25},{2,10},{3,27},{4,12},{5,29},{6,14},{7,31},{8,0},{9,17... | collective-permute-start | bytes 393224 | tf_op jit(solution)/shard_map/ppermute | solution.py:430
  34.8 0.4 collective-permute-done.8.refs_0_.refs_4_
  35.2 0.0 collective-permute-start.9
  35.2 2.7 %collective-permute-start.12 = (bf16[256,256]{1,0:T(8,128)(2,1)S(1)}, bf16[256,256]{1,0:T(8,128)(2,1)S(1)}, u32[]{:S(2)}, u32[]{:S(2)}) collective-permute-start(bf16[256,256]{1,0:T(8,128)(2,1)S(1)} %collective-permute-done.8.refs_0_.refs_4_), channel_id=1, source_target_pairs={{0,8},{1,25},{2,10},{3,27},{4,12},{5,29},{6,14},{7,31},{8,0},{9,17... | collective-permute-start | bytes 393224 | tf_op jit(solution)/shard_map/ppermute | solution.py:430
  37.9 0.6 pack.5
  38.5 0.0 collective-permute-start.20
  38.5 1.7 %collective-permute-done.9.refs_0_.refs_8_ = bf16[256,256]{1,0:T(8,128)(2,1)S(1)} collective-permute-done((bf16[256,256]{1,0:T(8,128)(2,1)S(1)}, bf16[256,256]{1,0:T(8,128)(2,1)S(1)}, u32[]{:S(2)}, u32[]{:S(2)}) %collective-permute-start.9) | collective-permute-done | bytes 131104 | tf_op jit(solution)/shard_map/ppermute | solution.py:421
  40.2 0.0 collective-permute-start.11
  40.2 2.7 %collective-permute-start.10 = (bf16[256,256]{1,0:T(8,128)(2,1)S(1)}, bf16[256,256]{1,0:T(8,128)(2,1)S(1)}, u32[]{:S(2)}, u32[]{:S(2)}) collective-permute-start(bf16[256,256]{1,0:T(8,128)(2,1)S(1)} %collective-permute-done.9.refs_0_.refs_8_), channel_id=1, source_target_pairs={{0,8},{1,25},{2,10},{3,27},{4,12},{5,29},{6,14},{7,31},{8,0},{9,17... | collective-permute-start | bytes 393224 | tf_op jit(solution)/shard_map/ppermute | solution.py:430
  43.0 0.1 collective-permute-start.18
  43.1 2.7 %collective-permute-done.11.refs_0_.far.refs_5_ = bf16[256,256]{1,0:T(8,128)(2,1)S(1)} collective-permute-done((bf16[256,256]{1,0:T(8,128)(2,1)S(1)}, bf16[256,256]{1,0:T(8,128)(2,1)S(1)}, u32[]{:S(2)}, u32[]{:S(2)}) %collective-permute-start.11) | collective-permute-done | bytes 131104 | tf_op jit(solution)/shard_map/ppermute | solution.py:421
  45.8 0.8 %collective-permute-start.15 = (bf16[256,256]{1,0:T(8,128)(2,1)S(1)}, bf16[256,256]{1,0:T(8,128)(2,1)S(1)}, u32[]{:S(2)}, u32[]{:S(2)}) collective-permute-start(bf16[256,256]{1,0:T(8,128)(2,1)S(1)} %get-tuple-element.70), channel_id=1, source_target_pairs={{0,8},{8,16},{16,24},{24,0},{32,40},{40,48},{48,56},{56,32},{64,72... | collective-permute-start | bytes 393224 | tf_op jit(solution)/shard_map/ppermute | solution.py:418
  46.7 1.9 %collective-permute-start.16 = (bf16[256,256]{1,0:T(8,128)(2,1)S(1)}, bf16[256,256]{1,0:T(8,128)(2,1)S(1)}, u32[]{:S(2)}, u32[]{:S(2)}) collective-permute-start(bf16[256,256]{1,0:T(8,128)(2,1)S(1)} %get-tuple-element.71), channel_id=1, source_target_pairs={{0,24},{8,0},{16,8},{24,16},{32,56},{40,32},{48,40},{56,48},{64,88... | collective-permute-start | bytes 393224 | tf_op jit(solution)/shard_map/ppermute | solution.py:418
  48.6 0.0 collective-permute-done.10.refs_1_.refs_4_
  48.6 1.2 %collective-permute-start.17 = (bf16[256,256]{1,0:T(8,128)(2,1)S(1)}, bf16[256,256]{1,0:T(8,128)(2,1)S(1)}, u32[]{:S(2)}, u32[]{:S(2)}) collective-permute-start(bf16[256,256]{1,0:T(8,128)(2,1)S(1)} %get-tuple-element.72), channel_id=1, source_target_pairs={{0,16},{8,24},{16,0},{24,8},{32,48},{40,56},{48,32},{56,40},{64,80... | collective-permute-start | bytes 393224 | tf_op jit(solution)/shard_map/ppermute | solution.py:418
  49.8 0.8 collective-permute-start.14
  50.5 1.3 %attend.5 = (f32[1024,256]{1,0:T(8,128)S(1)}, f32[8,128]{1,0:T(8,128)}) custom-call(s32[256]{0:T(256)S(1)} %select_reduce_fusion.start_s, bf16[1024,128]{1,0:T(8,128)(2,1)S(1)} %get-tuple-element.55.refs_0_, s32[256,1]{1,0:T(8,128)S(1)} %copy.19.refs_1_, s32[256,1]{1,0:T(8,128)S(1)} %iota_add_fusion.refs_2_, ...), custom_call_target="tpu_custom_call" | custom-call | flops 1879048192 | bytes 2097152 | tf_op jit(solution)/shard_map/attend/pallas_call | solution.py:333
  51.8 0.7 attend.6
  52.5 1.6 %fetch.1 = (bf16[4,512,512]{2,1,0:T(8,128)(2,1)S(1)}, f32[8,128]{1,0:T(8,128)S(1)}) custom-call(bf16[4,512,512]{2,1,0:T(8,128)(2,1)} %collective-permute-done.13.refs_0_.src, f32[8,128]{1,0:T(8,128)S(1)} %get-tuple-element.80.refs_0_.refs_3_), custom_call_target="tpu_custom_call" | custom-call | tf_op jit(solution)/shard_map/fetch/pallas_call | solution.py:101
  54.2 3.1 %collective-permute-done.14.refs_3_ = bf16[512,256]{1,0:T(8,128)(2,1)S(1)} collective-permute-done((bf16[512,256]{1,0:T(8,128)(2,1)S(1)}, bf16[512,256]{1,0:T(8,128)(2,1)S(1)}, u32[]{:S(2)}, u32[]{:S(2)}) %collective-permute-start.14) | collective-permute-done | bytes 262176 | tf_op jit(solution)/shard_map/ppermute | solution.py:430
  57.3 1.5 %attend.7 = (bf16[256,512]{1,0:T(8,128)(2,1)S(1)}, f32[8,128]{1,0:T(8,128)}) custom-call(s32[256]{0:T(256)S(1)} %select_reduce_fusion.start_s, bf16[1024,128]{1,0:T(8,128)(2,1)S(1)} %get-tuple-element.55.refs_0_, s32[256,1]{1,0:T(8,128)S(1)} %copy.19.refs_1_, s32[256,1]{1,0:T(8,128)S(1)} %iota_add_fusion.refs_2_, ...), custom_call_target="tpu_custom_call" | custom-call | flops 1342177280 | bytes 2097152 | tf_op jit(solution)/shard_map/attend/pallas_call | solution.py:333
  58.8 5.8 %collective-permute-start.21 = (bf16[256,512]{1,0:T(8,128)(2,1)S(1)}, bf16[256,512]{1,0:T(8,128)(2,1)S(1)}, u32[]{:S(2)}, u32[]{:S(2)}) collective-permute-start(bf16[256,512]{1,0:T(8,128)(2,1)S(1)} %get-tuple-element.82.a_ref), channel_id=1, source_target_pairs={{0,1},{1,0},{2,3},{3,2},{4,5},{5,4},{6,7},{7,6},{8,9},{9,8},{10,11... | collective-permute-start | bytes 786440 | tf_op jit(solution)/shard_map/ppermute | solution.py:405
  64.5 1.2 %collective-permute-done.21.b_ref = bf16[256,512]{1,0:T(8,128)(2,1)S(1)} collective-permute-done((bf16[256,512]{1,0:T(8,128)(2,1)S(1)}, bf16[256,512]{1,0:T(8,128)(2,1)S(1)}, u32[]{:S(2)}, u32[]{:S(2)}) %collective-permute-start.21) | collective-permute-done | bytes 262176 | tf_op jit(solution)/shard_map/ppermute | solution.py:405
  65.7 0.4 out_project.5
  66.1 2.8 %collective-permute-start.23 = (bf16[256,512]{1,0:T(8,128)(2,1)S(1)}, bf16[256,512]{1,0:T(8,128)(2,1)S(1)}, u32[]{:S(2)}, u32[]{:S(2)}) collective-permute-start(bf16[256,512]{1,0:T(8,128)(2,1)S(1)} %out_project.5), channel_id=1, source_target_pairs={{0,4},{1,5},{2,6},{3,7},{4,0},{5,1},{6,2},{7,3},{8,12},{9,13},{10,... | collective-permute-start | bytes 786440 | tf_op jit(solution)/shard_map/ppermute | solution.py:408
  69.0 0.7 out_project.4
  69.7 0.8 collective-permute-start.22
  70.5 0.7 collective-permute-start.24
  71.2 0.4 out_project.3.mine
  71.6 3.6 %collective-permute-done.23.b = bf16[256,512]{1,0:T(8,128)(2,1)S(1)} collective-permute-done((bf16[256,512]{1,0:T(8,128)(2,1)S(1)}, bf16[256,512]{1,0:T(8,128)(2,1)S(1)}, u32[]{:S(2)}, u32[]{:S(2)}) %collective-permute-start.23) | collective-permute-done | bytes 262176 | tf_op jit(solution)/shard_map/ppermute | solution.py:408
  75.2 5.5 %collective-permute-done.22.a = bf16[256,512]{1,0:T(8,128)(2,1)S(1)} collective-permute-done((bf16[256,512]{1,0:T(8,128)(2,1)S(1)}, bf16[256,512]{1,0:T(8,128)(2,1)S(1)}, u32[]{:S(2)}, u32[]{:S(2)}) %collective-permute-start.22) | collective-permute-done | bytes 262176 | tf_op jit(solution)/shard_map/ppermute | solution.py:408
  80.8 0.9 %collective-permute-done.24.c = bf16[256,512]{1,0:T(8,128)(2,1)S(1)} collective-permute-done((bf16[256,512]{1,0:T(8,128)(2,1)S(1)}, bf16[256,512]{1,0:T(8,128)(2,1)S(1)}, u32[]{:S(2)}, u32[]{:S(2)}) %collective-permute-start.24) | collective-permute-done | bytes 262176 | tf_op jit(solution)/shard_map/ppermute | solution.py:408
  81.6 0.8 add_up.1
  (25 shorter events, 0.2 us)
Async XLA Ops:
  0.0 17.4 %collective-permute-start = (bf16[256,512]{1,0:T(8,128)(2,1)}, bf16[256,512]{1,0:T(8,128)(2,1)S(1)}, u32[]{:S(2)}, u32[]{:S(2)}) collective-permute-start(bf16[256,512]{1,0:T(8,128)(2,1)} %refs_0_.3), channel_id=1, source_target_pairs={{0,4},{1,5},{2,6},{3,7},{4,0},{5,1},{6,2},{7,3},{8,12},{9,13},{10,... | collective-permute-start | bytes 786440 | tf_op jit(solution)/shard_map/ppermute | solution.py:408
  3.6 8.9 %collective-permute-start.4 = (bf16[256,512]{1,0:T(8,128)(2,1)}, bf16[256,512]{1,0:T(8,128)(2,1)S(1)}, u32[]{:S(2)}, u32[]{:S(2)}) collective-permute-start(bf16[256,512]{1,0:T(8,128)(2,1)} %refs_0_.3), channel_id=1, source_target_pairs={{0,1},{1,0},{2,3},{3,2},{4,5},{5,4},{6,7},{7,6},{8,9},{9,8},{10,11... | collective-permute-start | bytes 786440 | tf_op jit(solution)/shard_map/ppermute | solution.py:405
  4.5 11.4 %collective-permute-start.3 = (bf16[256,512]{1,0:T(8,128)(2,1)}, bf16[256,512]{1,0:T(8,128)(2,1)S(1)}, u32[]{:S(2)}, u32[]{:S(2)}) collective-permute-start(bf16[256,512]{1,0:T(8,128)(2,1)} %refs_0_.3), channel_id=1, source_target_pairs={{0,6},{1,3},{2,0},{3,5},{4,2},{5,7},{6,4},{7,1},{8,14},{9,11},{10,... | collective-permute-start | bytes 786440 | tf_op jit(solution)/shard_map/ppermute | solution.py:408
  4.8 12.2 %collective-permute-start.2 = (bf16[256,512]{1,0:T(8,128)(2,1)}, bf16[256,512]{1,0:T(8,128)(2,1)S(1)}, u32[]{:S(2)}, u32[]{:S(2)}) collective-permute-start(bf16[256,512]{1,0:T(8,128)(2,1)} %refs_0_.3), channel_id=1, source_target_pairs={{0,2},{1,7},{2,4},{3,1},{4,6},{5,3},{6,0},{7,5},{8,10},{9,15},{10,... | collective-permute-start | bytes 786440 | tf_op jit(solution)/shard_map/ppermute | solution.py:408
  8.9 3.6 %copy-start = (bf16[256,512]{1,0:T(8,128)(2,1)S(1)}, bf16[256,512]{1,0:T(8,128)(2,1)}, u32[]{:S(2)}) copy-start(bf16[256,512]{1,0:T(8,128)(2,1)} %refs_0_.3) | copy-start | bytes 786436
  15.9 2.2 %collective-permute-start.6 = (bf16[256,512]{1,0:T(8,128)(2,1)S(1)}, bf16[256,512]{1,0:T(8,128)(2,1)S(1)}, u32[]{:S(2)}, u32[]{:S(2)}) collective-permute-start(bf16[256,512]{1,0:T(8,128)(2,1)S(1)} %collective-permute-done.3.refs_1_), channel_id=1, source_target_pairs={{0,1},{1,0},{2,3},{3,2},{4,5},{5,4},{6,7},{7,6},{8,9},{9,8},{10,11... | collective-permute-start | bytes 786440 | tf_op jit(solution)/shard_map/ppermute | solution.py:405
  17.0 1.5 %collective-permute-start.5 = (bf16[256,512]{1,0:T(8,128)(2,1)S(1)}, bf16[256,512]{1,0:T(8,128)(2,1)S(1)}, u32[]{:S(2)}, u32[]{:S(2)}) collective-permute-start(bf16[256,512]{1,0:T(8,128)(2,1)S(1)} %collective-permute-done.2.refs_0_), channel_id=1, source_target_pairs={{0,1},{1,0},{2,3},{3,2},{4,5},{5,4},{6,7},{7,6},{8,9},{9,8},{10,11... | collective-permute-start | bytes 786440 | tf_op jit(solution)/shard_map/ppermute | solution.py:405
  17.4 2.2 %copy-start.1 = (f32[128]{0:T(128)S(1)}, f32[128]{0:T(128)}, u32[]{:S(2)}) copy-start(f32[128]{0:T(128)} %param.12) | copy-start | bytes 1540
  17.4 2.2 %copy-start.2 = (f32[128]{0:T(128)S(1)}, f32[128]{0:T(128)}, u32[]{:S(2)}) copy-start(f32[128]{0:T(128)} %param.13) | copy-start | bytes 1540
  17.4 2.1 %collective-permute-start.1 = (bf16[256,512]{1,0:T(8,128)(2,1)S(1)}, bf16[256,512]{1,0:T(8,128)(2,1)S(1)}, u32[]{:S(2)}, u32[]{:S(2)}) collective-permute-start(bf16[256,512]{1,0:T(8,128)(2,1)S(1)} %collective-permute-done.refs_0_), channel_id=1, source_target_pairs={{0,1},{1,0},{2,3},{3,2},{4,5},{5,4},{6,7},{7,6},{8,9},{9,8},{10,11... | collective-permute-start | bytes 786440 | tf_op jit(solution)/shard_map/ppermute | solution.py:405
  20.6 9.2 %collective-permute-start.7 = (bf16[256,256]{1,0:T(8,128)(2,1)S(1)}, bf16[256,256]{1,0:T(8,128)(2,1)S(1)}, u32[]{:S(2)}, u32[]{:S(2)}) collective-permute-start(bf16[256,256]{1,0:T(8,128)(2,1)S(1)} %get-tuple-element.59.refs_3_.own), channel_id=1, source_target_pairs={{0,32},{8,40},{16,48},{24,56},{32,64},{40,72},{48,80},{56,88},{64,... | collective-permute-start | bytes 393224 | tf_op jit(solution)/shard_map/ppermute | solution.py:421
  29.8 5.3 %collective-permute-start.8 = (bf16[256,256]{1,0:T(8,128)(2,1)S(1)}, bf16[256,256]{1,0:T(8,128)(2,1)S(1)}, u32[]{:S(2)}, u32[]{:S(2)}) collective-permute-start(bf16[256,256]{1,0:T(8,128)(2,1)S(1)} %collective-permute-done.7.refs_0_.refs_3_), channel_id=1, source_target_pairs={{0,32},{8,40},{16,48},{24,56},{32,64},{40,72},{48,80},{56,88},{64,... | collective-permute-start | bytes 393224 | tf_op jit(solution)/shard_map/ppermute | solution.py:421
  29.8 13.1 %collective-permute-start.13 = (bf16[4,512,512]{2,1,0:T(8,128)(2,1)}, bf16[4,512,512]{2,1,0:T(8,128)(2,1)}, u32[]{:S(2)}, u32[]{:S(2)}) collective-permute-start(bf16[4,512,512]{2,1,0:T(8,128)(2,1)} %get-tuple-element.66), channel_id=1, source_target_pairs={{0,1},{1,0},{2,3},{3,2},{4,5},{5,4},{6,7},{7,6},{8,9},{9,8},{10,11... | collective-permute-start | bytes 6291464 | tf_op jit(solution)/shard_map/ppermute | solution.py:405
  32.0 6.0 %collective-permute-start.19 = (bf16[256,256]{1,0:T(8,128)(2,1)S(1)}, bf16[256,256]{1,0:T(8,128)(2,1)S(1)}, u32[]{:S(2)}, u32[]{:S(2)}) collective-permute-start(bf16[256,256]{1,0:T(8,128)(2,1)S(1)} %collective-permute-done.7.refs_0_.refs_3_), channel_id=1, source_target_pairs={{0,8},{1,25},{2,10},{3,27},{4,12},{5,29},{6,14},{7,31},{8,0},{9,17... | collective-permute-start | bytes 393224 | tf_op jit(solution)/shard_map/ppermute | solution.py:430
  35.2 5.0 %collective-permute-start.9 = (bf16[256,256]{1,0:T(8,128)(2,1)S(1)}, bf16[256,256]{1,0:T(8,128)(2,1)S(1)}, u32[]{:S(2)}, u32[]{:S(2)}) collective-permute-start(bf16[256,256]{1,0:T(8,128)(2,1)S(1)} %collective-permute-done.8.refs_0_.refs_4_), channel_id=1, source_target_pairs={{0,32},{8,40},{16,48},{24,56},{32,64},{40,72},{48,80},{56,88},{64,... | collective-permute-start | bytes 393224 | tf_op jit(solution)/shard_map/ppermute | solution.py:421
  35.2 7.8 %collective-permute-start.12 = (bf16[256,256]{1,0:T(8,128)(2,1)S(1)}, bf16[256,256]{1,0:T(8,128)(2,1)S(1)}, u32[]{:S(2)}, u32[]{:S(2)}) collective-permute-start(bf16[256,256]{1,0:T(8,128)(2,1)S(1)} %collective-permute-done.8.refs_0_.refs_4_), channel_id=1, source_target_pairs={{0,8},{1,25},{2,10},{3,27},{4,12},{5,29},{6,14},{7,31},{8,0},{9,17... | collective-permute-start | bytes 393224 | tf_op jit(solution)/shard_map/ppermute | solution.py:430
  38.5 11.2 %collective-permute-start.20 = (bf16[512,256]{1,0:T(8,128)(2,1)S(1)}, bf16[512,256]{1,0:T(8,128)(2,1)S(1)}, u32[]{:S(2)}, u32[]{:S(2)}) collective-permute-start(bf16[512,256]{1,0:T(8,128)(2,1)S(1)} %get-tuple-element.75), channel_id=1, source_target_pairs={{0,24},{1,9},{2,26},{3,11},{4,28},{5,13},{6,30},{7,15},{8,16},{9,1... | collective-permute-start | bytes 786440 | tf_op jit(solution)/shard_map/ppermute | solution.py:430
  40.2 5.6 %collective-permute-start.11 = (bf16[256,256]{1,0:T(8,128)(2,1)S(1)}, bf16[256,256]{1,0:T(8,128)(2,1)S(1)}, u32[]{:S(2)}, u32[]{:S(2)}) collective-permute-start(bf16[256,256]{1,0:T(8,128)(2,1)S(1)} %collective-permute-done.9.refs_0_.refs_8_), channel_id=1, source_target_pairs={{0,32},{8,40},{16,48},{24,56},{32,64},{40,72},{48,80},{56,88},{64,... | collective-permute-start | bytes 393224 | tf_op jit(solution)/shard_map/ppermute | solution.py:421
  40.2 8.4 %collective-permute-start.10 = (bf16[256,256]{1,0:T(8,128)(2,1)S(1)}, bf16[256,256]{1,0:T(8,128)(2,1)S(1)}, u32[]{:S(2)}, u32[]{:S(2)}) collective-permute-start(bf16[256,256]{1,0:T(8,128)(2,1)S(1)} %collective-permute-done.9.refs_0_.refs_8_), channel_id=1, source_target_pairs={{0,8},{1,25},{2,10},{3,27},{4,12},{5,29},{6,14},{7,31},{8,0},{9,17... | collective-permute-start | bytes 393224 | tf_op jit(solution)/shard_map/ppermute | solution.py:430
  43.0 8.8 %collective-permute-start.18 = (bf16[512,256]{1,0:T(8,128)(2,1)S(1)}, bf16[512,256]{1,0:T(8,128)(2,1)S(1)}, u32[]{:S(2)}, u32[]{:S(2)}) collective-permute-start(bf16[512,256]{1,0:T(8,128)(2,1)S(1)} %get-tuple-element.73), channel_id=1, source_target_pairs={{0,24},{1,9},{2,26},{3,11},{4,28},{5,13},{6,30},{7,15},{8,16},{9,1... | collective-permute-start | bytes 786440 | tf_op jit(solution)/shard_map/ppermute | solution.py:430
  45.8 8.3 %collective-permute-start.15 = (bf16[256,256]{1,0:T(8,128)(2,1)S(1)}, bf16[256,256]{1,0:T(8,128)(2,1)S(1)}, u32[]{:S(2)}, u32[]{:S(2)}) collective-permute-start(bf16[256,256]{1,0:T(8,128)(2,1)S(1)} %get-tuple-element.70), channel_id=1, source_target_pairs={{0,8},{8,16},{16,24},{24,0},{32,40},{40,48},{48,56},{56,32},{64,72... | collective-permute-start | bytes 393224 | tf_op jit(solution)/shard_map/ppermute | solution.py:418
  46.7 7.5 %collective-permute-start.16 = (bf16[256,256]{1,0:T(8,128)(2,1)S(1)}, bf16[256,256]{1,0:T(8,128)(2,1)S(1)}, u32[]{:S(2)}, u32[]{:S(2)}) collective-permute-start(bf16[256,256]{1,0:T(8,128)(2,1)S(1)} %get-tuple-element.71), channel_id=1, source_target_pairs={{0,24},{8,0},{16,8},{24,16},{32,56},{40,32},{48,40},{56,48},{64,88... | collective-permute-start | bytes 393224 | tf_op jit(solution)/shard_map/ppermute | solution.py:418
  48.6 5.6 %collective-permute-start.17 = (bf16[256,256]{1,0:T(8,128)(2,1)S(1)}, bf16[256,256]{1,0:T(8,128)(2,1)S(1)}, u32[]{:S(2)}, u32[]{:S(2)}) collective-permute-start(bf16[256,256]{1,0:T(8,128)(2,1)S(1)} %get-tuple-element.72), channel_id=1, source_target_pairs={{0,16},{8,24},{16,0},{24,8},{32,48},{40,56},{48,32},{56,40},{64,80... | collective-permute-start | bytes 393224 | tf_op jit(solution)/shard_map/ppermute | solution.py:418
  49.8 7.5 %collective-permute-start.14 = (bf16[512,256]{1,0:T(8,128)(2,1)S(1)}, bf16[512,256]{1,0:T(8,128)(2,1)S(1)}, u32[]{:S(2)}, u32[]{:S(2)}) collective-permute-start(bf16[512,256]{1,0:T(8,128)(2,1)S(1)} %get-tuple-element.69), channel_id=1, source_target_pairs={{0,24},{1,9},{2,26},{3,11},{4,28},{5,13},{6,30},{7,15},{8,16},{9,1... | collective-permute-start | bytes 786440 | tf_op jit(solution)/shard_map/ppermute | solution.py:430
  58.8 6.9 %collective-permute-start.21 = (bf16[256,512]{1,0:T(8,128)(2,1)S(1)}, bf16[256,512]{1,0:T(8,128)(2,1)S(1)}, u32[]{:S(2)}, u32[]{:S(2)}) collective-permute-start(bf16[256,512]{1,0:T(8,128)(2,1)S(1)} %get-tuple-element.82.a_ref), channel_id=1, source_target_pairs={{0,1},{1,0},{2,3},{3,2},{4,5},{5,4},{6,7},{7,6},{8,9},{9,8},{10,11... | collective-permute-start | bytes 786440 | tf_op jit(solution)/shard_map/ppermute | solution.py:405
  66.1 9.1 %collective-permute-start.23 = (bf16[256,512]{1,0:T(8,128)(2,1)S(1)}, bf16[256,512]{1,0:T(8,128)(2,1)S(1)}, u32[]{:S(2)}, u32[]{:S(2)}) collective-permute-start(bf16[256,512]{1,0:T(8,128)(2,1)S(1)} %out_project.5), channel_id=1, source_target_pairs={{0,4},{1,5},{2,6},{3,7},{4,0},{5,1},{6,2},{7,3},{8,12},{9,13},{10,... | collective-permute-start | bytes 786440 | tf_op jit(solution)/shard_map/ppermute | solution.py:408
  69.7 11.1 %collective-permute-start.22 = (bf16[256,512]{1,0:T(8,128)(2,1)S(1)}, bf16[256,512]{1,0:T(8,128)(2,1)S(1)}, u32[]{:S(2)}, u32[]{:S(2)}) collective-permute-start(bf16[256,512]{1,0:T(8,128)(2,1)S(1)} %get-tuple-element.85), channel_id=1, source_target_pairs={{0,2},{1,7},{2,4},{3,1},{4,6},{5,3},{6,0},{7,5},{8,10},{9,15},{10,... | collective-permute-start | bytes 786440 | tf_op jit(solution)/shard_map/ppermute | solution.py:408
  70.5 11.2 %collective-permute-start.24 = (bf16[256,512]{1,0:T(8,128)(2,1)S(1)}, bf16[256,512]{1,0:T(8,128)(2,1)S(1)}, u32[]{:S(2)}, u32[]{:S(2)}) collective-permute-start(bf16[256,512]{1,0:T(8,128)(2,1)S(1)} %get-tuple-element.86), channel_id=1, source_target_pairs={{0,6},{1,3},{2,0},{3,5},{4,2},{5,7},{6,4},{7,1},{8,14},{9,11},{10,... | collective-permute-start | bytes 786440 | tf_op jit(solution)/shard_map/ppermute | solution.py:408

commit v5 on v4

--- a/solution.py
+++ b/solution.py
@@ -279,6 +279,8 @@
     tok = start_ref.shape[0]
     heads = rows // tok
     scale = math.log2(math.e) / math.sqrt(head)
+    if not final:
+        acc = out
     acc[...] = jnp.zeros_like(acc) if first else acc_in[...]
     place = Place()
     own = place.seq * tok
@@ -313,8 +315,6 @@
         for h in range(heads):
             part = slice(h * tok, (h + 1) * tok)
             out[:, h * head : (h + 1) * head] = (acc[part, :head] / acc[part, head:]).astype(BF)
-    else:
-        out[...] = acc[...]
 
 
 def attend(start, queries, start_col, index_col, pieces, acc=None, final=False, flags=()):

time: 82.6 us -> 82.6 us (level)
  no operation moved by 1% of the time
where the time goes in v5:
time: 82.6 us; the launch traced here: 82.4 us
  starting transfers between devices  34.7 us (42%)
  waiting for transfers between devices  26.7 us (32%)
  Pallas kernels  18.3 us (22%)
  other arithmetic  1.6 us (2%)
  local copies, waits for them, and re-layouts  0.88 us (1%)
    ppermute x6, waiting for transfers between devices, along_x(): lax.ppermute(a, 'tp', [(i, (i // 2 + (d if i % 2 == 0 else -d)) % nx * 2...  12.9 us
    ppermute x6, starting transfers between devices, along_x(): lax.ppermute(a, 'tp', [(i, (i // 2 + (d if i % 2 == 0 else -d)) % nx * 2...  10.6 us
    ppermute x6, starting transfers between devices, sibling(): return lax.ppermute(a, 'tp', [(i, i ^ 1) for i in range(tps)])  9.25 us
    ppermute x6, starting transfers between devices, swap_y(): return lax.ppermute(a, ('seq', 'tp'), pairs)  9.16 us
    ppermute x4, waiting for transfers between devices, along_z(): lax.ppermute(a, 'seq', [(i, (i // ny + d) % nz * ny + i % ny) for i in ra...  8.65 us
    pallas_call x2, Pallas kernels, stage(): pl.pallas_call(functools.partial(stage_kernel, plan, len(arrays)), in_spe...  6.61 us
    pallas_call x4, Pallas kernels, attend(): pl.pallas_call(functools.partial(attend_kernel, layout, first, final, len...  4.45 us
    ppermute x3, starting transfers between devices, along_y(): lax.ppermute(a, 'seq', [(i, i // ny * ny + (i + d) % ny) for i in range(s...  3.92 us
  transfers between devices with their start and end apart: 25, of which 12 were waited for; matrix products, arithmetic and copies ran while one was open for 3% of the time, Pallas kernels for 18%

profile of v5, /device:TPU:1, one launch (start us, length us, event | category | flops | bytes accessed | tf_op | source)
XLA Modules:
  0.0 82.4 jit_solution(8416934707660213510)
XLA Ops:
  0.0 3.6 %collective-permute-start = (bf16[256,512]{1,0:T(8,128)(2,1)}, bf16[256,512]{1,0:T(8,128)(2,1)S(1)}, u32[]{:S(2)}, u32[]{:S(2)}) collective-permute-start(bf16[256,512]{1,0:T(8,128)(2,1)} %refs_0_.3), channel_id=1, source_target_pairs={{0,4},{1,5},{2,6},{3,7},{4,0},{5,1},{6,2},{7,3},{8,12},{9,13},{10,... | collective-permute-start | bytes 786440 | tf_op jit(solution)/shard_map/ppermute | solution.py:408
  3.6 1.0 %collective-permute-start.4 = (bf16[256,512]{1,0:T(8,128)(2,1)}, bf16[256,512]{1,0:T(8,128)(2,1)S(1)}, u32[]{:S(2)}, u32[]{:S(2)}) collective-permute-start(bf16[256,512]{1,0:T(8,128)(2,1)} %refs_0_.3), channel_id=1, source_target_pairs={{0,1},{1,0},{2,3},{3,2},{4,5},{5,4},{6,7},{7,6},{8,9},{9,8},{10,11... | collective-permute-start | bytes 786440 | tf_op jit(solution)/shard_map/ppermute | solution.py:405
  4.5 0.3 collective-permute-start.3
  4.8 2.4 %collective-permute-start.2 = (bf16[256,512]{1,0:T(8,128)(2,1)}, bf16[256,512]{1,0:T(8,128)(2,1)S(1)}, u32[]{:S(2)}, u32[]{:S(2)}) collective-permute-start(bf16[256,512]{1,0:T(8,128)(2,1)} %refs_0_.3), channel_id=1, source_target_pairs={{0,2},{1,7},{2,4},{3,1},{4,6},{5,3},{6,0},{7,5},{8,10},{9,15},{10,... | collective-permute-start | bytes 786440 | tf_op jit(solution)/shard_map/ppermute | solution.py:408
  7.2 0.7 copy.15
  8.0 0.1 reduce
  8.1 0.7 select_reduce_fusion.start_s
  8.9 3.0 %stage_in.1 = (bf16[8,512,768]{2,1,0:T(8,128)(2,1)S(1)}, f32[8,128]{1,0:T(8,128)S(1)}) custom-call(bf16[4096,512]{1,0:T(8,128)(2,1)} %refs_0_.2, bf16[4096,128]{1,0:T(8,128)(2,1)} %refs_1_.1, bf16[4096,128]{1,0:T(8,128)(2,1)} %refs_2_.1), custom_call_target="tpu_custom_call" | custom-call | bytes 12582912 | tf_op jit(solution)/shard_map/stage_in/pallas_call | solution.py:114
  11.9 0.5 fusion
  12.4 0.0 collective-permute-done.4.refs_1_
  12.5 0.6 project.3.refs_5_
  13.0 2.9 %collective-permute-done.3.refs_1_ = bf16[256,512]{1,0:T(8,128)(2,1)S(1)} collective-permute-done((bf16[256,512]{1,0:T(8,128)(2,1)}, bf16[256,512]{1,0:T(8,128)(2,1)S(1)}, u32[]{:S(2)}, u32[]{:S(2)}) %collective-permute-start.3) | collective-permute-done | bytes 262176 | tf_op jit(solution)/shard_map/ppermute | solution.py:408
  15.9 1.1 %collective-permute-start.6 = (bf16[256,512]{1,0:T(8,128)(2,1)S(1)}, bf16[256,512]{1,0:T(8,128)(2,1)S(1)}, u32[]{:S(2)}, u32[]{:S(2)}) collective-permute-start(bf16[256,512]{1,0:T(8,128)(2,1)S(1)} %collective-permute-done.3.refs_1_), channel_id=1, source_target_pairs={{0,1},{1,0},{2,3},{3,2},{4,5},{5,4},{6,7},{7,6},{8,9},{9,8},{10,11... | collective-permute-start | bytes 786440 | tf_op jit(solution)/shard_map/ppermute | solution.py:405
  17.0 0.2 collective-permute-start.5
  17.2 0.1 pad_maximum_fusion
  17.4 0.0 collective-permute-done.refs_0_
  17.4 0.0 copy-start.1
  17.4 0.0 copy-start.2
  17.4 0.4 collective-permute-start.1
  17.8 0.4 collective-permute-done.6.refs_3_
  18.2 0.4 collective-permute-done.5.refs_2_
  18.6 1.0 %project.4.refs_3_ = f32[256,768]{1,0:T(8,128)S(1)} custom-call(bf16[256,512]{1,0:T(8,128)(2,1)S(1)} %collective-permute-done.2.refs_0_, bf16[256,512]{1,0:T(8,128)(2,1)S(1)} %collective-permute-done.3.refs_1_, bf16[256,512]{1,0:T(8,128)(2,1)S(1)} %collective-permute-done.5.refs_2_, bf16[256,512]{1,0:T(8,128)(2,1)S(1)} %collective-permute-done.6.refs_3_, ...), custom_call_target="tpu_custom_call" | custom-call | flops 1610612736 | bytes 3145728 | tf_op jit(solution)/shard_map/project/pallas_call | solution.py:250
  19.5 0.0 collective-permute-done.1.refs_1_
  19.6 1.0 %project.5 = (bf16[1024,128]{1,0:T(8,128)(2,1)S(1)}, bf16[256,256]{1,0:T(8,128)(2,1)S(1)}) custom-call(bf16[256,512]{1,0:T(8,128)(2,1)S(1)} %collective-permute-done.refs_0_, bf16[256,512]{1,0:T(8,128)(2,1)S(1)} %collective-permute-done.1.refs_1_, bf16[8,512,768]{2,1,0:T(8,128)(2,1)S(1)} %get-tuple-element.47.refs_2_.refs_4_, ...), custom_call_target="tpu_custom_call" | custom-call | flops 805306368 | bytes 1572864 | tf_op jit(solution)/shard_map/project/pallas_call | solution.py:250
  20.6 1.7 %collective-permute-start.7 = (bf16[256,256]{1,0:T(8,128)(2,1)S(1)}, bf16[256,256]{1,0:T(8,128)(2,1)S(1)}, u32[]{:S(2)}, u32[]{:S(2)}) collective-permute-start(bf16[256,256]{1,0:T(8,128)(2,1)S(1)} %get-tuple-element.59.refs_3_.own), channel_id=1, source_target_pairs={{0,32},{8,40},{16,48},{24,56},{32,64},{40,72},{48,80},{56,88},{64,... | collective-permute-start | bytes 393224 | tf_op jit(solution)/shard_map/ppermute | solution.py:421
  22.3 3.6 %stage_out.1 = (bf16[4,512,512]{2,1,0:T(8,128)(2,1)S(1)}, bf16[4,512,512]{2,1,0:T(8,128)(2,1)}, f32[8,128]{1,0:T(8,128)S(1)}) custom-call(bf16[512,4096]{1,0:T(8,128)(2,1)} %refs_0_.4), custom_call_target="tpu_custom_call" | custom-call | bytes 8388608 | tf_op jit(solution)/shard_map/stage_out/pallas_call | solution.py:114
  25.9 3.9 %collective-permute-done.7.refs_0_.refs_3_ = bf16[256,256]{1,0:T(8,128)(2,1)S(1)} collective-permute-done((bf16[256,256]{1,0:T(8,128)(2,1)S(1)}, bf16[256,256]{1,0:T(8,128)(2,1)S(1)}, u32[]{:S(2)}, u32[]{:S(2)}) %collective-permute-start.7) | collective-permute-done | bytes 131104 | tf_op jit(solution)/shard_map/ppermute | solution.py:421
  29.8 0.0 collective-permute-start.8
  29.8 0.9 %collective-permute-start.13 = (bf16[4,512,512]{2,1,0:T(8,128)(2,1)}, bf16[4,512,512]{2,1,0:T(8,128)(2,1)}, u32[]{:S(2)}, u32[]{:S(2)}) collective-permute-start(bf16[4,512,512]{2,1,0:T(8,128)(2,1)} %get-tuple-element.66), channel_id=1, source_target_pairs={{0,1},{1,0},{2,3},{3,2},{4,5},{5,4},{6,7},{7,6},{8,9},{9,8},{10,11... | collective-permute-start | bytes 6291464 | tf_op jit(solution)/shard_map/ppermute | solution.py:405
  30.7 0.1 copy.19.refs_1_
  30.9 1.1 %attend.4 = (f32[1024,256]{1,0:T(8,128)S(1)}, f32[8,128]{1,0:T(8,128)S(1)}) custom-call(s32[256]{0:T(256)S(1)} %select_reduce_fusion.start_s, bf16[1024,128]{1,0:T(8,128)(2,1)S(1)} %get-tuple-element.55.refs_0_, s32[256,1]{1,0:T(8,128)S(1)} %copy.19.refs_1_, s32[256,1]{1,0:T(8,128)S(1)} %iota_add_fusion.refs_2_, ...), custom_call_target="tpu_custom_call" | custom-call | flops 268435456 | bytes 2097152 | tf_op jit(solution)/shard_map/attend/pallas_call | solution.py:333
  32.0 2.8 %collective-permute-start.19 = (bf16[256,256]{1,0:T(8,128)(2,1)S(1)}, bf16[256,256]{1,0:T(8,128)(2,1)S(1)}, u32[]{:S(2)}, u32[]{:S(2)}) collective-permute-start(bf16[256,256]{1,0:T(8,128)(2,1)S(1)} %collective-permute-done.7.refs_0_.refs_3_), channel_id=1, source_target_pairs={{0,8},{1,25},{2,10},{3,27},{4,12},{5,29},{6,14},{7,31},{8,0},{9,17... | collective-permute-start | bytes 393224 | tf_op jit(solution)/shard_map/ppermute | solution.py:430
  34.8 0.4 collective-permute-done.8.refs_0_.refs_4_
  35.2 2.7 %collective-permute-start.12 = (bf16[256,256]{1,0:T(8,128)(2,1)S(1)}, bf16[256,256]{1,0:T(8,128)(2,1)S(1)}, u32[]{:S(2)}, u32[]{:S(2)}) collective-permute-start(bf16[256,256]{1,0:T(8,128)(2,1)S(1)} %collective-permute-done.8.refs_0_.refs_4_), channel_id=1, source_target_pairs={{0,8},{1,25},{2,10},{3,27},{4,12},{5,29},{6,14},{7,31},{8,0},{9,17... | collective-permute-start | bytes 393224 | tf_op jit(solution)/shard_map/ppermute | solution.py:430
  37.9 0.0 collective-permute-done.19.refs_1_.refs_5_
  37.9 0.6 pack.5
  38.5 0.0 collective-permute-start.20
  38.5 1.7 %collective-permute-done.9.refs_0_.refs_8_ = bf16[256,256]{1,0:T(8,128)(2,1)S(1)} collective-permute-done((bf16[256,256]{1,0:T(8,128)(2,1)S(1)}, bf16[256,256]{1,0:T(8,128)(2,1)S(1)}, u32[]{:S(2)}, u32[]{:S(2)}) %collective-permute-start.9) | collective-permute-done | bytes 131104 | tf_op jit(solution)/shard_map/ppermute | solution.py:421
  40.2 0.0 collective-permute-start.11
  40.2 2.7 %collective-permute-start.10 = (bf16[256,256]{1,0:T(8,128)(2,1)S(1)}, bf16[256,256]{1,0:T(8,128)(2,1)S(1)}, u32[]{:S(2)}, u32[]{:S(2)}) collective-permute-start(bf16[256,256]{1,0:T(8,128)(2,1)S(1)} %collective-permute-done.9.refs_0_.refs_8_), channel_id=1, source_target_pairs={{0,8},{1,25},{2,10},{3,27},{4,12},{5,29},{6,14},{7,31},{8,0},{9,17... | collective-permute-start | bytes 393224 | tf_op jit(solution)/shard_map/ppermute | solution.py:430
  42.9 0.0 collective-permute-done.12.refs_1_.refs_6_
  43.0 0.1 collective-permute-start.18
  43.1 2.7 %collective-permute-done.11.refs_0_.far.refs_5_ = bf16[256,256]{1,0:T(8,128)(2,1)S(1)} collective-permute-done((bf16[256,256]{1,0:T(8,128)(2,1)S(1)}, bf16[256,256]{1,0:T(8,128)(2,1)S(1)}, u32[]{:S(2)}, u32[]{:S(2)}) %collective-permute-start.11) | collective-permute-done | bytes 131104 | tf_op jit(solution)/shard_map/ppermute | solution.py:421
  45.8 0.8 %collective-permute-start.15 = (bf16[256,256]{1,0:T(8,128)(2,1)S(1)}, bf16[256,256]{1,0:T(8,128)(2,1)S(1)}, u32[]{:S(2)}, u32[]{:S(2)}) collective-permute-start(bf16[256,256]{1,0:T(8,128)(2,1)S(1)} %get-tuple-element.70), channel_id=1, source_target_pairs={{0,8},{8,16},{16,24},{24,0},{32,40},{40,48},{48,56},{56,32},{64,72... | collective-permute-start | bytes 393224 | tf_op jit(solution)/shard_map/ppermute | solution.py:418
  46.7 1.9 %collective-permute-start.16 = (bf16[256,256]{1,0:T(8,128)(2,1)S(1)}, bf16[256,256]{1,0:T(8,128)(2,1)S(1)}, u32[]{:S(2)}, u32[]{:S(2)}) collective-permute-start(bf16[256,256]{1,0:T(8,128)(2,1)S(1)} %get-tuple-element.71), channel_id=1, source_target_pairs={{0,24},{8,0},{16,8},{24,16},{32,56},{40,32},{48,40},{56,48},{64,88... | collective-permute-start | bytes 393224 | tf_op jit(solution)/shard_map/ppermute | solution.py:418
  48.6 1.2 %collective-permute-start.17 = (bf16[256,256]{1,0:T(8,128)(2,1)S(1)}, bf16[256,256]{1,0:T(8,128)(2,1)S(1)}, u32[]{:S(2)}, u32[]{:S(2)}) collective-permute-start(bf16[256,256]{1,0:T(8,128)(2,1)S(1)} %get-tuple-element.72), channel_id=1, source_target_pairs={{0,16},{8,24},{16,0},{24,8},{32,48},{40,56},{48,32},{56,40},{64,80... | collective-permute-start | bytes 393224 | tf_op jit(solution)/shard_map/ppermute | solution.py:418
  49.8 0.8 collective-permute-start.14
  50.5 1.3 %attend.5 = (f32[1024,256]{1,0:T(8,128)S(1)}, f32[8,128]{1,0:T(8,128)}) custom-call(s32[256]{0:T(256)S(1)} %select_reduce_fusion.start_s, bf16[1024,128]{1,0:T(8,128)(2,1)S(1)} %get-tuple-element.55.refs_0_, s32[256,1]{1,0:T(8,128)S(1)} %copy.19.refs_1_, s32[256,1]{1,0:T(8,128)S(1)} %iota_add_fusion.refs_2_, ...), custom_call_target="tpu_custom_call" | custom-call | flops 1879048192 | bytes 2097152 | tf_op jit(solution)/shard_map/attend/pallas_call | solution.py:333
  51.8 0.6 attend.6
  52.4 1.6 %fetch.1 = (bf16[4,512,512]{2,1,0:T(8,128)(2,1)S(1)}, f32[8,128]{1,0:T(8,128)S(1)}) custom-call(bf16[4,512,512]{2,1,0:T(8,128)(2,1)} %collective-permute-done.13.refs_0_.src, f32[8,128]{1,0:T(8,128)S(1)} %get-tuple-element.80.refs_0_.refs_3_), custom_call_target="tpu_custom_call" | custom-call | tf_op jit(solution)/shard_map/fetch/pallas_call | solution.py:101
  54.1 3.2 %collective-permute-done.14.refs_3_ = bf16[512,256]{1,0:T(8,128)(2,1)S(1)} collective-permute-done((bf16[512,256]{1,0:T(8,128)(2,1)S(1)}, bf16[512,256]{1,0:T(8,128)(2,1)S(1)}, u32[]{:S(2)}, u32[]{:S(2)}) %collective-permute-start.14) | collective-permute-done | bytes 262176 | tf_op jit(solution)/shard_map/ppermute | solution.py:430
  57.3 1.5 %attend.7 = (bf16[256,512]{1,0:T(8,128)(2,1)S(1)}, f32[8,128]{1,0:T(8,128)}) custom-call(s32[256]{0:T(256)S(1)} %select_reduce_fusion.start_s, bf16[1024,128]{1,0:T(8,128)(2,1)S(1)} %get-tuple-element.55.refs_0_, s32[256,1]{1,0:T(8,128)S(1)} %copy.19.refs_1_, s32[256,1]{1,0:T(8,128)S(1)} %iota_add_fusion.refs_2_, ...), custom_call_target="tpu_custom_call" | custom-call | flops 1342177280 | bytes 2097152 | tf_op jit(solution)/shard_map/attend/pallas_call | solution.py:333
  58.8 5.8 %collective-permute-start.21 = (bf16[256,512]{1,0:T(8,128)(2,1)S(1)}, bf16[256,512]{1,0:T(8,128)(2,1)S(1)}, u32[]{:S(2)}, u32[]{:S(2)}) collective-permute-start(bf16[256,512]{1,0:T(8,128)(2,1)S(1)} %get-tuple-element.82.a_ref), channel_id=1, source_target_pairs={{0,1},{1,0},{2,3},{3,2},{4,5},{5,4},{6,7},{7,6},{8,9},{9,8},{10,11... | collective-permute-start | bytes 786440 | tf_op jit(solution)/shard_map/ppermute | solution.py:405
  64.5 1.2 %collective-permute-done.21.b_ref = bf16[256,512]{1,0:T(8,128)(2,1)S(1)} collective-permute-done((bf16[256,512]{1,0:T(8,128)(2,1)S(1)}, bf16[256,512]{1,0:T(8,128)(2,1)S(1)}, u32[]{:S(2)}, u32[]{:S(2)}) %collective-permute-start.21) | collective-permute-done | bytes 262176 | tf_op jit(solution)/shard_map/ppermute | solution.py:405
  65.7 0.4 out_project.5
  66.1 2.8 %collective-permute-start.23 = (bf16[256,512]{1,0:T(8,128)(2,1)S(1)}, bf16[256,512]{1,0:T(8,128)(2,1)S(1)}, u32[]{:S(2)}, u32[]{:S(2)}) collective-permute-start(bf16[256,512]{1,0:T(8,128)(2,1)S(1)} %out_project.5), channel_id=1, source_target_pairs={{0,4},{1,5},{2,6},{3,7},{4,0},{5,1},{6,2},{7,3},{8,12},{9,13},{10,... | collective-permute-start | bytes 786440 | tf_op jit(solution)/shard_map/ppermute | solution.py:408
  69.0 0.7 out_project.4
  69.7 0.8 collective-permute-start.22
  70.5 0.7 collective-permute-start.24
  71.2 0.4 out_project.3.mine
  71.6 3.6 %collective-permute-done.23.b = bf16[256,512]{1,0:T(8,128)(2,1)S(1)} collective-permute-done((bf16[256,512]{1,0:T(8,128)(2,1)S(1)}, bf16[256,512]{1,0:T(8,128)(2,1)S(1)}, u32[]{:S(2)}, u32[]{:S(2)}) %collective-permute-start.23) | collective-permute-done | bytes 262176 | tf_op jit(solution)/shard_map/ppermute | solution.py:408
  75.2 5.5 %collective-permute-done.22.a = bf16[256,512]{1,0:T(8,128)(2,1)S(1)} collective-permute-done((bf16[256,512]{1,0:T(8,128)(2,1)S(1)}, bf16[256,512]{1,0:T(8,128)(2,1)S(1)}, u32[]{:S(2)}, u32[]{:S(2)}) %collective-permute-start.22) | collective-permute-done | bytes 262176 | tf_op jit(solution)/shard_map/ppermute | solution.py:408
  80.8 0.9 %collective-permute-done.24.c = bf16[256,512]{1,0:T(8,128)(2,1)S(1)} collective-permute-done((bf16[256,512]{1,0:T(8,128)(2,1)S(1)}, bf16[256,512]{1,0:T(8,128)(2,1)S(1)}, u32[]{:S(2)}, u32[]{:S(2)}) %collective-permute-start.24) | collective-permute-done | bytes 262176 | tf_op jit(solution)/shard_map/ppermute | solution.py:408
  81.6 0.8 add_up.1
  (25 shorter events, 0.2 us)
Async XLA Ops:
  0.0 17.4 %collective-permute-start = (bf16[256,512]{1,0:T(8,128)(2,1)}, bf16[256,512]{1,0:T(8,128)(2,1)S(1)}, u32[]{:S(2)}, u32[]{:S(2)}) collective-permute-start(bf16[256,512]{1,0:T(8,128)(2,1)} %refs_0_.3), channel_id=1, source_target_pairs={{0,4},{1,5},{2,6},{3,7},{4,0},{5,1},{6,2},{7,3},{8,12},{9,13},{10,... | collective-permute-start | bytes 786440 | tf_op jit(solution)/shard_map/ppermute | solution.py:408
  3.6 8.9 %collective-permute-start.4 = (bf16[256,512]{1,0:T(8,128)(2,1)}, bf16[256,512]{1,0:T(8,128)(2,1)S(1)}, u32[]{:S(2)}, u32[]{:S(2)}) collective-permute-start(bf16[256,512]{1,0:T(8,128)(2,1)} %refs_0_.3), channel_id=1, source_target_pairs={{0,1},{1,0},{2,3},{3,2},{4,5},{5,4},{6,7},{7,6},{8,9},{9,8},{10,11... | collective-permute-start | bytes 786440 | tf_op jit(solution)/shard_map/ppermute | solution.py:405
  4.5 11.4 %collective-permute-start.3 = (bf16[256,512]{1,0:T(8,128)(2,1)}, bf16[256,512]{1,0:T(8,128)(2,1)S(1)}, u32[]{:S(2)}, u32[]{:S(2)}) collective-permute-start(bf16[256,512]{1,0:T(8,128)(2,1)} %refs_0_.3), channel_id=1, source_target_pairs={{0,6},{1,3},{2,0},{3,5},{4,2},{5,7},{6,4},{7,1},{8,14},{9,11},{10,... | collective-permute-start | bytes 786440 | tf_op jit(solution)/shard_map/ppermute | solution.py:408
  4.8 12.2 %collective-permute-start.2 = (bf16[256,512]{1,0:T(8,128)(2,1)}, bf16[256,512]{1,0:T(8,128)(2,1)S(1)}, u32[]{:S(2)}, u32[]{:S(2)}) collective-permute-start(bf16[256,512]{1,0:T(8,128)(2,1)} %refs_0_.3), channel_id=1, source_target_pairs={{0,2},{1,7},{2,4},{3,1},{4,6},{5,3},{6,0},{7,5},{8,10},{9,15},{10,... | collective-permute-start | bytes 786440 | tf_op jit(solution)/shard_map/ppermute | solution.py:408
  8.9 3.6 %copy-start = (bf16[256,512]{1,0:T(8,128)(2,1)S(1)}, bf16[256,512]{1,0:T(8,128)(2,1)}, u32[]{:S(2)}) copy-start(bf16[256,512]{1,0:T(8,128)(2,1)} %refs_0_.3) | copy-start | bytes 786436
  15.9 2.2 %collective-permute-start.6 = (bf16[256,512]{1,0:T(8,128)(2,1)S(1)}, bf16[256,512]{1,0:T(8,128)(2,1)S(1)}, u32[]{:S(2)}, u32[]{:S(2)}) collective-permute-start(bf16[256,512]{1,0:T(8,128)(2,1)S(1)} %collective-permute-done.3.refs_1_), channel_id=1, source_target_pairs={{0,1},{1,0},{2,3},{3,2},{4,5},{5,4},{6,7},{7,6},{8,9},{9,8},{10,11... | collective-permute-start | bytes 786440 | tf_op jit(solution)/shard_map/ppermute | solution.py:405
  17.0 1.5 %collective-permute-start.5 = (bf16[256,512]{1,0:T(8,128)(2,1)S(1)}, bf16[256,512]{1,0:T(8,128)(2,1)S(1)}, u32[]{:S(2)}, u32[]{:S(2)}) collective-permute-start(bf16[256,512]{1,0:T(8,128)(2,1)S(1)} %collective-permute-done.2.refs_0_), channel_id=1, source_target_pairs={{0,1},{1,0},{2,3},{3,2},{4,5},{5,4},{6,7},{7,6},{8,9},{9,8},{10,11... | collective-permute-start | bytes 786440 | tf_op jit(solution)/shard_map/ppermute | solution.py:405
  17.4 2.2 %copy-start.1 = (f32[128]{0:T(128)S(1)}, f32[128]{0:T(128)}, u32[]{:S(2)}) copy-start(f32[128]{0:T(128)} %param.12) | copy-start | bytes 1540
  17.4 2.2 %copy-start.2 = (f32[128]{0:T(128)S(1)}, f32[128]{0:T(128)}, u32[]{:S(2)}) copy-start(f32[128]{0:T(128)} %param.13) | copy-start | bytes 1540
  17.4 2.1 %collective-permute-start.1 = (bf16[256,512]{1,0:T(8,128)(2,1)S(1)}, bf16[256,512]{1,0:T(8,128)(2,1)S(1)}, u32[]{:S(2)}, u32[]{:S(2)}) collective-permute-start(bf16[256,512]{1,0:T(8,128)(2,1)S(1)} %collective-permute-done.refs_0_), channel_id=1, source_target_pairs={{0,1},{1,0},{2,3},{3,2},{4,5},{5,4},{6,7},{7,6},{8,9},{9,8},{10,11... | collective-permute-start | bytes 786440 | tf_op jit(solution)/shard_map/ppermute | solution.py:405
  20.6 9.2 %collective-permute-start.7 = (bf16[256,256]{1,0:T(8,128)(2,1)S(1)}, bf16[256,256]{1,0:T(8,128)(2,1)S(1)}, u32[]{:S(2)}, u32[]{:S(2)}) collective-permute-start(bf16[256,256]{1,0:T(8,128)(2,1)S(1)} %get-tuple-element.59.refs_3_.own), channel_id=1, source_target_pairs={{0,32},{8,40},{16,48},{24,56},{32,64},{40,72},{48,80},{56,88},{64,... | collective-permute-start | bytes 393224 | tf_op jit(solution)/shard_map/ppermute | solution.py:421
  29.8 5.3 %collective-permute-start.8 = (bf16[256,256]{1,0:T(8,128)(2,1)S(1)}, bf16[256,256]{1,0:T(8,128)(2,1)S(1)}, u32[]{:S(2)}, u32[]{:S(2)}) collective-permute-start(bf16[256,256]{1,0:T(8,128)(2,1)S(1)} %collective-permute-done.7.refs_0_.refs_3_), channel_id=1, source_target_pairs={{0,32},{8,40},{16,48},{24,56},{32,64},{40,72},{48,80},{56,88},{64,... | collective-permute-start | bytes 393224 | tf_op jit(solution)/shard_map/ppermute | solution.py:421
  29.8 13.1 %collective-permute-start.13 = (bf16[4,512,512]{2,1,0:T(8,128)(2,1)}, bf16[4,512,512]{2,1,0:T(8,128)(2,1)}, u32[]{:S(2)}, u32[]{:S(2)}) collective-permute-start(bf16[4,512,512]{2,1,0:T(8,128)(2,1)} %get-tuple-element.66), channel_id=1, source_target_pairs={{0,1},{1,0},{2,3},{3,2},{4,5},{5,4},{6,7},{7,6},{8,9},{9,8},{10,11... | collective-permute-start | bytes 6291464 | tf_op jit(solution)/shard_map/ppermute | solution.py:405
  32.0 5.9 %collective-permute-start.19 = (bf16[256,256]{1,0:T(8,128)(2,1)S(1)}, bf16[256,256]{1,0:T(8,128)(2,1)S(1)}, u32[]{:S(2)}, u32[]{:S(2)}) collective-permute-start(bf16[256,256]{1,0:T(8,128)(2,1)S(1)} %collective-permute-done.7.refs_0_.refs_3_), channel_id=1, source_target_pairs={{0,8},{1,25},{2,10},{3,27},{4,12},{5,29},{6,14},{7,31},{8,0},{9,17... | collective-permute-start | bytes 393224 | tf_op jit(solution)/shard_map/ppermute | solution.py:430
  35.2 5.0 %collective-permute-start.9 = (bf16[256,256]{1,0:T(8,128)(2,1)S(1)}, bf16[256,256]{1,0:T(8,128)(2,1)S(1)}, u32[]{:S(2)}, u32[]{:S(2)}) collective-permute-start(bf16[256,256]{1,0:T(8,128)(2,1)S(1)} %collective-permute-done.8.refs_0_.refs_4_), channel_id=1, source_target_pairs={{0,32},{8,40},{16,48},{24,56},{32,64},{40,72},{48,80},{56,88},{64,... | collective-permute-start | bytes 393224 | tf_op jit(solution)/shard_map/ppermute | solution.py:421
  35.2 7.8 %collective-permute-start.12 = (bf16[256,256]{1,0:T(8,128)(2,1)S(1)}, bf16[256,256]{1,0:T(8,128)(2,1)S(1)}, u32[]{:S(2)}, u32[]{:S(2)}) collective-permute-start(bf16[256,256]{1,0:T(8,128)(2,1)S(1)} %collective-permute-done.8.refs_0_.refs_4_), channel_id=1, source_target_pairs={{0,8},{1,25},{2,10},{3,27},{4,12},{5,29},{6,14},{7,31},{8,0},{9,17... | collective-permute-start | bytes 393224 | tf_op jit(solution)/shard_map/ppermute | solution.py:430
  38.5 11.2 %collective-permute-start.20 = (bf16[512,256]{1,0:T(8,128)(2,1)S(1)}, bf16[512,256]{1,0:T(8,128)(2,1)S(1)}, u32[]{:S(2)}, u32[]{:S(2)}) collective-permute-start(bf16[512,256]{1,0:T(8,128)(2,1)S(1)} %get-tuple-element.75), channel_id=1, source_target_pairs={{0,24},{1,9},{2,26},{3,11},{4,28},{5,13},{6,30},{7,15},{8,16},{9,1... | collective-permute-start | bytes 786440 | tf_op jit(solution)/shard_map/ppermute | solution.py:430
  40.2 5.6 %collective-permute-start.11 = (bf16[256,256]{1,0:T(8,128)(2,1)S(1)}, bf16[256,256]{1,0:T(8,128)(2,1)S(1)}, u32[]{:S(2)}, u32[]{:S(2)}) collective-permute-start(bf16[256,256]{1,0:T(8,128)(2,1)S(1)} %collective-permute-done.9.refs_0_.refs_8_), channel_id=1, source_target_pairs={{0,32},{8,40},{16,48},{24,56},{32,64},{40,72},{48,80},{56,88},{64,... | collective-permute-start | bytes 393224 | tf_op jit(solution)/shard_map/ppermute | solution.py:421
  40.2 8.4 %collective-permute-start.10 = (bf16[256,256]{1,0:T(8,128)(2,1)S(1)}, bf16[256,256]{1,0:T(8,128)(2,1)S(1)}, u32[]{:S(2)}, u32[]{:S(2)}) collective-permute-start(bf16[256,256]{1,0:T(8,128)(2,1)S(1)} %collective-permute-done.9.refs_0_.refs_8_), channel_id=1, source_target_pairs={{0,8},{1,25},{2,10},{3,27},{4,12},{5,29},{6,14},{7,31},{8,0},{9,17... | collective-permute-start | bytes 393224 | tf_op jit(solution)/shard_map/ppermute | solution.py:430
  43.0 8.8 %collective-permute-start.18 = (bf16[512,256]{1,0:T(8,128)(2,1)S(1)}, bf16[512,256]{1,0:T(8,128)(2,1)S(1)}, u32[]{:S(2)}, u32[]{:S(2)}) collective-permute-start(bf16[512,256]{1,0:T(8,128)(2,1)S(1)} %get-tuple-element.73), channel_id=1, source_target_pairs={{0,24},{1,9},{2,26},{3,11},{4,28},{5,13},{6,30},{7,15},{8,16},{9,1... | collective-permute-start | bytes 786440 | tf_op jit(solution)/shard_map/ppermute | solution.py:430
  45.8 8.2 %collective-permute-start.15 = (bf16[256,256]{1,0:T(8,128)(2,1)S(1)}, bf16[256,256]{1,0:T(8,128)(2,1)S(1)}, u32[]{:S(2)}, u32[]{:S(2)}) collective-permute-start(bf16[256,256]{1,0:T(8,128)(2,1)S(1)} %get-tuple-element.70), channel_id=1, source_target_pairs={{0,8},{8,16},{16,24},{24,0},{32,40},{40,48},{48,56},{56,32},{64,72... | collective-permute-start | bytes 393224 | tf_op jit(solution)/shard_map/ppermute | solution.py:418
  46.7 7.4 %collective-permute-start.16 = (bf16[256,256]{1,0:T(8,128)(2,1)S(1)}, bf16[256,256]{1,0:T(8,128)(2,1)S(1)}, u32[]{:S(2)}, u32[]{:S(2)}) collective-permute-start(bf16[256,256]{1,0:T(8,128)(2,1)S(1)} %get-tuple-element.71), channel_id=1, source_target_pairs={{0,24},{8,0},{16,8},{24,16},{32,56},{40,32},{48,40},{56,48},{64,88... | collective-permute-start | bytes 393224 | tf_op jit(solution)/shard_map/ppermute | solution.py:418
  48.6 5.5 %collective-permute-start.17 = (bf16[256,256]{1,0:T(8,128)(2,1)S(1)}, bf16[256,256]{1,0:T(8,128)(2,1)S(1)}, u32[]{:S(2)}, u32[]{:S(2)}) collective-permute-start(bf16[256,256]{1,0:T(8,128)(2,1)S(1)} %get-tuple-element.72), channel_id=1, source_target_pairs={{0,16},{8,24},{16,0},{24,8},{32,48},{40,56},{48,32},{56,40},{64,80... | collective-permute-start | bytes 393224 | tf_op jit(solution)/shard_map/ppermute | solution.py:418
  49.8 7.5 %collective-permute-start.14 = (bf16[512,256]{1,0:T(8,128)(2,1)S(1)}, bf16[512,256]{1,0:T(8,128)(2,1)S(1)}, u32[]{:S(2)}, u32[]{:S(2)}) collective-permute-start(bf16[512,256]{1,0:T(8,128)(2,1)S(1)} %get-tuple-element.69), channel_id=1, source_target_pairs={{0,24},{1,9},{2,26},{3,11},{4,28},{5,13},{6,30},{7,15},{8,16},{9,1... | collective-permute-start | bytes 786440 | tf_op jit(solution)/shard_map/ppermute | solution.py:430
  58.8 6.9 %collective-permute-start.21 = (bf16[256,512]{1,0:T(8,128)(2,1)S(1)}, bf16[256,512]{1,0:T(8,128)(2,1)S(1)}, u32[]{:S(2)}, u32[]{:S(2)}) collective-permute-start(bf16[256,512]{1,0:T(8,128)(2,1)S(1)} %get-tuple-element.82.a_ref), channel_id=1, source_target_pairs={{0,1},{1,0},{2,3},{3,2},{4,5},{5,4},{6,7},{7,6},{8,9},{9,8},{10,11... | collective-permute-start | bytes 786440 | tf_op jit(solution)/shard_map/ppermute | solution.py:405
  66.1 9.1 %collective-permute-start.23 = (bf16[256,512]{1,0:T(8,128)(2,1)S(1)}, bf16[256,512]{1,0:T(8,128)(2,1)S(1)}, u32[]{:S(2)}, u32[]{:S(2)}) collective-permute-start(bf16[256,512]{1,0:T(8,128)(2,1)S(1)} %out_project.5), channel_id=1, source_target_pairs={{0,4},{1,5},{2,6},{3,7},{4,0},{5,1},{6,2},{7,3},{8,12},{9,13},{10,... | collective-permute-start | bytes 786440 | tf_op jit(solution)/shard_map/ppermute | solution.py:408
  69.7 11.1 %collective-permute-start.22 = (bf16[256,512]{1,0:T(8,128)(2,1)S(1)}, bf16[256,512]{1,0:T(8,128)(2,1)S(1)}, u32[]{:S(2)}, u32[]{:S(2)}) collective-permute-start(bf16[256,512]{1,0:T(8,128)(2,1)S(1)} %get-tuple-element.85), channel_id=1, source_target_pairs={{0,2},{1,7},{2,4},{3,1},{4,6},{5,3},{6,0},{7,5},{8,10},{9,15},{10,... | collective-permute-start | bytes 786440 | tf_op jit(solution)/shard_map/ppermute | solution.py:408
  70.5 11.2 %collective-permute-start.24 = (bf16[256,512]{1,0:T(8,128)(2,1)S(1)}, bf16[256,512]{1,0:T(8,128)(2,1)S(1)}, u32[]{:S(2)}, u32[]{:S(2)}) collective-permute-start(bf16[256,512]{1,0:T(8,128)(2,1)S(1)} %get-tuple-element.86), channel_id=1, source_target_pairs={{0,6},{1,3},{2,0},{3,5},{4,2},{5,7},{6,4},{7,1},{8,14},{9,11},{10,... | collective-permute-start | bytes 786440 | tf_op jit(solution)/shard_map/ppermute | solution.py:408
